TPU v7x, 32 devices: a whole 2x2x4 slice. The times are simulated.
32 devices in a mesh: fsdp: 8 (over y, x, core), tensor: 4 (over z).
Axes of the slice: x: 2, y: 2, z: 4, core: 2. Of those that a mesh axis runs over, the one named last changes fastest.
Arguments:
- student_in: bfloat16 [24576, 768], P('fsdp'), may hold values from -6 to 6
- teacher_in: bfloat16 [24576, 768], P('fsdp'), may hold values from -6 to 6
- bucket_size: int32 [384], P('fsdp'), may hold values from 64 to 256, as said below
- seq_length: int32 [384], P('fsdp'), may hold values from 33 to 256, as said below
- qkv_latent: float32 [3, 768, 768], P(None, 'fsdp', 'tensor'), may hold values from -7.2 to 7.2
- out_latent: float32 [768, 768], P('tensor', 'fsdp'), may hold values from -7.2 to 7.2
- up_latent: float32 [768, 3072], P('fsdp', 'tensor'), may hold values from -7.2 to 7.2
- down_latent: float32 [3072, 768], P('tensor', 'fsdp'), may hold values from -7.2 to 7.2
- gain_attn: bfloat16 [768], P('fsdp'), may hold values from 0.25 to 1.75
- gain_ffn: bfloat16 [768], P('fsdp'), may hold values from 0.25 to 1.75
- teach_qkv: bfloat16 [3, 768, 768], P(None, 'fsdp', 'tensor'), may hold values from -0.21875 to 0.21875
- teach_out: bfloat16 [768, 768], P('tensor', 'fsdp'), may hold values from -0.625 to 0.625
- teach_up: bfloat16 [768, 3072], P('fsdp', 'tensor'), may hold values from -0.21875 to 0.21875
- teach_down: bfloat16 [3072, 768], P('tensor', 'fsdp'), may hold values from -0.109375 to 0.109375
Outputs:
- student_out: bfloat16 [24576, 768], P('fsdp', 'tensor')
- teacher_out: bfloat16 [24576, 768], P('fsdp', 'tensor')
- input_grad: float32 [24576, 768], P('fsdp', 'tensor')
- grad_qkv: float32 [3, 768, 768], P(None, 'fsdp', 'tensor')
- grad_out: float32 [768, 768], P('tensor', 'fsdp')
- grad_up: float32 [768, 3072], P('fsdp', 'tensor')
- grad_down: float32 [3072, 768], P('tensor', 'fsdp')
- grad_gain_attn: float32 [768], P('fsdp')
- grad_gain_ffn: float32 [768], P('fsdp')
Inputs may be any that keep to these rules, and one draw needn't show every extreme that they name: `bucket_size`: for each unit of 64 slots, the size (64, 128 or 256) of the bucket that holds it; a bucket of size s covers s / 64 units and starts at a slot that is a multiple of s. `seq_length`: for each unit, the live tokens of the sequence in its bucket, equal over the units of a bucket; a bucket of size s holds more than s / 2 and at most s, at its start.
All inputs are finite; a program needn't handle non-finite values.
Results may differ from a plain program's by a relative error of at most 0.02.
The roundings to bfloat16 on the way count: a program that leaves them out, or rounds other values in their place, can miss the bound.
Values may be sent and summed in bfloat16 or wider, within the bound.
No kernel may reach another device: no remote copies, remote signals or barrier semaphores. Data moves between devices by JAX's collectives and lax.ppermute only.
A program may use at most 256 MiB of HBM per device.

v0:
```python
import math

import jax
import jax.numpy as jnp
from jax import lax
from jax.sharding import PartitionSpec as P

D = 768
HEAD_DIM = 64
FF = 3072
MICRO = 3
BLOCK = 512


CLIP_RANGE = 2.5
ATT_WEIGHT = 0.015625
EPSILON = 1e-06
NEG_FILL = -1000000000.0


def soft_clip(value):
    return CLIP_RANGE * jnp.tanh(value / CLIP_RANGE)


def layer_norm(value):
    centre = value - jnp.mean(value, axis=-1, keepdims=True)
    return centre * lax.rsqrt(jnp.mean(centre * centre, axis=-1, keepdims=True) + EPSILON)


def norm_gain(value, gain):
    return layer_norm(value) * gain


def gelu_exact(value):
    return jax.nn.gelu(value, approximate=False)


def product(left, right):
    return jnp.dot(left, right, preferred_element_type=jnp.float32)


def product_left(left, right):
    return lax.dot_general(
        left, right, (((0,), (0,)), ((), ())), preferred_element_type=jnp.float32
    )


def product_right(left, right):
    return lax.dot_general(
        left, right, (((1,), (1,)), ((), ())), preferred_element_type=jnp.float32
    )


def slot_tables(bucket_size, seq_length):
    slots = jnp.arange(bucket_size.shape[0] * 64, dtype=jnp.int32)
    sizes = jnp.repeat(bucket_size, 64)
    lengths = jnp.repeat(seq_length, 64)
    begin = slots // sizes * sizes
    return (begin, slots - begin < lengths)


def binary_set(qkv_rows, out_rows, up_rows, down_rows, first_gain, second_gain):
    return (
        jnp.sign(qkv_rows),
        jnp.sign(out_rows),
        jnp.sign(up_rows),
        jnp.sign(down_rows),
        first_gain.astype(jnp.float32),
        second_gain.astype(jnp.float32),
    )


def fetch_layer(
    qkv_latent,
    out_latent,
    up_latent,
    down_latent,
    gain_attn,
    gain_ffn,
    teach_qkv,
    teach_out,
    teach_up,
    teach_down,
):
    whole = (
        lax.all_gather(qkv_latent.astype(jnp.bfloat16), "fsdp", axis=1, tiled=True),
        lax.all_gather(out_latent.astype(jnp.bfloat16), "fsdp", axis=1, tiled=True),
        lax.all_gather(up_latent.astype(jnp.bfloat16), "fsdp", axis=0, tiled=True),
        lax.all_gather(down_latent.astype(jnp.bfloat16), "fsdp", axis=1, tiled=True),
        lax.all_gather(gain_attn, "fsdp", axis=0, tiled=True),
        lax.all_gather(gain_ffn, "fsdp", axis=0, tiled=True),
        lax.all_gather(teach_qkv, "fsdp", axis=1, tiled=True),
        lax.all_gather(teach_out, "fsdp", axis=1, tiled=True),
        lax.all_gather(teach_up, "fsdp", axis=0, tiled=True),
        lax.all_gather(teach_down, "fsdp", axis=1, tiled=True),
    )
    out_full = None
    return (
        binary_set(whole[0], whole[1], whole[2], whole[3], whole[4], whole[5]),
        (whole[6], whole[7], whole[8], whole[9]),
        out_full,
    )


def fetch_student(qkv_latent, out_latent, up_latent, down_latent, gain_attn, gain_ffn):
    whole = (
        lax.all_gather(qkv_latent.astype(jnp.bfloat16), "fsdp", axis=1, tiled=True),
        lax.all_gather(out_latent.astype(jnp.bfloat16), "fsdp", axis=1, tiled=True),
        lax.all_gather(up_latent.astype(jnp.bfloat16), "fsdp", axis=0, tiled=True),
        lax.all_gather(down_latent.astype(jnp.bfloat16), "fsdp", axis=1, tiled=True),
        lax.all_gather(gain_attn, "fsdp", axis=0, tiled=True),
        lax.all_gather(gain_ffn, "fsdp", axis=0, tiled=True),
    )
    return binary_set(whole[0], whole[1], whole[2], whole[3], whole[4], whole[5])


def head_total(student_part, teacher_part):
    return lax.psum((student_part, teacher_part), "tensor")


def input_total(partial_grad):
    return lax.psum(partial_grad.astype(jnp.bfloat16), "tensor").astype(jnp.float32)


def reduce_grads(grad_qkv, grad_out, grad_up, grad_down, grad_first, grad_second):
    return (
        lax.psum_scatter(
            grad_qkv.astype(jnp.bfloat16), "fsdp", scatter_dimension=1, tiled=True
        ).astype(jnp.float32),
        lax.psum_scatter(
            grad_out.astype(jnp.bfloat16), "fsdp", scatter_dimension=1, tiled=True
        ).astype(jnp.float32),
        lax.psum_scatter(
            grad_up.astype(jnp.bfloat16), "fsdp", scatter_dimension=0, tiled=True
        ).astype(jnp.float32),
        lax.psum_scatter(
            grad_down.astype(jnp.bfloat16), "fsdp", scatter_dimension=1, tiled=True
        ).astype(jnp.float32),
        lax.psum_scatter(
            grad_first.astype(jnp.bfloat16), "fsdp", scatter_dimension=0, tiled=True
        ).astype(jnp.float32),
        lax.psum_scatter(
            grad_second.astype(jnp.bfloat16), "fsdp", scatter_dimension=0, tiled=True
        ).astype(jnp.float32),
    )


def softmax_forward(query, keys, value, keep):
    scale = HEAD_DIM ** (-0.5)
    raw = jnp.einsum("qhd,khd->hqk", query, keys, preferred_element_type=jnp.float32)
    masked = jnp.where(keep[None], raw * scale, NEG_FILL)
    top = jnp.max(masked, axis=-1, keepdims=True)
    expo = jnp.exp(masked - top)
    total = jnp.sum(expo, axis=-1, keepdims=True)
    probs = (expo / total).astype(jnp.bfloat16)
    attended = jnp.einsum("hqk,khd->qhd", probs, value, preferred_element_type=jnp.float32).astype(
        jnp.bfloat16
    )
    return (attended, (top + jnp.log(total))[..., 0])


def attend_forward(pieces):
    query, keys, value, t_query, t_keys, t_value, begin, live = pieces
    keep = (begin[:, None] == begin[None, :]) & live[None, :]
    attended, log_total = softmax_forward(query, keys, value, keep)
    teach_attended, unused_total = softmax_forward(t_query, t_keys, t_value, keep)
    return (attended, log_total, teach_attended)


def body(
    student_in,
    teacher_in,
    bucket_size,
    seq_length,
    qkv_latent,
    out_latent,
    up_latent,
    down_latent,
    gain_attn,
    gain_ffn,
    teach_qkv,
    teach_out,
    teach_up,
    teach_down,
):
    width = student_in.shape[1]
    batch_rows = student_in.shape[0] // MICRO
    blocks = batch_rows // BLOCK
    heads_here = qkv_latent.shape[2] // HEAD_DIM
    columns = width // lax.axis_size("tensor")
    col_first = lax.axis_index("tensor") * columns
    scale = HEAD_DIM ** (-0.5)
    begin_all, live_all = slot_tables(bucket_size, seq_length)
    totals = lax.psum(
        (
            jnp.sum(jnp.abs(qkv_latent)),
            jnp.sum(jnp.abs(out_latent)),
            jnp.sum(jnp.abs(up_latent)),
            jnp.sum(jnp.abs(down_latent)),
        ),
        ("fsdp", "tensor"),
    )
    beta_qkv = 2.0 * totals[0] / (3 * D * D) / math.sqrt(D)
    beta_out = 2.0 * totals[1] / (D * D) / math.sqrt(D)
    beta_up = 2.0 * totals[2] / (D * FF) / math.sqrt(D)
    beta_down = 2.0 * totals[3] / (D * FF) / math.sqrt(FF)

    def split_heads(value):
        return value.reshape(blocks, BLOCK, heads_here, HEAD_DIM)

    def merge_heads(value):
        return value.reshape(batch_rows, heads_here * HEAD_DIM)

    def attend_backward(pieces):
        query, keys, value, t_query, t_keys, log_total, grad_attended, begin, live = pieces
        keep = (begin[:, None] == begin[None, :]) & live[None, :]
        scores = jnp.einsum("qhd,khd->hqk", query, keys, preferred_element_type=jnp.float32) * scale
        masked = jnp.where(keep[None], scores, NEG_FILL)
        probs = jnp.exp(masked - log_total[..., None])
        d_probs = jnp.einsum(
            "qhd,khd->hqk", grad_attended, value, preferred_element_type=jnp.float32
        )
        d_value = jnp.einsum(
            "hqk,qhd->khd",
            probs.astype(jnp.bfloat16),
            grad_attended,
            preferred_element_type=jnp.float32,
        )
        inner = jnp.sum(probs * d_probs, axis=-1, keepdims=True)
        teach = (
            jnp.einsum("qhd,khd->hqk", t_query, t_keys, preferred_element_type=jnp.float32) * scale
        )
        both = keep[None] & live[None, :, None]
        d_scores = probs * (d_probs - inner) + ATT_WEIGHT * jnp.where(both, scores - teach, 0.0)
        d_raw = (d_scores * scale).astype(jnp.bfloat16)
        d_query = jnp.einsum("hqk,khd->qhd", d_raw, keys, preferred_element_type=jnp.float32)
        d_keys = jnp.einsum("hqk,qhd->khd", d_raw, query, preferred_element_type=jnp.float32)
        return (
            (beta_qkv * d_query).astype(jnp.bfloat16),
            (beta_qkv * d_keys).astype(jnp.bfloat16),
            (beta_qkv * d_value).astype(jnp.bfloat16),
        )

    summed = None
    student_rows = []
    teacher_rows = []
    input_rows = []
    for step in range(MICRO):
        student_set, teacher_set, out_full = fetch_layer(
            qkv_latent,
            out_latent,
            up_latent,
            down_latent,
            gain_attn,
            gain_ffn,
            teach_qkv,
            teach_out,
            teach_up,
            teach_down,
        )
        sign_qkv, sign_out, sign_up, sign_down, first_gain, second_gain = student_set
        teach_qkv_all, teach_out_all, teach_up_all, teach_down_all = teacher_set
        first_row = step * batch_rows
        x_student = lax.slice_in_dim(student_in, first_row, first_row + batch_rows, axis=0).astype(
            jnp.float32
        )
        x_teach_low = lax.slice_in_dim(teacher_in, first_row, first_row + batch_rows, axis=0)
        x_teacher = x_teach_low.astype(jnp.float32)
        begin_here = lax.slice_in_dim(begin_all, first_row, first_row + batch_rows, axis=0).reshape(
            blocks, BLOCK
        )
        live_here = lax.slice_in_dim(live_all, first_row, first_row + batch_rows, axis=0)
        entry = soft_clip(x_student).astype(jnp.bfloat16)
        projected = [
            (beta_qkv * product(entry, sign_qkv[j])).astype(jnp.bfloat16) for j in range(3)
        ]
        teach_proj = [product(x_teach_low, teach_qkv_all[j]).astype(jnp.bfloat16) for j in range(3)]
        attended, log_total, teach_attended = lax.map(
            attend_forward,
            (
                split_heads(projected[0]),
                split_heads(projected[1]),
                split_heads(projected[2]),
                split_heads(teach_proj[0]),
                split_heads(teach_proj[1]),
                split_heads(teach_proj[2]),
                begin_here,
                live_here.reshape(blocks, BLOCK),
            ),
        )
        attended = merge_heads(attended)
        attn_student, attn_teacher = head_total(
            product(attended, sign_out), product(merge_heads(teach_attended), teach_out_all)
        )
        pre_first = x_student + beta_out * attn_student
        h_first = norm_gain(pre_first, first_gain)
        t_first = layer_norm(x_teacher + attn_teacher)
        middle = soft_clip(h_first).astype(jnp.bfloat16)
        up_value = beta_up * product(middle, sign_up)
        hidden = gelu_exact(up_value).astype(jnp.bfloat16)
        t_hidden = gelu_exact(product(t_first.astype(jnp.bfloat16), teach_up_all)).astype(
            jnp.bfloat16
        )
        down_student, down_teacher = head_total(
            product(hidden, sign_down), product(t_hidden, teach_down_all)
        )
        pre_second = h_first + beta_down * down_student
        result = norm_gain(pre_second, second_gain)
        t_result = layer_norm(t_first + down_teacher)
        student_rows.append(
            lax.dynamic_slice_in_dim(result.astype(jnp.bfloat16), col_first, columns, 1)
        )
        teacher_rows.append(
            lax.dynamic_slice_in_dim(t_result.astype(jnp.bfloat16), col_first, columns, 1)
        )
        back_set = fetch_student(
            qkv_latent, out_latent, up_latent, down_latent, gain_attn, gain_ffn
        )
        back_qkv, back_out, back_up, back_down, back_first, back_second = back_set
        d_result = jnp.where(live_here[:, None], result - t_result, 0.0)
        unused_second, second_back = jax.vjp(norm_gain, pre_second, back_second)
        d_pre_second, d_gain_second = second_back(d_result)
        grad_z = (beta_down * d_pre_second).astype(jnp.bfloat16)
        d_hidden = product_right(grad_z, back_down)
        grad_down_part = product_left(hidden, grad_z)
        unused_gelu, gelu_back = jax.vjp(gelu_exact, up_value)
        grad_u = (beta_up * gelu_back(d_hidden)[0]).astype(jnp.bfloat16)
        grad_up_part = product_left(middle, grad_u)
        d_middle = input_total(product_right(grad_u, back_up))
        unused_clip, clip_back = jax.vjp(soft_clip, h_first)
        d_h_first = d_pre_second + clip_back(d_middle)[0]
        unused_first, first_back = jax.vjp(norm_gain, pre_first, back_first)
        d_pre_first, d_gain_first = first_back(d_h_first)
        grad_o = (beta_out * d_pre_first).astype(jnp.bfloat16)
        grad_out_part = product_left(attended, grad_o)
        d_attended = product_right(grad_o, back_out).astype(jnp.bfloat16)
        grad_q, grad_k, grad_v = lax.map(
            attend_backward,
            (
                split_heads(projected[0]),
                split_heads(projected[1]),
                split_heads(projected[2]),
                split_heads(teach_proj[0]),
                split_heads(teach_proj[1]),
                log_total,
                split_heads(d_attended),
                begin_here,
                live_here.reshape(blocks, BLOCK),
            ),
        )
        grads_proj = (merge_heads(grad_q), merge_heads(grad_k), merge_heads(grad_v))
        grad_qkv_part = jnp.stack([product_left(entry, grads_proj[j]) for j in range(3)])
        d_entry_part = (
            product_right(grads_proj[0], back_qkv[0])
            + product_right(grads_proj[1], back_qkv[1])
            + product_right(grads_proj[2], back_qkv[2])
        )
        d_entry = input_total(d_entry_part)
        unused_entry, entry_back = jax.vjp(soft_clip, x_student)
        d_input = d_pre_first + entry_back(d_entry)[0]
        input_rows.append(lax.dynamic_slice_in_dim(d_input, col_first, columns, 1))
        terms = (
            grad_qkv_part,
            grad_out_part,
            grad_up_part,
            grad_down_part,
            d_gain_first,
            d_gain_second,
        )
        shares = reduce_grads(terms[0], terms[1], terms[2], terms[3], terms[4], terms[5])
        if summed is None:
            summed = shares
        else:
            summed = jax.tree.map(lambda left, right: left + right, summed, shares)
    grad_qkv = summed[0] * (jnp.abs(qkv_latent) <= 1.0).astype(jnp.float32)
    grad_out = summed[1] * (jnp.abs(out_latent) <= 1.0).astype(jnp.float32)
    grad_up = summed[2] * (jnp.abs(up_latent) <= 1.0).astype(jnp.float32)
    grad_down = summed[3] * (jnp.abs(down_latent) <= 1.0).astype(jnp.float32)
    return (
        jnp.concatenate(student_rows, axis=0),
        jnp.concatenate(teacher_rows, axis=0),
        jnp.concatenate(input_rows, axis=0),
        grad_qkv,
        grad_out,
        grad_up,
        grad_down,
        summed[4],
        summed[5],
    )


def solution(mesh):
    placed = (
        P("fsdp", None),
        P("fsdp", None),
        P("fsdp"),
        P("fsdp"),
        P(None, "fsdp", "tensor"),
        P("tensor", "fsdp"),
        P("fsdp", "tensor"),
        P("tensor", "fsdp"),
        P("fsdp"),
        P("fsdp"),
        P(None, "fsdp", "tensor"),
        P("tensor", "fsdp"),
        P("fsdp", "tensor"),
        P("tensor", "fsdp"),
    )
    return jax.shard_map(
        body,
        mesh=mesh,
        in_specs=placed,
        out_specs=(
            P("fsdp", "tensor"),
            P("fsdp", "tensor"),
            P("fsdp", "tensor"),
            P(None, "fsdp", "tensor"),
            P("tensor", "fsdp"),
            P("fsdp", "tensor"),
            P("tensor", "fsdp"),
            P("fsdp"),
            P("fsdp"),
        ),
        check_vma=False,
    )
```

profile of v0, /device:TPU:0, one launch (start us, length us, event | category | flops | bytes accessed | tf_op | source)
XLA Modules:
  0.0 2328.8 jit_solution(7184701089439029027)
XLA Ops:
  10.2 13.0 all_gather.20
  28.0 40.0 %all-reduce.8 = (f32[]{:T(128)}, f32[]{:T(128)}, f32[]{:T(128)}, f32[]{:T(128)}) all-reduce(f32[]{:T(128)} %abs_reduce_fusion.2, f32[]{:T(128)} %abs_reduce_fusion.3, f32[]{:T(128)} %get-tuple-element.988, f32[]{:T(128)} %get-tuple-element.987), channel_id=1, replica_groups=mesh['fsdp'=8,'tensor'=4] {'fsdp','tensor'}, use_global_device_ids=true, to_apply=%region_3.4 | all-reduce | flops 4 | bytes 32 | tf_op jit(solution)/shard_map/psum | solution.py:194
  68.6 3.1 fusion.579
  77.7 12.7 all_gather.21
  124.1 16.5 while.85
  141.6 9.2 all_gather.22
  160.7 18.0 while.84
  190.9 17.1 while.86
  211.7 8.9 all_gather.27
  232.8 14.7 all-reduce.12
  248.8 613.5 %all-reduce.22.cloned.1.call-done = (f32[1024,768]{1,0:T(8,128)}, f32[1024,768]{1,0:T(8,128)}, f32[1024,768]{1,0:T(8,128)}, f32[1024,768]{1,0:T(8,128)}, f32[1024,768]{1,0:T(8,128)}, /*index=5*/f32[1024,768]{1,0:T(8,128)}) async-done(((f32[1024,768]{1,0:T(8,128)}, f32[1024,768]{1,0:T(8,128)}, f32[1024,768]{1,0:T(8,128)}, f32[1024,768]{1,0:T(8,128)}, f32[1024,768]{1,0:T(8,128)}, ...) | async-done | bytes 18874384 | tf_op jit(solution)/shard_map/psum | solution.py:118
  862.3 6.2 fusion.751
  873.8 6.9 fusion.767
  883.4 12.9 fusion.574
  896.4 13.1 fusion.572
  909.5 13.0 fusion.570
  922.4 12.7 multiply_convert_fusion.18
  935.1 10.9 multiply_convert_fusion.15
  946.0 5.0 fusion.613
  954.1 11.2 multiply_convert_fusion.12
  966.4 3.2 fusion.609
  971.5 631.8 %all-reduce.20.cloned.1.call-done = (f32[1024,768]{1,0:T(8,128)}, f32[1024,768]{1,0:T(8,128)}, f32[1024,768]{1,0:T(8,128)}, f32[1024,768]{1,0:T(8,128)}, f32[1024,768]{1,0:T(8,128)}, /*index=5*/f32[1024,768]{1,0:T(8,128)}) async-done(((f32[1024,768]{1,0:T(8,128)}, f32[1024,768]{1,0:T(8,128)}, f32[1024,768]{1,0:T(8,128)}, f32[1024,768]{1,0:T(8,128)}, f32[1024,768]{1,0:T(8,128)}, ...) | async-done | bytes 18874384 | tf_op jit(solution)/shard_map/psum | solution.py:118
  1603.3 7.3 fusion.763
  1611.2 10.3 fusion.760
  1625.5 6.2 multiply_reduce_fusion.4
  1631.8 6.2 fusion.757
  1640.1 3.3 copy-done.150
  1665.3 5.0 convolution_convert_fusion.5
  1670.3 5.1 convolution_convert_fusion.4
  1675.5 5.1 convolution_convert_fusion.3
  1680.7 5.3 convolution_convert_fusion.8
  1686.2 5.3 convolution_convert_fusion.7
  1691.6 4.3 convolution_convert_fusion.6
  1696.0 141.0 %all-reduce.26.cloned.1.call-done = (bf16[1024,768]{1,0:T(8,128)(2,1)}, bf16[1024,768]{1,0:T(8,128)(2,1)}, bf16[1024,768]{1,0:T(8,128)(2,1)}) async-done(((bf16[1024,768]{1,0:T(8,128)(2,1)}, bf16[1024,768]{1,0:T(8,128)(2,1)}, bf16[1024,768]{1,0:T(8,128)(2,1)}), (bf16[1024,768]{1,0:T(8,128)(2,1)}, bf16[1024,768]{1,0:T(8,128)(2,1)}, bf16[1024,768]{1,0:T(8,128)(2,1)})) %all-reduce.26.cloned.1.call-update) | async-done | bytes 4718608 | tf_op jit(solution)/shard_map/psum | solution.py:122
  1837.0 12.0 multiply_reduce_fusion.8
  1849.1 5.9 fusion.754
  1855.6 3.7 fusion.756
  1866.1 51.5 %while.87 = (s32[]{:T(128)}, bf16[2,512,3,64]{1,3,2,0:T(8,128)(2,1)}, bf16[2,512,3,64]{1,3,2,0:T(8,128)(2,1)}, bf16[2,512,3,64]{1,3,2,0:T(8,128)(2,1)}, f32[]{:T...) while((s32[]{:T(128)}, ...), condition=%wide.region_69.70_spmd, body=%wide.region_67.69_spmd.sunk | while | flops 633671680 | bytes 55166244 | solution.py:337
  1874.0 7.8 fusion.980
  1881.9 7.5 fusion.979
  1899.7 7.7 fusion.980
  1907.4 7.5 fusion.979
  1925.6 50.8 %while.88 = (s32[]{:T(128)}, bf16[2,512,3,64]{1,3,2,0:T(8,128)(2,1)}, bf16[2,512,3,64]{1,3,2,0:T(8,128)(2,1)}, bf16[2,512,3,64]{1,3,2,0:T(8,128)(2,1)}, f32[]{:T...) while((s32[]{:T(128)}, ...), condition=%wide.region_78.79_spmd, body=%wide.region_76.78_spmd.sunk | while | flops 633671680 | bytes 55166244 | solution.py:337
  1933.3 7.5 fusion.998
  1940.9 7.5 fusion.997
  1958.7 7.5 fusion.998
  1966.2 7.5 fusion.997
  1984.4 50.6 %while.89 = (s32[]{:T(128)}, bf16[2,512,3,64]{1,3,2,0:T(8,128)(2,1)}, bf16[2,512,3,64]{1,3,2,0:T(8,128)(2,1)}, bf16[2,512,3,64]{1,3,2,0:T(8,128)(2,1)}, f32[]{:T...) while((s32[]{:T(128)}, ...), condition=%wide.region_87.88_spmd, body=%wide.region_85.87_spmd.sunk | while | flops 633671680 | bytes 57787740 | solution.py:337
  1992.2 7.5 fusion.1016
  1999.7 7.6 fusion.1015
  2017.4 7.5 fusion.1016
  2024.9 7.6 fusion.1015
  2057.4 3.4 copy.286
  2060.9 4.1 reshape.1055
  2086.3 3.4 copy.288
  2089.7 4.1 reshape.1057
  2109.7 3.4 copy.290
  2113.2 4.1 reshape.1059
  2117.3 3.6 fusion.634
  2128.2 5.0 add_convert_fusion.2
  2160.1 25.5 %all-reduce.11 = (bf16[768]{0:T(1024)(128)(2,1)}, bf16[768]{0:T(1024)(128)(2,1)}, bf16[768]{0:T(1024)(128)(2,1)}, bf16[768]{0:T(1024)(128)(2,1)}, bf16[768]{0:T(1024)(128)(2,1)}, /*index=5*/bf16[768]{0:T(1024)(128)(2,1)}) all-reduce(bf16[768]{0:T(1024)(128)(2,1)} %get-tuple-element.723, ...), channel_id=16, replica_groups=mesh['fsdp'=8,'tensor'=4] {'fsdp'}, use_global_device_ids=true, to_apply=%region_106.107.clone | all-reduce | flops 4608 | bytes 18432
  2197.7 33.6 %reduce-scatter.39.cloned.1.call-done = bf16[96,576]{1,0:T(8,128)(2,1)} async-done(((bf16[768,576]{1,0:T(8,128)(2,1)}), bf16[96,576]{1,0:T(8,128)(2,1)}) %reduce-scatter.39.cloned.1.call-update) | async-done | bytes 110608
  2234.8 35.5 %reduce-scatter.41.cloned.1.call-done = bf16[96,576]{1,0:T(8,128)(2,1)} async-done(((bf16[768,576]{1,0:T(8,128)(2,1)}), bf16[96,576]{1,0:T(8,128)(2,1)}) %reduce-scatter.41.cloned.1.call-update) | async-done | bytes 110608
  2277.5 33.4 %all-reduce.24.cloned.1.call-done = (bf16[1024,768]{1,0:T(8,128)(2,1)}, bf16[1024,768]{1,0:T(8,128)(2,1)}, bf16[1024,768]{1,0:T(8,128)(2,1)}) async-done(((bf16[1024,768]{1,0:T(8,128)(2,1)}, bf16[1024,768]{1,0:T(8,128)(2,1)}, bf16[1024,768]{1,0:T(8,128)(2,1)}), (bf16[1024,768]{1,0:T(8,128)(2,1)}, bf16[1024,768]{1,0:T(8,128)(2,1)}, bf16[1024,768]{1,0:T(8,128)(2,1)})) %all-reduce.24.cloned.1.call-update) | async-done | bytes 4718608 | tf_op jit(solution)/shard_map/psum | solution.py:122
  (787 shorter events, 387.1 us)
Async XLA Ops:
  8.0 16.8 copy-start.90
  8.0 18.0 copy-start.91
  8.0 19.3 copy-start.92
  8.0 854.2 %all-reduce.22.cloned.1.call-start = ((), (), s32[]{:S(2)}) async-start(), calls=%async_computation.29 | async-start | bytes 37748736 | tf_op jit(solution)/shard_map/psum | solution.py:118
  10.2 61.5 %copy-start.68 = (f32[3,96,192]{1,2,0:T(8,128)}, f32[3,96,192]{1,2,0:T(8,128)S(1)}, u32[]{:S(2)}) copy-start(f32[3,96,192]{1,2,0:T(8,128)S(1)} %copy.192) | copy-start | bytes 663556
  23.9 89.0 %copy-start.23 = (bf16[3,768,192]{2,1,0:T(8,128)(2,1)}, bf16[3,768,192]{2,1,0:T(8,128)(2,1)S(1)}, u32[]{:S(2)}) copy-start(bf16[3,768,192]{2,1,0:T(8,128)(2,1)S(1)} %sign.56) | copy-start | bytes 2654212
  68.6 21.9 slice-start
  71.7 18.7 slice-start.1
  93.3 9.2 slice-start.2
  106.9 9.1 slice-start.4
  140.6 11.7 copy-start.42
  140.6 13.0 copy-start.44
  140.7 14.4 copy-start.28
  140.7 14.4 copy-start.46
  140.7 14.4 copy-start.103
  140.7 14.4 copy-start.109
  140.7 14.4 copy-start.115
  141.6 37.7 %copy-start.63 = (bf16[24,8,2,512]{3,1,2,0:T(8,128)(2,1)}, bf16[24,8,2,512]{3,1,2,0:T(8,128)(2,1)S(1)}, u32[]{:S(2)}) copy-start(bf16[24,8,2,512]{3,1,2,0:T(8,128)(2,1)S(1)} %copy.299) | copy-start | bytes 1179652
  150.8 57.8 %copy-start.21 = (bf16[192,768]{0,1:T(8,128)(2,1)}, bf16[192,768]{0,1:T(8,128)(2,1)S(1)}, u32[]{:S(2)}) copy-start(bf16[192,768]{0,1:T(8,128)(2,1)S(1)} %all_gather.22) | copy-start | bytes 884740
  208.6 12.0 copy-start.75
  228.6 654.9 %all-gather.11.cloned.1.call-start = ((), (), s32[]{:S(2)}) async-start(), calls=%async_computation.15 | async-start | bytes 1327104 | tf_op jit(solution)/shard_map/all_gather | solution.py:95
  229.1 654.3 %all-gather.9.cloned.1.call-start = ((), (), s32[]{:S(2)}) async-start(), calls=%async_computation.14 | async-start | bytes 1327104 | tf_op jit(solution)/shard_map/all_gather | solution.py:94
  229.7 692.7 %all-gather.5.cloned.1.call-start = ((), (), s32[]{:S(2)}) async-start(), calls=%async_computation.12 | async-start | bytes 1327104 | tf_op jit(solution)/shard_map/all_gather | solution.py:88
  230.3 715.7 %all-gather.7.cloned.1.call-start = ((), (), s32[]{:S(2)}) async-start(), calls=%async_computation.13 | async-start | bytes 1327104 | tf_op jit(solution)/shard_map/all_gather | solution.py:89
  231.0 1372.3 %all-reduce.20.cloned.1.call-start = ((), (), s32[]{:S(2)}) async-start(), calls=%async_computation.28 | async-start | bytes 37748736 | tf_op jit(solution)/shard_map/psum | solution.py:118
  862.3 7.4 copy-start.12
  862.3 8.3 copy-start.13
  862.3 9.2 copy-start.14
  883.4 13.0 copy-start.121
  883.4 13.0 copy-start.125
  922.4 12.7 copy-start.3
  922.4 12.7 copy-start.137
  969.7 867.2 %all-reduce.26.cloned.1.call-start = ((), (), s32[]{:S(2)}) async-start(), calls=%async_computation.31 | async-start | bytes 9437184 | tf_op jit(solution)/shard_map/psum | solution.py:122
  1603.3 7.8 slice-start.8
  1603.3 7.8 slice-start.9
  1637.9 12.1 copy-start.15
  1639.5 17.7 copy-start.17
  1665.2 490.9 %reduce-scatter.31.cloned.1.call-start = ((), (), s32[]{:S(2)}) async-start(), calls=%async_computation.19 | async-start | bytes 1327104 | tf_op jit(solution)/shard_map/reduce_scatter | solution.py:136
  1670.3 485.9 %reduce-scatter.33.cloned.1.call-start = ((), (), s32[]{:S(2)}) async-start(), calls=%async_computation.20 | async-start | bytes 1327104 | tf_op jit(solution)/shard_map/reduce_scatter | solution.py:136
  1675.4 480.7 %reduce-scatter.35.cloned.1.call-start = ((), (), s32[]{:S(2)}) async-start(), calls=%async_computation.21 | async-start | bytes 1327104 | tf_op jit(solution)/shard_map/reduce_scatter | solution.py:136
  1680.6 477.5 %reduce-scatter.25.cloned.1.call-start = ((), (), s32[]{:S(2)}) async-start(), calls=%async_computation.16 | async-start | bytes 1327104 | tf_op jit(solution)/shard_map/reduce_scatter | solution.py:133
  1685.9 472.2 %reduce-scatter.27.cloned.1.call-start = ((), (), s32[]{:S(2)}) async-start(), calls=%async_computation.17 | async-start | bytes 1327104 | tf_op jit(solution)/shard_map/reduce_scatter | solution.py:133
  1691.5 466.6 %reduce-scatter.29.cloned.1.call-start = ((), (), s32[]{:S(2)}) async-start(), calls=%async_computation.18 | async-start | bytes 1327104 | tf_op jit(solution)/shard_map/reduce_scatter | solution.py:133
  1695.9 492.3 %reduce-scatter.43.cloned.1.call-start = ((), (), s32[]{:S(2)}) async-start(), calls=%async_computation.25 | async-start | bytes 442368
  1837.0 12.0 copy-start.126
  1837.0 12.0 copy-start.124
  1837.0 12.1 copy-start.1
  1837.0 12.1 copy-start.4
  1837.0 12.1 copy-start.16
  1837.0 12.1 copy-start.18
  1837.0 12.1 copy-start.40
  1837.0 12.1 copy-start.41
  1999.7 7.6 copy-start.38
  2024.9 7.6 copy-start.38
  2046.5 143.3 %reduce-scatter.45.cloned.1.call-start = ((), (), s32[]{:S(2)}) async-start(), calls=%async_computation.26 | async-start | bytes 442368
  2046.9 6.8 copy-start.79
  2071.9 119.3 %reduce-scatter.47.cloned.1.call-start = ((), (), s32[]{:S(2)}) async-start(), calls=%async_computation.27 | async-start | bytes 442368
  2077.9 116.4 %reduce-scatter.37.cloned.1.call-start = ((), (), s32[]{:S(2)}) async-start(), calls=%async_computation.22 | async-start | bytes 1105920
  2083.9 147.4 %reduce-scatter.39.cloned.1.call-start = ((), (), s32[]{:S(2)}) async-start(), calls=%async_computation.23 | async-start | bytes 1105920
  2107.5 162.8 %reduce-scatter.41.cloned.1.call-start = ((), (), s32[]{:S(2)}) async-start(), calls=%async_computation.24 | async-start | bytes 1105920
  2127.9 183.0 %all-reduce.24.cloned.1.call-start = ((), (), s32[]{:S(2)}) async-start(), calls=%async_computation.30 | async-start | bytes 9437184 | tf_op jit(solution)/shard_map/psum | solution.py:122
  2153.6 6.6 copy-start.130
  2153.6 39.2 %copy-start.93 = (f32[192,96]{1,0:T(8,128)S(1)}, f32[192,96]{1,0:T(8,128)}, u32[]{:S(2)}) copy-start(f32[192,96]{1,0:T(8,128)} %param.31) | copy-start | bytes 221188
  2153.6 120.2 %copy-start.69 = (f32[3,96,192]{1,2,0:T(8,128)S(1)}, f32[3,96,192]{1,2,0:T(8,128)}, u32[]{:S(2)}) copy-start(f32[3,96,192]{1,2,0:T(8,128)} %copy-done.68) | copy-start | bytes 663556
  (140 other events, 511.2 us)
Sparse Core Ops, SparseCore 0:
  228.7 633.5 all-reduce.21
  969.8 633.4 all-reduce.19
  1665.3 171.5 all-reduce.25
  2139.3 171.4 all-reduce.23
Sparse Core Ops, SparseCore 1:
  231.1 22.9 all-gather.10
  255.9 23.9 all-gather.8
  282.3 23.9 all-gather.4
  308.9 23.9 all-gather.6
  1670.3 35.6 reduce-scatter.30
  1709.6 36.6 reduce-scatter.32
  1749.4 36.6 reduce-scatter.34
  1789.5 36.7 reduce-scatter.24
  1829.3 36.6 reduce-scatter.26
  1869.5 36.7 reduce-scatter.28
  2046.5 32.6 reduce-scatter.42
  2082.3 33.8 reduce-scatter.44
  2119.1 33.8 reduce-scatter.46
  2156.2 35.8 reduce-scatter.36
  2195.6 35.6 reduce-scatter.38
  2234.6 35.7 reduce-scatter.40
where the time goes:
time: 2340 us; the launch traced here: 2330 us
  waiting for transfers between devices  1490 us (64%)
  matrix products  431 us (18%)
  local copies, waits for them, and re-layouts  133 us (6%)
  other arithmetic  124 us (5%)
  blocking collectives  124 us (5%)
    psum x2, waiting for transfers between devices, head_total(): return lax.psum((student_part, teacher_part), 'tensor')  1250 us
    psum x2, waiting for transfers between devices, input_total(): lax.psum(partial_grad.astype(jnp.bfloat16), 'tensor').astype(jnp.float32)  174 us
    dot_general x33, matrix products, product(): return jnp.dot(left, right, preferred_element_type=jnp.float32)  138 us
    unnamed x345, local copies, waits for them, and re-layouts  83.2 us
    unnamed x26, waiting for transfers between devices  71.6 us
    dot_general x18, matrix products, product_left(): lax.dot_general(left, right, (((0,), (0,)), ((), ())), preferred_element_...  61 us
    reduce_sum x8, other arithmetic, layer_norm(): centre = value - jnp.mean(value, axis=-1, keepdims=True)  47.9 us
  transfers between devices with their start and end apart: 20, of which 6 were waited for; matrix products, arithmetic and copies ran while one was open for 19% of the time, Pallas kernels for 0%

commit v1 on v0

v1 whole, which is shorter than its diff:
```python
import functools
import math
import types

import jax
import jax.numpy as jnp
from jax import lax
from jax.experimental import pallas as pl
from jax.experimental.pallas import tpu as pltpu
from jax.sharding import PartitionSpec as P

HEAD_DIM = 64
PAIR = 2 * HEAD_DIM
TILE = 256
CLIP_RANGE = 2.5
ATT_WEIGHT = 0.015625
EPSILON = 1e-06
NEG_FILL = -1000000000.0
LOW = jnp.bfloat16
WIDE = jnp.float32
FSDP = "fsdp"
TENSOR = "tensor"
VMEM_BYTES = 60 * 1024 * 1024
WEIGH = 5


IN_PLACE = pl.BlockSpec(memory_space=pl.ANY)
SCALARS = pl.BlockSpec(memory_space=pltpu.SMEM)


class Task:
    def __init__(self, stages):
        self.stages = stages
        self.arrays = None

    def go_on(self):
        try:
            got = next(self.stages) if self.arrays is None else self.stages.send(self.arrays)
            self.arrays = list(got)
        except StopIteration:
            self.arrays = ()

    def finish(self):
        while self.arrays != ():
            self.go_on()


class Order:
    def __init__(self):
        self.after = []
        self.landing = []
        self.shards = []

    def land(self, *tasks, only=None):
        for task in tasks:
            for k in range(len(task.arrays)):
                if only is None or only == k:
                    self.landing.append((task, k))

    def wait(self, *arrays):
        self.after = self.after + list(arrays)

    def fence(self):
        def kernel(out):
            out[...] = jnp.zeros((8, 128), WIDE)

        self.call("fence", kernel, [], [((8, 128), WIDE, whole(8, 128))])

    def call(self, name, kernel, ins, outs, grid=(1,), scratch=(), flops=0, moved=0, onto=()):
        waits = [value for value in self.after if not any(value is array for array in onto)]
        passed = [task.arrays[k] for task, k in self.landing]
        count, given = len(ins), len(outs)
        skip = len(onto) + len(passed) + len(waits)

        def wrapped(*refs):
            kernel(*refs[:count], *refs[count + skip : count + skip + given], *refs[count + skip + given + len(passed) :])

        aliases = {count + k: k for k in range(len(onto))}
        aliases.update({count + len(onto) + k: given + k for k in range(len(passed))})
        results = pl.pallas_call(
            wrapped,
            grid=grid,
            in_specs=[spec for _, spec in ins] + [IN_PLACE] * skip,
            out_specs=[spec for _, _, spec in outs] + [IN_PLACE] * len(passed),
            out_shape=[jax.ShapeDtypeStruct(shape, dtype) for shape, dtype, _ in outs]
            + [jax.ShapeDtypeStruct(array.shape, array.dtype) for array in passed],
            scratch_shapes=list(scratch),
            input_output_aliases=aliases,
            compiler_params=pltpu.CompilerParams(vmem_limit_bytes=VMEM_BYTES),
            cost_estimate=pl.CostEstimate(flops=flops * WEIGH, bytes_accessed=moved * WEIGH, transcendentals=0),
            name=name,
        )(*[array for array, _ in ins], *onto, *passed, *waits)
        rest = list(results[given:])
        for task, k in self.landing:
            task.arrays[k] = rest.pop(0)
        self.landing = []
        self.after = [results[0]]
        return list(results[:given])


def whole(*shape):
    return pl.BlockSpec(shape, lambda *_: (0,) * len(shape))


def swap(value, axis, bit):
    size = lax.axis_size(axis)
    return lax.ppermute(value, axis, [(i, i ^ bit) for i in range(size)])


def swap_first(value):
    return lax.ppermute(value, FSDP, [(i, i ^ (4 if i % 2 else 2)) for i in range(8)])


def swap_second(value):
    return lax.ppermute(value, FSDP, [(i, i ^ (2 if i % 2 else 4)) for i in range(8)])


def bits_of(axis):
    size = lax.axis_size(axis)
    bits = [1 << k for k in range(size.bit_length() - 1)]
    return [bits[0]] + bits[:0:-1] if bits else []


def order_of(axis):
    order = [0]
    for bit in reversed(bits_of(axis)):
        order = order + [o ^ bit for o in order]
    return order


def two_links(rows):
    return lax.axis_size(FSDP) == 8 and rows % 32 == 0


CHIP_ORDERS = ([0, 2, 4, 6, 1, 5, 3, 7], [0, 4, 2, 6, 1, 3, 5, 7])


def feature_order(depth):
    if not two_links(depth):
        return jnp.array(order_of(FSDP), jnp.int32)
    odd = lax.axis_index(FSDP) & 1
    return jnp.where(odd > 0, jnp.array(CHIP_ORDERS[1], jnp.int32), jnp.array(CHIP_ORDERS[0], jnp.int32))


def reorder(blocks, back):
    plain = order_of(FSDP)
    results = []
    for chip in CHIP_ORDERS:
        if back:
            results.append([blocks[chip.index(m)] for m in plain])
        else:
            results.append([blocks[plain.index(m)] for m in chip])
    odd = lax.axis_index(FSDP) & 1
    return [jnp.where(odd > 0, two, one) for one, two in zip(*results)]


def join_columns(run, name, arrays, moves, columns):
    rows = arrays[0].shape[0]

    def kernel(*refs):
        for k, source, target, count in moves:
            refs[-1][:, target : target + count] = refs[k][:, source : source + count]

    return run.call(
        name,
        kernel,
        [(array, whole(*array.shape)) for array in arrays],
        [((rows, columns), LOW, whole(rows, columns))],
        moved=4 * rows * columns,
    )[0]


def side_by_side(run, name, left, right):
    n = left.shape[1]
    return join_columns(run, name, [left, right], [(0, 0, 0, n), (1, 0, n, n)], 2 * n)


def rows_side_by_side(run, name, value, rows):
    total, n = value.shape
    count = total // rows

    def kernel(ref, out):
        for k in range(count):
            out[:, k * n : (k + 1) * n] = ref[k * rows : (k + 1) * rows]

    return run.call(
        name, kernel, [(value, whole(total, n))], [((rows, count * n), LOW, whole(rows, count * n))], moved=4 * total * n
    )[0]


def gather_weight(run, name, shard, finish, store):
    value = shard()
    run.shards.append(value)
    if finish is None:
        (got,) = yield [lax.all_gather(value, TENSOR, axis=0, tiled=True)]
        mine = rows_side_by_side(run, name + "_rows", got, value.shape[0])
    else:
        (got,) = yield [swap(value, TENSOR, 2)]
        value = side_by_side(run, name + "_join", value, got)
        (got,) = yield [swap(value, TENSOR, 1)]
        mine = finish(name + "_rows", value, got)
    if two_links(mine.shape[0]):
        sibling = swap(mine, FSDP, 1)
        first, first_other = yield [swap_first(mine), swap_first(sibling)]
        second = swap(first_other, FSDP, 1)
        second_other, both = yield [swap(first, FSDP, 1), swap_first(second)]
        both_other = swap(both, FSDP, 1)
        store((mine, first, second, both, sibling, second_other, first_other, both_other))
    else:
        for bit in reversed(bits_of(FSDP)):
            mine = jnp.concatenate([mine, swap(mine, FSDP, bit)], axis=0)
        store((mine,))


def add_low(left, right):
    return (left.astype(WIDE) + right.astype(WIDE)).astype(LOW)


def scatter_weight(run, name, left, right, split, store, beside=None, swaps=False):
    rows, width = left.shape
    fsdp = lax.axis_size(FSDP)
    depth = width // fsdp
    columns = right.shape[1]
    middle, half = width // 2, columns // 2
    step = half
    steps = half // step
    side = pl.BlockSpec((rows, step), lambda j: (0, j))
    cost = dict(flops=2 * rows * middle * columns, moved=2 * (rows * columns + 2 * middle * columns))
    added = []
    out_step = step
    if beside is not None:
        added = [(value, whole(8, width)) for value in beside]
        lanes = step // 2
        out_step = 2 * (lanes + 64)
        half = steps * out_step
        columns = 2 * half

    def product(left_ref, right_ref, sums, start):
        value = kernel_tn(left_ref[...], right_ref[...])
        if not sums:
            return value
        turned = [
            jnp.broadcast_to(jnp.sum(ref[:, start : start + middle], axis=0, keepdims=True), (128, middle)).T for ref in sums
        ]
        lane = lax.broadcasted_iota(jnp.int32, (middle, 128), 1)
        more = jnp.where(lane == 0, turned[0], jnp.where(lane == 1, turned[1], 0.0))[:, :64]
        return jnp.concatenate([value[:, :lanes], more, value[:, lanes:], more], axis=1)

    def far_kernel(left_ref, right_ref, *refs):
        refs[-1][...] = product(left_ref, right_ref, refs[:-1], middle).astype(LOW)

    far = run.call(
        name + "_far",
        far_kernel,
        [(left, pl.BlockSpec((rows, middle), lambda j: (0, 1))), (right, side)] + added,
        [((middle, columns), LOW, pl.BlockSpec((middle, out_step), lambda j: (0, j)))],
        grid=(2 * steps,),
        **cost,
    )[0]
    (got,) = yield [swap(far, FSDP, 1)]
    near_ins = [
        (left, pl.BlockSpec((rows, middle), lambda j: (0, 0))),
        (right, side),
        (got, pl.BlockSpec((middle, out_step), lambda j: (0, j))),
    ] + added
    if two_links(depth):
        one = ((depth, columns), LOW, whole(depth, columns))
        at = [slice(k * depth, (k + 1) * depth) for k in range(4)]

        def near_kernel(left_ref, right_ref, got_ref, *refs):
            keep, send = refs[-2:]
            total = (product(left_ref, right_ref, refs[:-2], 0) + got_ref[...].astype(WIDE)).astype(LOW)
            keep[at[0]], keep[at[1]] = total[at[0]], total[at[2]]
            send[at[0]], send[at[1]] = total[at[1]], total[at[3]]

        def second(keep, got, own, onward):
            own[...] = add_low(keep[at[0]], got[at[0]])
            onward[...] = add_low(keep[at[1]], got[at[1]])

        def third(own, got, *outs):
            n = columns // len(outs)
            for k, out in enumerate(outs):
                lanes = slice(k * n, (k + 1) * n)
                out[...] = add_low(own[:, lanes], got[:, lanes])

        def third_rows(where, own, got, out):
            n = columns // 4
            for k in range(4):
                lanes = slice(k * n, (k + 1) * n)
                row = pl.multiple_of(where[k] * depth, depth)
                out[pl.ds(row, depth)] = add_low(own[:, lanes], got[:, lanes])

        pair = ((2 * depth, columns), LOW, pl.BlockSpec((2 * depth, out_step), lambda j: (0, j)))
        keep, send = run.call(name + "_near", near_kernel, near_ins, [pair] * 2, grid=(2 * steps,), **cost)
        (got,) = yield [swap_first(send)]
        full = whole(2 * depth, columns)
        own, onward = run.call(name + "_add2", second, [(keep, full), (got, full)], [one] * 2, moved=6 * depth * columns)
        (got,) = yield [swap_second(onward)]
        ins = [(own, one[2]), (got, one[2])]
        if split is None:
            shape = (4 * depth, columns // 4)
            m = jnp.arange(4, dtype=jnp.int32) ^ lax.axis_index(TENSOR)
            places = (m & 1) * 2 + (m >> 1) if swaps else jnp.arange(4, dtype=jnp.int32)
            ins = [(places, SCALARS)] + ins
            here = run.call(name + "_add3", third_rows, ins, [(shape, LOW, whole(*shape))], moved=6 * depth * columns)[0]
        else:
            shape = (depth, half)
            here = run.call(name + "_add3", third, ins, [(shape, LOW, whole(*shape))] * 2, moved=6 * depth * columns)
    else:

        def near_kernel(left_ref, right_ref, got_ref, *refs):
            value = product(left_ref, right_ref, refs[:-1], 0)
            refs[-1][...] = (value + got_ref[...].astype(WIDE)).astype(LOW)

        here = run.call(
            name + "_near",
            near_kernel,
            near_ins,
            [((middle, columns), LOW, pl.BlockSpec((middle, out_step), lambda j: (0, j)))],
            grid=(2 * steps,),
            **cost,
        )[0].reshape(fsdp // 2, depth, columns)
        count = fsdp // 2
        for bit in bits_of(FSDP)[1:]:
            count //= 2
            (got,) = yield [swap(here[count:], FSDP, bit)]
            here = add_low(here[:count], got)
        if split is None:
            here = here[0].reshape(depth, 4, -1).transpose(1, 0, 2).reshape(4 * depth, -1)
            swaps = False
        else:
            here = (here[0, :, :half], here[0, :, half:])
    if split is None and swaps:
        split = lambda blocks: tuple(blocks.reshape(2, 2, depth, -1))
        here = (here,)
    if split is None:
        (here,) = yield [lax.psum_scatter(here, TENSOR, scatter_dimension=0, tiled=True)]
        store(here.astype(WIDE))
        return
    keep, send = split(*here)
    for bit in bits_of(TENSOR):
        (got,) = yield [swap(send, TENSOR, bit)]
        total = add_low(keep, got)
        keep, send = total[: total.shape[0] // 2], total[total.shape[0] // 2 :]
    store(total[0].astype(WIDE))


def gather_small(gains, sums, store):
    depth = gains.shape[1]
    block = jnp.concatenate([sums, jnp.pad(gains, ((0, 6), (0, 128 - depth)))], axis=0)[None]
    for bit in reversed(bits_of(FSDP)):
        (got,) = yield [swap(block, FSDP, bit)]
        block = jnp.concatenate([block, got], axis=0)
    parts = [block[k, 8:10, :depth] for k in range(block.shape[0])]
    gains = jnp.concatenate(reorder(parts, False) if two_links(depth) else parts, axis=1)
    sums = block[:, :8]
    while sums.shape[0] > 1:
        sums = sums[: sums.shape[0] // 2] + sums[sums.shape[0] // 2 :]
    sums = sums[0]
    for bit in bits_of(TENSOR):
        (got,) = yield [swap(sums, TENSOR, bit)]
        sums = sums + got
    store(gains, sums[0])


def leave_columns(run, name, value, dtype, store):
    size = lax.axis_size(TENSOR)
    (got,) = yield [lax.all_to_all(value, TENSOR, 0, 0, tiled=True)]
    columns, rows = got.shape[0] // size, got.shape[1]

    def kernel(ref, out):
        out[...] = ref[...].astype(dtype)

    store(
        run.call(
            name,
            kernel,
            [(got, pl.BlockSpec((columns, rows), lambda i: (i, 0)))],
            [((columns, size * rows), dtype, pl.BlockSpec((columns, rows), lambda i: (0, i)))],
            grid=(size,),
            moved=8 * columns * rows,
        )[0].T
    )


def put_turned(value, natural, out, tile):
    out[:, tile * TILE : (tile + 1) * TILE] = kernel_nt(natural[...], value).astype(LOW)


def dot(left, right):
    return jnp.dot(left, right, preferred_element_type=WIDE)


def dot_tn(left, right):
    return lax.dot_general(left, right, (((0,), (0,)), ((), ())), preferred_element_type=WIDE)


def dot_nt(left, right):
    return lax.dot_general(left, right, (((1,), (1,)), ((), ())), preferred_element_type=WIDE)


def soft_clip(value):
    return CLIP_RANGE * jnp.tanh(value / CLIP_RANGE)


def clip_slope(value):
    bent = jnp.tanh(value / CLIP_RANGE)
    return 1.0 - bent * bent


def norm_parts(value):
    centre = value - jnp.mean(value, axis=-1, keepdims=True)
    scale = lax.rsqrt(jnp.mean(centre * centre, axis=-1, keepdims=True) + EPSILON)
    return centre * scale, scale


def norm_back(grad, normed, scale):
    return scale * (
        grad
        - jnp.mean(grad, axis=-1, keepdims=True)
        - normed * jnp.mean(grad * normed, axis=-1, keepdims=True)
    )


def gelu_cdf(value):
    return 0.5 + 0.5 * lax.erf(value * math.sqrt(0.5))


def gelu_density(value):
    return jnp.exp(-0.5 * value * value) * (1.0 / math.sqrt(2.0 * math.pi))


def kernel_nt(left, right):
    return lax.dot_general(left, right, (((1,), (1,)), ((), ())), preferred_element_type=WIDE)


def kernel_tn(left, right):
    return lax.dot_general(left, right, (((0,), (0,)), ((), ())), preferred_element_type=WIDE)


def kernel_nn(left, right):
    return jnp.dot(left, right, preferred_element_type=WIDE)


def times_weight(run, name, left, parts, tiles, work, extras, outs):
    rows, width = left.shape
    base, stride = tiles[0], tiles[1] - tiles[0]
    count = len(parts)

    def kernel(*refs):
        weight = refs[-1]
        row = 0
        for block in refs[1 : 1 + count]:
            weight[pl.ds(row, block.shape[0])] = block[...]
            row += block.shape[0]
        for r in range(0, rows, TILE):
            here = pl.ds(r, TILE)
            values = work(kernel_nn(refs[0][here], weight[...]), refs[1 + count : 1 + count + len(extras)], here)
            for ref, value in zip(refs[1 + count + len(extras) : -1], values):
                ref[here] = value

    columns = width * len(tiles)
    return run.call(
        name,
        kernel,
        [(left, whole(rows, width))]
        + [(part, pl.BlockSpec((part.shape[0], width), lambda j: (0, base + stride * j))) for part in parts]
        + extras,
        [((rows, columns), dtype, pl.BlockSpec((rows, width), lambda j: (0, j))) for dtype in outs],
        grid=(len(tiles),),
        scratch=[pltpu.VMEM((width, width), LOW)],
        flops=2 * rows * width * columns,
        moved=2 * (rows * width + width * columns + len(outs) * rows * columns),
    )


def times_turned(run, name, left, parts, tiles, work, extras, late, outs):
    rows, wide = left.shape
    width = sum(part.shape[0] for part in parts)
    step = wide // len(tiles)
    base, stride = tiles[0], tiles[1] - tiles[0] if len(tiles) > 1 else 1
    count, more = len(parts), len(extras)
    sources, held = [], []
    for item in late:
        pieces, column = item if isinstance(item, tuple) else ([item], 0)
        columns = pieces[0].shape[1] if column == 0 and not isinstance(item, tuple) else width
        row = 0
        for piece in pieces:
            sources.append((piece, len(held), row, column, columns))
            row += piece.shape[0]
        held.append(pltpu.VMEM((row, columns), pieces[0].dtype))
    first_late = 1 + count + more
    first_out = first_late + len(sources)
    first_held = first_out + len(outs) + 2

    def kernel(*refs):
        total, weight = refs[first_out + len(outs)], refs[first_out + len(outs) + 1]
        scratch, sems = refs[first_held:-1], refs[-1]
        j = pl.program_id(0)
        copies = []
        for k, (piece, to, row, column, columns) in enumerate(sources):
            copies.append(
                pltpu.make_async_copy(
                    refs[first_late + k].at[:, pl.ds(column, columns)],
                    scratch[to].at[pl.ds(row, piece.shape[0])],
                    sems.at[k],
                )
            )

        @pl.when(j == 0)
        def _():
            for copy in copies:
                copy.start()

        row = 0
        for block in refs[1 : 1 + count]:
            weight[pl.ds(row, block.shape[0])] = block[...]
            row += block.shape[0]
        product = kernel_nt(refs[0][...], weight[...])

        @pl.when(j == 0)
        def _():
            total[...] = product

        @pl.when(j > 0)
        def _():
            total[...] = total[...] + product

        @pl.when(j == len(tiles) - 1)
        def _():
            for copy in copies:
                copy.wait()
            for tile in range(rows // TILE):
                work(
                    total[pl.ds(tile * TILE, TILE)],
                    list(refs[1 + count : first_late]) + list(scratch),
                    refs[first_out : first_out + len(outs)],
                    tile,
                )

    return run.call(
        name,
        kernel,
        [(left, pl.BlockSpec((rows, step), lambda j: (0, j)))]
        + [(part, pl.BlockSpec((part.shape[0], step), lambda j: (0, base + stride * j))) for part in parts]
        + extras
        + [(piece, IN_PLACE) for piece, _, _, _, _ in sources],
        [(shape, dtype, whole(*shape)) for shape, dtype in outs],
        grid=(len(tiles),),
        scratch=[pltpu.VMEM((rows, width), WIDE), pltpu.VMEM((width, step), LOW)]
        + held
        + [pltpu.SemaphoreType.DMA((max(len(sources), 1),))],
        flops=2 * rows * width * wide,
        moved=2 * (rows * wide + width * wide),
    )


def rows_at(tile):
    return pl.ds(tile * TILE, TILE)


def tile_rows(columns):
    return pl.BlockSpec((TILE, columns), lambda i: (i, 0))


def add_column_sums(ref, value, tile):
    total = jnp.sum(value.reshape(value.shape[0] // 8, 8, value.shape[1]), axis=0)
    ref[...] = total if tile == 0 else ref[...] + total


def both_heads(value):
    first = lax.broadcasted_iota(jnp.int32, (1, PAIR), 1) < HEAD_DIM
    zero = jnp.zeros((), value.dtype)
    return jnp.concatenate([jnp.where(first, value, zero), jnp.where(first, zero, value)], axis=0)


def own_heads(value):
    return jnp.concatenate([value[:HEAD_DIM, :TILE], value[HEAD_DIM:, TILE:]], axis=0).T


def attend_forward(qid, kid, qs, ks, vs, qt, kt, vt, os, ot, probs_out, gap_out):
    keep = kid[:, 0:1] == qid[0:1, :]
    both = keep & (qid[1:2, :] > 0)
    bias = jnp.where(keep, 0.0, NEG_FILL)
    bias = jnp.concatenate([bias, bias], axis=1)
    seen = jnp.where(both, 1.0, 0.0)
    seen = jnp.concatenate([seen, seen], axis=1)

    def soft(score):
        masked = score + bias
        expo = jnp.exp(masked - jnp.max(masked, axis=0, keepdims=True))
        return (expo * (1.0 / jnp.sum(expo, axis=0, keepdims=True))).astype(LOW)

    for p in range(qs.shape[1] // PAIR):
        here = slice(p * PAIR, (p + 1) * PAIR)
        score_s = kernel_nt(ks[:, here], both_heads(qs[:, here]))
        score_t = kernel_nt(kt[:, here], both_heads(qt[:, here]))
        gap_out[0, p] = ((score_s - score_t) * seen).astype(LOW)
        probs = soft(score_s)
        probs_out[0, p] = probs
        os[:, here] = own_heads(kernel_tn(vs[:, here], probs)).astype(LOW)
        ot[:, here] = own_heads(kernel_tn(vt[:, here], soft(score_t))).astype(LOW)


def attend_backward(betas, proj, grad, probs, gap, out):
    width = grad.shape[1]
    up = jnp.asarray(1.0 / ATT_WEIGHT, LOW)
    b = betas[0] * ATT_WEIGHT
    scale = HEAD_DIM ** (-0.5)
    for p in range(width // PAIR):
        at_q = slice(p * PAIR, (p + 1) * PAIR)
        at_k = slice(width + p * PAIR, width + (p + 1) * PAIR)
        at_v = slice(2 * width + p * PAIR, 2 * width + (p + 1) * PAIR)
        grad_two = both_heads(grad[:, at_q] * up)
        prob_low = probs[0, p]
        prob = prob_low.astype(WIDE)
        weighted = prob * kernel_nt(proj[:, at_v], grad_two)
        inner = jnp.sum(weighted, axis=0, keepdims=True)
        d_score = (weighted - prob * inner + gap[0, p].astype(WIDE)).astype(LOW)
        out[:, at_v] = (b * kernel_nn(prob_low, grad_two)).astype(LOW)
        out[:, at_k] = (b * kernel_nn(d_score, both_heads(proj[:, at_q]))).astype(LOW)
        out[:, at_q] = own_heads((b * scale) * kernel_tn(proj[:, at_k], d_score)).astype(LOW)


def run_forward(run, step, steps, onto, qid, kid, proj_s, proj_t):
    rows, wide = proj_s.shape
    width = wide // 3
    pairs = width // PAIR
    tiles = rows // TILE

    def part(j):
        return pl.BlockSpec((TILE, width // steps), lambda b: (b, j * steps + step))

    square = pl.BlockSpec((1, pairs // steps, TILE, 2 * TILE), lambda b: (b, step, 0, 0))
    return run.call(
        "attend_forward",
        attend_forward,
        [(qid, pl.BlockSpec((8, TILE), lambda b: (0, b))), (kid, pl.BlockSpec((TILE, 128), lambda b: (b, 0)))]
        + [(value, part(j)) for value in (proj_s, proj_t) for j in range(3)],
        [((rows, width), LOW, part(0))] * 2 + [((tiles, pairs, TILE, 2 * TILE), LOW, square)] * 2,
        grid=(tiles,),
        flops=32 * rows * TILE * width // steps,
        moved=8 * rows * wide // steps,
        onto=onto,
    )


def run_backward(run, betas, proj_s, grad, probs, gap):
    rows, wide = proj_s.shape
    width = wide // 3
    pairs = width // PAIR
    square = pl.BlockSpec((1, pairs, TILE, 2 * TILE), lambda b: (b, 0, 0, 0))
    return run.call(
        "attend_backward",
        attend_backward,
        [(betas, SCALARS), (proj_s, tile_rows(wide)), (grad, tile_rows(width)), (probs, square), (gap, square)],
        [((rows, wide), LOW, tile_rows(wide))],
        grid=(rows // TILE,),
        flops=16 * rows * TILE * width,
        moved=8 * rows * wide,
    )[0]


def body(
    student_in,
    teacher_in,
    bucket_size,
    seq_length,
    qkv_latent,
    out_latent,
    up_latent,
    down_latent,
    gain_attn,
    gain_ffn,
    teach_qkv,
    teach_out,
    teach_up,
    teach_down,
):
    width = student_in.shape[1]
    fsdp = lax.axis_size(FSDP)
    tensor = lax.axis_size(TENSOR)
    rows = student_in.shape[0] // tensor
    depth = width // fsdp
    hidden_width = up_latent.shape[1] * tensor
    my_fsdp = lax.axis_index(FSDP)
    my_tensor = lax.axis_index(TENSOR)
    first_row = my_tensor * rows
    order = feature_order(depth)
    order_t = order_of(TENSOR)

    have = types.SimpleNamespace()
    run = Order()

    def keep(name):
        def store(value):
            setattr(have, name, value)

        return store

    def go_on(*tasks):
        for task in tasks:
            task.go_on()

    def finish(*tasks):
        for task in tasks:
            task.finish()

    gains = jnp.stack([gain_attn, gain_ffn]).astype(WIDE)

    def magnitudes():
        latents = (qkv_latent.reshape(-1, qkv_latent.shape[2]), out_latent, up_latent, down_latent)

        def kernel(*refs):
            lane = lax.broadcasted_iota(jnp.int32, (8, 128), 1)
            total = jnp.zeros((8, 128), WIDE)
            for k in range(4):
                total = jnp.where(lane == k, jnp.sum(jnp.abs(refs[k][...])), total)
            refs[4][...] = total

        return run.call(
            "magnitudes", kernel, [(value, whole(*value.shape)) for value in latents], [((8, 128), WIDE, whole(8, 128))]
        )[0]

    def pack_qkv(value):
        return value.astype(LOW).transpose(1, 0, 2).reshape(depth, -1)

    part = width // tensor

    def finish_qkv(name, near, far):
        moves = []
        for p in range(tensor):
            for k in range(4):
                moves.append((p // 2, (p % 2) * 4 * part + k * part, k * width + p * part, part))
        return join_columns(run, name, [near, far], moves, 4 * width)

    narrow_tiles = [0, 1, 2]

    def wide_tiles(which):
        return [2 * p + which for p in range(tensor)]

    def signs(value):
        return jnp.sign(value).astype(LOW)


    def shard_tqkv():
        return jnp.concatenate([pack_qkv(teach_qkv), teach_out.T], axis=1)

    def shard_qkv():
        return jnp.concatenate([pack_qkv(signs(qkv_latent)), signs(out_latent).T], axis=1)

    def pack_signs(name, teach, latent):
        def kernel(teach_ref, latent_ref, out):
            value = latent_ref[...]
            n = value.shape[1]
            out[:, :n] = teach_ref[...]
            out[:, n:] = jnp.where(value > 0, 1.0, jnp.where(value < 0, -1.0, 0.0)).astype(LOW)

        r, n = teach.shape
        return run.call(
            name, kernel, [(teach, whole(r, n)), (latent, whole(r, n))], [((r, 2 * n), LOW, whole(r, 2 * n))]
        )[0]

    def shard_up():
        return pack_signs("pack_up", teach_up, up_latent)

    def shard_down():
        return pack_signs("pack_down", teach_down.T, down_latent.T)

    def small_store(all_gains, totals):
        have.first_gain = all_gains[0:1]
        have.second_gain = all_gains[1:2]
        factors = (
            2.0 / (3 * width * width) / math.sqrt(width),
            2.0 / (width * width) / math.sqrt(width),
            2.0 / (width * hidden_width) / math.sqrt(width),
            2.0 / (width * hidden_width) / math.sqrt(hidden_width),
        )
        have.betas = totals[:4] * jnp.array(factors, WIDE)

    packed = ((width, rows), LOW)

    def prepare():
        scalars = jnp.concatenate([my_tensor.reshape(1), order ^ my_fsdp]).astype(jnp.int32)

        def kernel(where, student, teacher, x_low, entry, xt_low, to_place, rows_s, rows_t, sems):
            start = pl.multiple_of(where[0] * rows, rows)
            copies = [
                pltpu.make_async_copy(ref.at[pl.ds(start, rows)], to, sems.at[k])
                for k, (ref, to) in enumerate(((student, rows_s), (teacher, rows_t)))
            ]
            for copy in copies:
                copy.start()
            natural = lax.broadcasted_iota(jnp.int32, (width, width), 0)
            place = lax.broadcasted_iota(jnp.int32, (1, width), 1)
            source = place
            for k in range(fsdp):
                inside = (place >= k * depth) & (place < (k + 1) * depth)
                source = jnp.where(inside, place + (where[1 + k] - k) * depth, source)
            to_place[...] = jnp.where(natural == source, 1.0, 0.0).astype(LOW)
            copies[0].wait()
            x = kernel_nn(rows_s[...], to_place[...])
            x_low[...] = x.astype(LOW)
            entry[...] = soft_clip(x).astype(LOW)
            copies[1].wait()
            xt_low[...] = kernel_nn(rows_t[...], to_place[...]).astype(LOW)

        full = ((rows, width), LOW, whole(rows, width))
        have.x_low, have.entry, have.xt_low, have.leave = run.call(
            "place_rows",
            kernel,
            [
                (scalars, SCALARS),
                (student_in, IN_PLACE),
                (teacher_in, IN_PLACE),
            ],
            [full, full, full, ((width, width), LOW, whole(width, width))],
            scratch=[pltpu.VMEM((rows, width), LOW), pltpu.VMEM((rows, width), LOW), pltpu.SemaphoreType.DMA((2,))],
        )

    def prepare_slots():
        units = rows // 64
        first_unit = my_tensor * units

        def kernel(first, sizes, lengths, qid, kid, live_rows):
            for u in range(units):
                unit = first[0] + u
                slot = unit * 64
                size, length = sizes[unit], lengths[unit]
                begin = slot - lax.rem(slot, size)
                here = slice(u * 64, (u + 1) * 64)
                down = slot - begin + lax.broadcasted_iota(jnp.int32, (64, 128), 0)
                kid[here] = jnp.where(down < length, begin, -1)
                live_rows[here] = jnp.where(down < length, 1.0, 0.0)
                across = slot - begin + lax.broadcasted_iota(jnp.int32, (8, 64), 1)
                row = lax.broadcasted_iota(jnp.int32, (8, 64), 0)
                qid[:, here] = jnp.where(row == 0, begin, jnp.where(across < length, 1, 0))

        have.qid, have.kid, have.live_rows = run.call(
            "slots",
            kernel,
            [
                (first_unit.astype(jnp.int32).reshape(1), SCALARS),
                (bucket_size, SCALARS),
                (seq_length, SCALARS),
            ],
            [
                ((8, rows), jnp.int32, whole(8, rows)),
                ((rows, 128), jnp.int32, whole(rows, 128)),
                ((rows, 128), WIDE, whole(rows, 128)),
            ],
        )

    scale = HEAD_DIM ** (-0.5)

    def project_teacher():
        def work(product, refs, here):
            factor = jnp.where(pl.program_id(0) == 0, scale, 1.0)
            return [(product.astype(LOW) * factor.astype(LOW)).astype(LOW)]

        have.proj_t = times_weight(
            run, "project_teacher", have.xt_low, have.w_tqkv, narrow_tiles, work, [], [LOW]
        )[0]

    def project_student():
        def work(product, refs, here):
            factor = jnp.where(pl.program_id(0) == 0, scale, 1.0)
            return [((refs[0][0] * product).astype(LOW) * factor.astype(LOW)).astype(LOW)]

        have.proj_s = times_weight(
            run, "project_student", have.entry, have.w_qkv, narrow_tiles, work,
            [(have.betas, SCALARS)], [LOW],
        )[0]

    def attend(step):
        onto = [have.attended, have.t_attended, have.probs, have.gap] if step else []
        have.attended, have.t_attended, have.probs, have.gap = run_forward(
            run, step, 2, onto, have.qid, have.kid, have.proj_s, have.proj_t
        )

    square = ((rows, width), WIDE)
    square_low = ((rows, width), LOW)

    def close_teacher():
        def work(product, refs, outs, tile):
            here = rows_at(tile)
            normed, _ = norm_parts(refs[0][here].astype(WIDE) + product)
            outs[0][here] = normed
            outs[1][here] = normed.astype(LOW)

        have.t_first, have.t_first_low = times_turned(
            run, "close_teacher", have.t_attended, have.w_tqkv, [3], work,
            [], [have.xt_low], [square, square_low],
        )

    def close_student():
        def work(product, refs, outs, tile):
            betas, gain, x = refs
            here = rows_at(tile)
            normed, size = norm_parts(x[here].astype(WIDE) + betas[1] * product)
            outs[0][here] = normed
            outs[1][here] = jnp.broadcast_to(size, (TILE, 128))
            outs[2][here] = soft_clip(normed * gain[...]).astype(LOW)

        have.n_first, have.r_first, have.middle = times_turned(
            run, "close_student", have.attended, have.w_qkv, [3], work,
            [(have.betas, SCALARS), (have.first_gain, whole(1, width))],
            [have.x_low],
            [square, ((rows, 128), WIDE), square_low],
        )

    def up_teacher():
        def work(product, refs, here):
            return [(product * gelu_cdf(product)).astype(LOW)]

        have.t_hidden = times_weight(
            run, "up_teacher", have.t_first_low, have.w_up, wide_tiles(0), work, [], [LOW]
        )[0]

    def up_student():
        def work(product, refs, here):
            up = refs[0][2] * product
            cdf = gelu_cdf(up)
            return [(up * cdf).astype(LOW), (cdf + up * gelu_density(up)).astype(LOW)]

        have.hidden, have.slope = times_weight(
            run, "up_student", have.middle, have.w_up, wide_tiles(1), work,
            [(have.betas, SCALARS)], [LOW, LOW],
        )

    def down_teacher():
        def work(product, refs, outs, tile):
            here = rows_at(tile)
            normed, _ = norm_parts(refs[0][here] + product)
            outs[0][here] = normed
            put_turned(normed.astype(LOW), refs[1], outs[1], tile)

        have.t_result, have.t_leave = times_turned(
            run, "down_teacher", have.t_hidden, have.w_down, wide_tiles(0), work,
            [], [have.t_first, have.leave], [square, packed],
        )

    def down_student():
        def work(product, refs, outs, tile):
            betas, first_gain, second_gain, n_first, t_result, live_rows, leave = refs
            here = rows_at(tile)
            normed, size = norm_parts(n_first[here] * first_gain[...] + betas[3] * product)
            result = normed * second_gain[...]
            d_result = jnp.where(live_rows[here][:, 0:1] > 0, result - t_result[here], 0.0)
            add_column_sums(outs[2], d_result * normed, tile)
            d_second = norm_back(d_result * second_gain[...], normed, size)
            outs[0][here] = d_second
            outs[1][here] = (betas[3] * d_second).astype(LOW)
            put_turned(result.astype(LOW), leave, outs[3], tile)

        have.d_second, have.grad_z, have.sums_second, have.s_leave = times_turned(
            run, "down_student", have.hidden, have.w_down, wide_tiles(1), work,
            [
                (have.betas, SCALARS),
                (have.first_gain, whole(1, width)),
                (have.second_gain, whole(1, width)),
            ],
            [have.n_first, have.t_result, have.live_rows, have.leave],
            [square, square_low, ((8, width), WIDE), packed],
        )


    def split_one(a, b):
        return tuple(value.reshape(depth, tensor // 2, -1).transpose(1, 0, 2) for value in (a, b))

    def split_qkv(a, b):
        value = jnp.concatenate([a, b], axis=1).reshape(depth, 3, tensor, part).transpose(2, 0, 1, 3)
        value = value.reshape(tensor, depth, 3 * part)
        return value[: tensor // 2], value[tensor // 2 :]

    def share_down():
        return Task(scatter_weight(run, "g_down", have.grad_z, have.hidden, None, keep("grad_down")))

    def back_down():
        def work(product, refs, here):
            return [(refs[0][2] * (product * refs[1][here].astype(WIDE))).astype(LOW)]

        have.grad_u = times_weight(
            run, "back_down", have.grad_z, have.w_down, wide_tiles(1), work,
            [(have.betas, SCALARS), (have.slope, pl.BlockSpec((rows, width), lambda j: (0, j)))],
            [LOW],
        )[0]

    def share_up():
        return Task(scatter_weight(run, "g_up", have.middle, have.grad_u, None, keep("grad_up"), swaps=True))

    def back_up():
        def work(product, refs, outs, tile):
            betas, gain, d_second, n_first, r_first, w_out = refs
            here = rows_at(tile)
            normed = n_first[here]
            d_h = d_second[here] + product * clip_slope(normed * gain[...])
            add_column_sums(outs[3], d_h * normed, tile)
            d_first = norm_back(d_h * gain[...], normed, r_first[here][:, 0:1])
            outs[0][here] = d_first
            grad_o = (betas[1] * d_first).astype(LOW)
            outs[1][here] = grad_o
            outs[2][here] = kernel_nn(grad_o, w_out[...]).astype(LOW)

        have.d_first, have.grad_o, have.d_attended, have.sums_first = times_turned(
            run, "back_up", have.grad_u, have.w_up, wide_tiles(1), work,
            [(have.betas, SCALARS), (have.first_gain, whole(1, width))],
            [have.d_second, have.n_first, have.r_first, (have.w_qkv, 3 * width)],
            [square, square_low, square_low, ((8, width), WIDE)],
        )

    def share_out():
        beside = (have.sums_first, have.sums_second)
        return Task(
            scatter_weight(run, "g_out", have.grad_o, have.attended, split_one, keep("grad_out"), beside)
        )

    def back_attend():
        have.g_all = run_backward(
            run, have.betas, have.proj_s, have.d_attended, have.probs, have.gap
        )

    def share_qkv():
        return Task(scatter_weight(run, "g_qkv", have.entry, have.g_all, split_qkv, keep("grad_qkv")))

    def back_entry():
        def work(product, refs, outs, tile):
            here = rows_at(tile)
            x = refs[1][here].astype(WIDE)
            put_turned((refs[0][here] + product * clip_slope(x)).astype(LOW), refs[2], outs[0], tile)

        have.g_leave = times_turned(
            run, "back_entry", have.g_all, have.w_qkv, narrow_tiles, work,
            [], [have.d_first, have.x_low, have.leave], [packed],
        )[0]

    def bring(name, shard, finish_rows):
        return Task(gather_weight(run, name, shard, finish_rows, keep(name)))

    ta = bring("w_tqkv", shard_tqkv, finish_qkv)
    sa = bring("w_qkv", shard_qkv, finish_qkv)
    c = bring("w_up", shard_up, None)
    d = bring("w_down", shard_down, None)
    go_on(ta)
    run.wait(run.shards[0])
    small = Task(gather_small(gains, magnitudes(), small_store))
    go_on(sa)
    go_on(small)
    run.land(small)
    prepare_slots()
    go_on(small)
    run.land(small)
    go_on(ta)
    go_on(small)
    prepare()
    run.land(small)
    go_on(sa)
    go_on(ta)
    run.land(sa)
    go_on(c)
    go_on(d)
    run.land(ta, only=0)
    go_on(sa)
    go_on(small)
    run.land(ta, only=1)
    run.land(small)
    run.fence()
    go_on(ta)
    go_on(small)
    run.land(sa, small)
    run.fence()
    finish(small)
    finish(ta)
    go_on(sa)
    go_on(c)
    project_teacher()
    finish(sa)
    project_student()
    attend(0)
    run.land(c, d)
    run.fence()
    go_on(c)
    attend(1)
    go_on(d)
    close_teacher()
    run.land(c)
    close_student()
    finish(c)
    run.land(d, only=0)
    up_teacher()
    up_student()
    run.land(d, only=1)
    run.fence()
    finish(d)
    down_teacher()
    t_leave = Task(leave_columns(run, "arrive_teacher", have.t_leave, LOW, keep("teacher_out")))
    go_on(t_leave)
    down_student()
    s_leave = Task(leave_columns(run, "arrive_student", have.s_leave, LOW, keep("student_out")))
    down = share_down()
    go_on(down)
    back_down()
    run.land(t_leave)
    up = share_up()
    go_on(up)
    go_on(s_leave)
    go_on(down)
    go_on(up)
    back_up()
    run.land(s_leave)
    back_attend()
    go_on(down)
    qkv = share_qkv()
    go_on(qkv)
    go_on(up)
    back_entry()
    g_leave = Task(leave_columns(run, "arrive_grad", have.g_leave, WIDE, keep("input_grad")))
    go_on(g_leave)
    go_on(qkv)
    go_on(down)
    go_on(up)
    out = share_out()
    go_on(out)
    finish(t_leave)
    run.land(qkv)
    go_on(out)
    go_on(qkv)
    run.land(up)
    finish(s_leave)
    go_on(up)
    go_on(out)
    run.land(qkv, down)
    finish(g_leave)
    go_on(qkv)
    go_on(out)
    finish(qkv)
    finish(out)
    finish(up)
    finish(down)

    def inside(grad, latent):
        return jnp.where(jnp.abs(latent) <= 1.0, grad, 0.0)

    return (
        have.student_out,
        have.teacher_out,
        have.input_grad,
        inside(have.grad_qkv.reshape(depth, 3, part).transpose(1, 0, 2), qkv_latent),
        inside(have.grad_out[:, :part].T, out_latent),
        inside(have.grad_up, up_latent),
        inside(have.grad_down.T, down_latent),
        have.grad_out[:, part],
        have.grad_out[:, part + 1],
    )


def solution(mesh):
    placed = (
        P(FSDP, None),
        P(FSDP, None),
        P(FSDP),
        P(FSDP),
        P(None, FSDP, TENSOR),
        P(TENSOR, FSDP),
        P(FSDP, TENSOR),
        P(TENSOR, FSDP),
        P(FSDP),
        P(FSDP),
        P(None, FSDP, TENSOR),
        P(TENSOR, FSDP),
        P(FSDP, TENSOR),
        P(TENSOR, FSDP),
    )
    return jax.shard_map(
        body,
        mesh=mesh,
        in_specs=placed,
        out_specs=(
            P(FSDP, TENSOR),
            P(FSDP, TENSOR),
            P(FSDP, TENSOR),
            P(None, FSDP, TENSOR),
            P(TENSOR, FSDP),
            P(FSDP, TENSOR),
            P(TENSOR, FSDP),
            P(FSDP),
            P(FSDP),
        ),
        check_vma=False,
    )
```

time: 2340 us -> 435 us (0.19)
  waiting for transfers between devices: 1490 us -> 87.3 us
  matrix products: 431 us -> 0 us
  Pallas kernels: 0 us -> 221 us
  blocking collectives: 124 us -> 0 us
  other arithmetic: 124 us -> 11.4 us
  local copies, waits for them, and re-layouts: 133 us -> 31.1 us
  starting transfers between devices: 1.86 us -> 62.1 us
    psum x4 -> x0, waiting for transfers between devices: 1420 us -> none  [the longest x2 1250 us: head_total(): return lax.psum((student_part, teacher_part), 'tensor')]
    dot_general x123 -> x0, matrix products: 413 us -> none  [the longest x33 138 us: product(): return jnp.dot(left, right, preferred_element_type=jnp.float32)]
    pallas_call x0 -> x48, Pallas kernels: none -> 221 us  [call(): pl.pallas_call(wrapped, grid=grid, in_specs=[spec for _, spec in ins] + [...]
    ppermute x0 -> x55, waiting for transfers between devices: none -> 84.1 us  [the longest x35 42.9 us: swap(): return lax.ppermute(value, axis, [(i, i ^ bit) for i in range(size)])]
    reduce_sum x28 -> x0, other arithmetic: 79.9 us -> none  [the longest x8 47.9 us: layer_norm(): centre = value - jnp.mean(value, axis=-1, keepdims=True)]
    unnamed x26 -> x3, waiting for transfers between devices: 71.6 us -> 0.05 us
    unnamed x345 -> x121, local copies, waits for them, and re-layouts: 83.2 us -> 24.3 us
    ppermute x0 -> x55, starting transfers between devices: none -> 50.3 us  [the longest x35 29.2 us: swap(): return lax.ppermute(value, axis, [(i, i ^ bit) for i in range(size)])]
  transfers between devices with their start and end apart: 20 -> 61, of which waited for: 6 -> 26; matrix products, arithmetic and copies ran while one was open for 19% -> 4% of each run, Pallas kernels for 0% -> 48%
where the time goes in v1:
time: 435 us; the launch traced here: 428 us
  Pallas kernels  221 us (51%)
  waiting for transfers between devices  87.3 us (20%)
  starting transfers between devices  62.1 us (14%)
  local copies, waits for them, and re-layouts  31.1 us (7%)
  between operations  14.6 us (3%)
  other arithmetic  11.4 us (3%)
    pallas_call x48, Pallas kernels, call(): pl.pallas_call(wrapped, grid=grid, in_specs=[spec for _, spec in ins] + [...  221 us
    ppermute x35, waiting for transfers between devices, swap(): return lax.ppermute(value, axis, [(i, i ^ bit) for i in range(size)])  42.9 us
    ppermute x16, waiting for transfers between devices, swap_first(): lax.ppermute(value, FSDP, [(i, i ^ (4 if i % 2 else 2)) for i in range(8)])  41.2 us
    ppermute x35, starting transfers between devices, swap(): return lax.ppermute(value, axis, [(i, i ^ bit) for i in range(size)])  29.2 us
    unnamed x121, local copies, waits for them, and re-layouts  24.3 us
    ppermute x16, starting transfers between devices, swap_first(): lax.ppermute(value, FSDP, [(i, i ^ (4 if i % 2 else 2)) for i in range(8)])  17.8 us
    all_to_all x3, starting transfers between devices, leave_columns(): got, = (yield [lax.all_to_all(value, TENSOR, 0, 0, tiled=True)])  11.6 us
  transfers between devices with their start and end apart: 61, of which 26 were waited for; matrix products, arithmetic and copies ran while one was open for 4% of the time, Pallas kernels for 48%

profile of v1, /device:TPU:0, one launch (start us, length us, event | category | flops | bytes accessed | tf_op | source)
XLA Modules:
  0.0 427.9 jit_solution(762311418112296093)
XLA Ops:
  9.6 4.1 collective-permute-start.1
  14.6 2.1 magnitudes.1.refs_4_
  26.1 1.7 collective-permute-done.2.refs_2_
  33.1 5.8 %place_rows.1 = (bf16[768,768]{1,0:T(8,128)(2,1)}, bf16[768,768]{1,0:T(8,128)(2,1)}, bf16[768,768]{1,0:T(8,128)(2,1)}, bf16[768,768]{1,0:T(8,128)(2,1)}) custom-call(s32[9]{0:T(128)} %pad_add_fusion.refs_0_, bf16[3072,768]{1,0:T(8,128)(2,1)} %refs_1_.6, bf16[3072,768]{1,0:T(8,128)(2,1)} %refs_2_.5, bf16[96,1536]{1,0:T(8,128)(2,1)} %get-tuple-element.100.refs_3_.refs_0_), custom_call_target="tpu_custom_call" | custom-call | tf_op jit(solution)/shard_map/place_rows/pallas_call | solution.py:80
  39.6 1.7 w_qkv_join.1
  42.0 2.0 w_tqkv_rows.1.refs_3_.refs_1_
  46.2 8.7 %collective-permute-done.9.refs_2_ = bf16[96,1536]{1,0:T(8,128)(2,1)S(1)} collective-permute-done((bf16[96,1536]{1,0:T(8,128)(2,1)S(1)}, bf16[96,1536]{1,0:T(8,128)(2,1)S(1)}, u32[]{:S(2)}, u32[]{:S(2)}) %collective-permute-start.9) | collective-permute-done | bytes 294944 | tf_op jit(solution)/shard_map/ppermute | solution.py:107
  55.7 1.8 pack_up.1
  57.5 1.8 pack_down.1.refs_3_
  60.1 2.1 w_qkv_rows.1
  67.2 5.1 %collective-permute-done.7.refs_0_ = bf16[96,3072]{1,0:T(8,128)(2,1)S(1)} collective-permute-done((bf16[96,3072]{1,0:T(8,128)(2,1)}, bf16[96,3072]{1,0:T(8,128)(2,1)S(1)}, u32[]{:S(2)}, u32[]{:S(2)}) %collective-permute-start.7) | collective-permute-done | bytes 589856 | tf_op jit(solution)/shard_map/ppermute | solution.py:111
  75.3 3.3 collective-permute-done.11.refs_0_
  79.1 5.9 %collective-permute-done.13.refs_1_ = bf16[96,3072]{1,0:T(8,128)(2,1)S(1)} collective-permute-done((bf16[96,3072]{1,0:T(8,128)(2,1)}, bf16[96,3072]{1,0:T(8,128)(2,1)S(1)}, u32[]{:S(2)}, u32[]{:S(2)}) %collective-permute-start.13) | collective-permute-done | bytes 589856 | tf_op jit(solution)/shard_map/ppermute | solution.py:111
  89.9 6.5 %collective-permute-done.20.refs_4_ = bf16[96,3072]{1,0:T(8,128)(2,1)} collective-permute-done((bf16[96,3072]{1,0:T(8,128)(2,1)S(1)}, bf16[96,3072]{1,0:T(8,128)(2,1)}, u32[]{:S(2)}, u32[]{:S(2)}) %collective-permute-start.20) | collective-permute-done | bytes 589856 | tf_op jit(solution)/shard_map/ppermute | solution.py:111
  98.2 2.4 w_up_rows.1.refs_9_.refs_1_
  102.7 7.2 %project_teacher.1.refs_10_.refs_5_.refs_6_.refs_7_ = bf16[768,2304]{1,0:T(8,128)(2,1)} custom-call(bf16[768,768]{1,0:T(8,128)(2,1)} %get-tuple-element.113.refs_0_.refs_9_, bf16[96,3072]{1,0:T(8,128)(2,1)} %w_tqkv_rows.1.refs_3_.refs_1_, bf16[96,3072]{1,0:T(8,128)(2,1)} %get-tuple-element.114.refs_2_, bf16[96,3072]{1,0:T(8,128)(2,1)} %copy-done.55, ...), custom_call_target="tpu_custom_call" | custom-call | flops 13589544960 | bytes 41287680 | tf_op jit(solution)/shard_map/project_teacher/pallas_call | solution.py:80
  111.3 7.0 %project_student.1.refs_2_.refs_3_.refs_4_.refs_8_.refs_1_ = bf16[768,2304]{1,0:T(8,128)(2,1)} custom-call(bf16[768,768]{1,0:T(8,128)(2,1)} %get-tuple-element.110.refs_0_, bf16[96,3072]{1,0:T(8,128)(2,1)} %get-tuple-element.106.refs_2_.refs_1_.refs_14_, bf16[96,3072]{1,0:T(8,128)(2,1)} %get-tuple-element.111.refs_2_.refs_15_, ...), custom_call_target="tpu_custom_call" | custom-call | flops 13589544960 | bytes 41287680 | tf_op jit(solution)/shard_map/project_student/pallas_call | solution.py:80
  118.3 8.5 %attend_forward.2 = (bf16[768,768]{1,0:T(8,128)(2,1)}, bf16[768,768]{1,0:T(8,128)(2,1)}, bf16[3,6,256,512]{3,2,1,0:T(8,128)(2,1)}, bf16[3,6,256,512]{3,2,1,0:T(8,128)(2,1)}) custom-call(s32[8,768]{1,0:T(8,128)} %get-tuple-element.98.refs_3_.refs_0_, s32[768,128]{1,0:T(8,128)} %get-tuple-element.117.refs_1_, ...), custom_call_target="tpu_custom_call" | custom-call | flops 12079595520 | bytes 35389440 | tf_op jit(solution)/shard_map/attend_forward/pallas_call | solution.py:80
  126.9 2.8 collective-permute-done.25.refs_1_
  135.7 8.5 %attend_forward.3 = (bf16[768,768]{1,0:T(8,128)(2,1)}, bf16[768,768]{1,0:T(8,128)(2,1)}, bf16[3,6,256,512]{3,2,1,0:T(8,128)(2,1)}, bf16[3,6,256,512]{3,2,1,0:T(8,128)(2,1)}) custom-call(s32[8,768]{1,0:T(8,128)} %get-tuple-element.98.refs_3_.refs_0_, ...), custom_call_target="tpu_custom_call", output_to_operand_aliasing={{0}: (8, {}), {1}: (9, {}), {2}: (10, {}), {3}: (11, {})} | custom-call | flops 12079595520 | bytes 35389440 | tf_op jit(solution)/shard_map/attend_forward/pallas_call | solution.py:80
  144.1 2.4 w_down_rows.1.refs_10_.refs_1_
  147.3 5.6 %close_teacher.1 = (f32[768,768]{1,0:T(8,128)}, bf16[768,768]{1,0:T(8,128)(2,1)}) custom-call(bf16[768,768]{1,0:T(8,128)(2,1)} %get-tuple-element.126.refs_0_, bf16[96,3072]{1,0:T(8,128)(2,1)} %w_tqkv_rows.1.refs_3_.refs_1_, bf16[96,3072]{1,0:T(8,128)(2,1)} %get-tuple-element.114.refs_2_, bf16[96,3072]{1,0:T(8,128)(2,1)} %copy-done.55, ...), custom_call_target="tpu_custom_call" | custom-call | flops 4529848320 | bytes 11796480 | tf_op jit(solution)/shard_map/close_teacher/pallas_call | solution.py:80
  154.3 6.0 %close_student.1 = (f32[768,768]{1,0:T(8,128)}, f32[768,128]{1,0:T(8,128)}, bf16[768,768]{1,0:T(8,128)(2,1)}, bf16[96,6144]{1,0:T(8,128)(2,1)}, bf16[96,6144]{1,0:T(8,128)(2,1)}) custom-call(bf16[768,768]{1,0:T(8,128)(2,1)} %get-tuple-element.123.refs_1_.refs_0_, ...), custom_call_target="tpu_custom_call", output_to_operand_aliasing={{3}: (12, {}), {4}: (13, {})} | custom-call | flops 4529848320 | bytes 11796480 | tf_op jit(solution)/shard_map/close_student/pallas_call | solution.py:80
  164.6 8.3 %up_teacher.1 = (bf16[768,3072]{1,0:T(8,128)(2,1)}, bf16[96,6144]{1,0:T(8,128)(2,1)}) custom-call(bf16[768,768]{1,0:T(8,128)(2,1)} %get-tuple-element.132.refs_0_, bf16[96,6144]{1,0:T(8,128)(2,1)} %w_up_rows.1.refs_9_.refs_1_, bf16[96,6144]{1,0:T(8,128)(2,1)} %get-tuple-element.124.refs_2_, ...), custom_call_target="tpu_custom_call", output_to_operand_aliasing={{1}: (9, {})} | custom-call | flops 18119393280 | bytes 53084160 | tf_op jit(solution)/shard_map/up_teacher/pallas_call | solution.py:80
  172.9 10.3 %up_student.1 = (bf16[768,3072]{1,0:T(8,128)(2,1)}, bf16[768,3072]{1,0:T(8,128)(2,1)}) custom-call(bf16[768,768]{1,0:T(8,128)(2,1)} %get-tuple-element.129.refs_0_, bf16[96,6144]{1,0:T(8,128)(2,1)} %w_up_rows.1.refs_9_.refs_1_, bf16[96,6144]{1,0:T(8,128)(2,1)} %get-tuple-element.124.refs_2_, bf16[96,6144]{1,0:T(8,128)(2,1)} %copy-done.47, ...), custom_call_target="tpu_custom_call" | custom-call | flops 18119393280 | bytes 76677120 | tf_op jit(solution)/shard_map/up_student/pallas_call | solution.py:80
  185.3 2.7 collective-permute-done.33.refs_3_
  189.6 14.6 %collective-permute-done.34.refs_4_ = bf16[96,6144]{1,0:T(8,128)(2,1)S(1)} collective-permute-done((bf16[96,6144]{1,0:T(8,128)(2,1)S(1)}, bf16[96,6144]{1,0:T(8,128)(2,1)S(1)}, u32[]{:S(2)}, u32[]{:S(2)}) %collective-permute-start.34) | collective-permute-done | bytes 1179680 | tf_op jit(solution)/shard_map/ppermute | solution.py:111
  204.2 2.8 collective-permute-done.36.refs_8_
  208.0 10.8 %down_teacher.1 = (f32[768,768]{1,0:T(8,128)}, bf16[768,768]{1,0:T(8,128)(2,1)}) custom-call(bf16[768,3072]{1,0:T(8,128)(2,1)} %get-tuple-element.134.refs_10_.refs_0_, bf16[96,6144]{1,0:T(8,128)(2,1)} %w_down_rows.1.refs_10_.refs_1_, bf16[96,6144]{1,0:T(8,128)(2,1)} %get-tuple-element.136.refs_2_, bf16[96,6144]{1,0:T(8,128)(2,1)} %copy-done.49, ...), custom_call_target="tpu_custom_call" | custom-call | flops 18119393280 | bytes 47185920 | tf_op jit(solution)/shard_map/down_teacher/pallas_call | solution.py:80
  218.8 3.5 all-to-all-start
  222.4 13.3 %down_student.1 = (f32[768,768]{1,0:T(8,128)}, bf16[768,768]{1,0:T(8,128)(2,1)}, f32[8,768]{1,0:T(8,128)}, bf16[768,768]{1,0:T(8,128)(2,1)}) custom-call(bf16[768,3072]{1,0:T(8,128)(2,1)} %get-tuple-element.135.refs_1_.refs_0_, bf16[96,6144]{1,0:T(8,128)(2,1)} %w_down_rows.1.refs_10_.refs_1_, bf16[96,6144]{1,0:T(8,128)(2,1)} %get-tuple-element.136.refs_2_, ...), custom_call_target="tpu_custom_call" | custom-call | flops 18119393280 | bytes 47185920 | tf_op jit(solution)/shard_map/down_student/pallas_call | solution.py:80
  235.7 5.1 %g_down_far.1.refs_11_ = bf16[384,3072]{1,0:T(8,128)(2,1)} custom-call(bf16[768,768]{1,0:T(8,128)(2,1)} %get-tuple-element.142.refs_0_, bf16[768,3072]{1,0:T(8,128)(2,1)} %get-tuple-element.135.refs_1_.refs_0_, f32[768,768]{1,0:T(8,128)} %get-tuple-element.144.refs_2_.refs_11_), custom_call_target="tpu_custom_call" | custom-call | flops 9059696640 | bytes 47185920 | tf_op jit(solution)/shard_map/g_down_far/pallas_call | solution.py:80
  240.9 9.3 %back_down.1.refs_1_.refs_3_.refs_0_ = bf16[768,3072]{1,0:T(8,128)(2,1)} custom-call(bf16[768,768]{1,0:T(8,128)(2,1)} %get-tuple-element.142.refs_0_, bf16[96,6144]{1,0:T(8,128)(2,1)} %w_down_rows.1.refs_10_.refs_1_, bf16[96,6144]{1,0:T(8,128)(2,1)} %get-tuple-element.136.refs_2_, bf16[96,6144]{1,0:T(8,128)(2,1)} %copy-done.49, bf16[96,6144]{1,0:T(8,128)(2,1)} %copy-done.51, ...), custom_call_target="tpu_custom_call" | custom-call | flops 18119393280 | bytes 53084160 | tf_op jit(solution)/shard_map/back_down/pallas_call | solution.py:80
  252.5 5.1 %g_up_far.1 = (bf16[384,3072]{1,0:T(8,128)(2,1)}, bf16[768,768]{1,0:T(8,128)(2,1)}) custom-call(bf16[768,768]{1,0:T(8,128)(2,1)} %get-tuple-element.129.refs_0_, bf16[768,3072]{1,0:T(8,128)(2,1)} %back_down.1.refs_1_.refs_3_.refs_0_, bf16[768,768]{1,0:T(8,128)(2,1)} %bitcast.88, ...), custom_call_target="tpu_custom_call", output_to_operand_aliasing={{1}: (2, {})} | custom-call | flops 9059696640 | bytes 47185920 | tf_op jit(solution)/shard_map/g_up_far/pallas_call | solution.py:80
  257.6 4.5 %all-to-all-start.1 = ((bf16[4,192,768]{2,1,0:T(8,128)(2,1)}), bf16[4,192,768]{2,1,0:T(8,128)(2,1)S(1)}, u32[]{:S(2)}, u32[]{:S(2)}) async-start(bf16[4,192,768]{2,1,0:T(8,128)(2,1)} %bitcast.26), calls=%async_computation.1 | async-start | bytes 2359296 | tf_op jit(solution)/shard_map/all_to_all | solution.py:368
  263.5 5.5 %g_down_near.1 = (bf16[192,3072]{1,0:T(8,128)(2,1)}, bf16[192,3072]{1,0:T(8,128)(2,1)}) custom-call(bf16[768,768]{1,0:T(8,128)(2,1)} %get-tuple-element.142.refs_0_, bf16[768,3072]{1,0:T(8,128)(2,1)} %get-tuple-element.135.refs_1_.refs_0_, bf16[384,3072]{1,0:T(8,128)(2,1)} %copy-done.45, bf16[384,3072]{1,0:T(8,128)(2,1)} %get-tuple-element.147.refs_3_), custom_call_target="tpu_custom_call" | custom-call | flops 9059696640 | bytes 47185920 | tf_op jit(solution)/shard_map/g_down_near/pallas_call | solution.py:80
  270.2 5.4 %g_up_near.1 = (bf16[192,3072]{1,0:T(8,128)(2,1)}, bf16[192,3072]{1,0:T(8,128)(2,1)}) custom-call(bf16[768,768]{1,0:T(8,128)(2,1)} %get-tuple-element.129.refs_0_, bf16[768,3072]{1,0:T(8,128)(2,1)} %back_down.1.refs_1_.refs_3_.refs_0_, bf16[384,3072]{1,0:T(8,128)(2,1)} %collective-permute-done.37.refs_2_, bf16[192,3072]{1,0:T(8,128)(2,1)} %get-tuple-element.148.refs_3_.refs_0_), custom_call_target="tpu_custom_call" | custom-call | flops 9059696640 | bytes 47185920 | tf_op jit(solution)/shard_map/g_up_near/pallas_call | solution.py:80
  276.5 12.7 %back_up.1 = (f32[768,768]{1,0:T(8,128)}, bf16[768,768]{1,0:T(8,128)(2,1)}, bf16[768,768]{1,0:T(8,128)(2,1)}, f32[8,768]{1,0:T(8,128)}) custom-call(bf16[768,3072]{1,0:T(8,128)(2,1)} %back_down.1.refs_1_.refs_3_.refs_0_, bf16[96,6144]{1,0:T(8,128)(2,1)} %w_up_rows.1.refs_9_.refs_1_, bf16[96,6144]{1,0:T(8,128)(2,1)} %get-tuple-element.124.refs_2_, ...), custom_call_target="tpu_custom_call" | custom-call | flops 18119393280 | bytes 47185920 | tf_op jit(solution)/shard_map/back_up/pallas_call | solution.py:80
  289.1 1.8 all-to-all-done.1
  292.0 11.5 %attend_backward.1 = (bf16[768,2304]{1,0:T(8,128)(2,1)}, bf16[768,768]{1,0:T(8,128)(2,1)}) custom-call(f32[4]{0:T(128)} %multiply_bitcast_fusion.refs_9_.refs_0_, bf16[768,2304]{1,0:T(8,128)(2,1)} %project_student.1.refs_2_.refs_3_.refs_4_.refs_8_.refs_1_, bf16[768,768]{1,0:T(8,128)(2,1)} %get-tuple-element.150.refs_2_, ...), custom_call_target="tpu_custom_call", output_to_operand_aliasing={{1}: (5, {})} | custom-call | flops 12079595520 | bytes 70778880 | tf_op jit(solution)/shard_map/attend_backward/pallas_call | solution.py:80
  304.5 2.8 g_down_add2.1
  307.3 4.5 %g_qkv_far.1.refs_2_ = bf16[384,2304]{1,0:T(8,128)(2,1)} custom-call(bf16[768,768]{1,0:T(8,128)(2,1)} %get-tuple-element.110.refs_0_, bf16[768,2304]{1,0:T(8,128)(2,1)} %get-tuple-element.157.refs_2_.refs_1_.refs_0_, bf16[96,3072]{1,0:T(8,128)(2,1)} %get-tuple-element.159.refs_2_.refs_1_), custom_call_target="tpu_custom_call" | custom-call | flops 6794772480 | bytes 35389440 | tf_op jit(solution)/shard_map/g_qkv_far/pallas_call | solution.py:80
  314.9 2.8 g_up_add2.1
  318.2 8.8 %back_entry.1.refs_3_ = bf16[768,768]{1,0:T(8,128)(2,1)} custom-call(bf16[768,2304]{1,0:T(8,128)(2,1)} %get-tuple-element.157.refs_2_.refs_1_.refs_0_, bf16[96,3072]{1,0:T(8,128)(2,1)} %get-tuple-element.106.refs_2_.refs_1_.refs_14_, bf16[96,3072]{1,0:T(8,128)(2,1)} %get-tuple-element.111.refs_2_.refs_15_, ...), custom_call_target="tpu_custom_call" | custom-call | flops 13589544960 | bytes 35389440 | tf_op jit(solution)/shard_map/back_entry/pallas_call | solution.py:80
  327.0 3.5 all-to-all-start.2
  330.6 5.0 %g_qkv_near.1 = (bf16[192,2304]{1,0:T(8,128)(2,1)}, bf16[192,2304]{1,0:T(8,128)(2,1)}) custom-call(bf16[768,768]{1,0:T(8,128)(2,1)} %get-tuple-element.110.refs_0_, bf16[768,2304]{1,0:T(8,128)(2,1)} %get-tuple-element.157.refs_2_.refs_1_.refs_0_, bf16[384,2304]{1,0:T(8,128)(2,1)} %collective-permute-done.43.refs_2_, bf16[768,768]{1,0:T(8,128)(2,1)} %back_entry.1.refs_3_), custom_call_target="tpu_custom_call" | custom-call | flops 6794772480 | bytes 35389440 | tf_op jit(solution)/shard_map/g_qkv_near/pallas_call | solution.py:80
  337.6 2.2 g_down_add3.1.refs_3_
  340.6 2.2 g_up_add3.1.refs_4_
  342.9 3.3 g_out_far.1.refs_1_
  346.2 2.0 collective-permute-start.44
  348.2 3.4 arrive_teacher.1.refs_6_
  351.6 3.4 g_out_near.1
  355.0 2.4 g_qkv_add2.1
  358.2 7.1 %collective-permute-done.44.refs_1_ = bf16[2,96,768]{2,1,0:T(8,128)(2,1)S(1)} collective-permute-done((bf16[2,96,768]{2,1,0:T(8,128)(2,1)S(1)}, bf16[2,96,768]{2,1,0:T(8,128)(2,1)S(1)}, u32[]{:S(2)}, u32[]{:S(2)}) %collective-permute-start.44) | collective-permute-done | bytes 294944 | tf_op jit(solution)/shard_map/ppermute | solution.py:107
  366.1 3.5 arrive_student.1
  370.6 7.1 %collective-permute-start.54 = (bf16[1,96,768]{2,1,0:T(8,128)(2,1)S(1)}, bf16[1,96,768]{2,1,0:T(8,128)(2,1)S(1)}, u32[]{:S(2)}, u32[]{:S(2)}) collective-permute-start(bf16[1,96,768]{2,1,0:T(8,128)(2,1)S(1)} %slice.146), channel_id=1, source_target_pairs={{0,2},{1,3},{2,0},{3,1},{4,6},{5,7},{6,4},{7,5},{8,10},{9,11},{10,... | collective-permute-start | bytes 442376 | tf_op jit(solution)/shard_map/ppermute | solution.py:107
  378.1 6.0 %collective-permute-done.54 = bf16[1,96,768]{2,1,0:T(8,128)(2,1)S(1)} collective-permute-done((bf16[1,96,768]{2,1,0:T(8,128)(2,1)S(1)}, bf16[1,96,768]{2,1,0:T(8,128)(2,1)S(1)}, u32[]{:S(2)}, u32[]{:S(2)}) %collective-permute-start.54) | collective-permute-done | bytes 147488 | tf_op jit(solution)/shard_map/ppermute | solution.py:107
  386.5 1.9 g_out_add2.1
  390.2 3.6 arrive_grad.1
  393.8 2.0 g_qkv_add3.1
  398.3 2.7 collective-permute-start.49
  406.4 3.1 collective-permute-done.52
  409.8 2.9 collective-permute-start.50
  412.7 5.1 %collective-permute-done.53 = bf16[1,96,256]{1,2,0:T(8,128)(2,1)S(1)} collective-permute-done((bf16[1,96,256]{1,2,0:T(8,128)(2,1)S(1)}, bf16[1,96,256]{1,2,0:T(8,128)(2,1)S(1)}, u32[]{:S(2)}, u32[]{:S(2)}) %collective-permute-start.53) | collective-permute-done | bytes 49184 | tf_op jit(solution)/shard_map/ppermute | solution.py:107
  (277 shorter events, 91.6 us)
Async XLA Ops:
  7.2 91.0 %all-gather.3.cloned.1.call-start = ((), (), s32[]{:S(2)}) async-start(), calls=%async_computation.4 | async-start | bytes 1474560 | tf_op jit(solution)/shard_map/all_gather | solution.py:195
  9.6 18.2 %collective-permute-start.1 = (bf16[96,768]{1,0:T(8,128)(2,1)S(1)}, bf16[96,768]{1,0:T(8,128)(2,1)S(1)}, u32[]{:S(2)}, u32[]{:S(2)}) collective-permute-start(bf16[96,768]{1,0:T(8,128)(2,1)S(1)} %pad_maximum_fusion.1.refs_4_.refs_0_), channel_id=1, source_target_pairs={{0,2},{1,3},{2,0},{3,1},{4,6},{5,7},{6,4},{7,5},{8,10},{9,11},{10,... | collective-permute-start | bytes 442376 | tf_op jit(solution)/shard_map/ppermute | solution.py:107
  17.5 3.7 collective-permute-start
  24.0 3.7 collective-permute-start.2
  25.7 13.2 %collective-permute-start.3 = (bf16[96,768]{1,0:T(8,128)(2,1)S(1)}, bf16[96,768]{1,0:T(8,128)(2,1)S(1)}, u32[]{:S(2)}, u32[]{:S(2)}) collective-permute-start(bf16[96,768]{1,0:T(8,128)(2,1)S(1)} %pad_maximum_fusion.2.refs_0_), channel_id=1, source_target_pairs={{0,2},{1,3},{2,0},{3,1},{4,6},{5,7},{6,4},{7,5},{8,10},{9,11},{10,... | collective-permute-start | bytes 442376 | tf_op jit(solution)/shard_map/ppermute | solution.py:107
  30.2 11.1 %collective-permute-start.5 = (bf16[96,1536]{1,0:T(8,128)(2,1)}, bf16[96,1536]{1,0:T(8,128)(2,1)S(1)}, u32[]{:S(2)}, u32[]{:S(2)}) collective-permute-start(bf16[96,1536]{1,0:T(8,128)(2,1)} %get-tuple-element.100.refs_3_.refs_0_), channel_id=1, source_target_pairs={{0,1},{1,0},{2,3},{3,2},{4,5},{5,4},{6,7},{7,6},{8,9},{9,8},{10,11... | collective-permute-start | bytes 884744 | tf_op jit(solution)/shard_map/ppermute | solution.py:107
  32.5 6.5 %collective-permute-start.4 = (f32[4,16,128]{2,1,0:T(8,128)S(1)}, f32[4,16,128]{2,1,0:T(8,128)S(1)}, u32[]{:S(2)}, u32[]{:S(2)}) collective-permute-start(f32[4,16,128]{2,1,0:T(8,128)S(1)} %pad_maximum_fusion.3), channel_id=1, source_target_pairs={{0,4},{4,0},{8,12},{12,8},{16,20},{20,16},{24,28},{28,24},{1,5},{5... | collective-permute-start | bytes 98312 | tf_op jit(solution)/shard_map/ppermute | solution.py:107
  44.0 15.3 %collective-permute-start.10 = (bf16[96,3072]{1,0:T(8,128)(2,1)}, bf16[96,3072]{1,0:T(8,128)(2,1)S(1)}, u32[]{:S(2)}, u32[]{:S(2)}) collective-permute-start(bf16[96,3072]{1,0:T(8,128)(2,1)} %w_tqkv_rows.1.refs_3_.refs_1_), channel_id=1, source_target_pairs={{0,8},{4,20},{8,0},{12,28},{16,24},{20,4},{24,16},{28,12},{1,9},{5... | collective-permute-start | bytes 1769480 | tf_op jit(solution)/shard_map/ppermute | solution.py:111
  45.5 16.7 %collective-permute-start.6 = (bf16[96,3072]{1,0:T(8,128)(2,1)}, bf16[96,3072]{1,0:T(8,128)(2,1)}, u32[]{:S(2)}, u32[]{:S(2)}) collective-permute-start(bf16[96,3072]{1,0:T(8,128)(2,1)} %w_tqkv_rows.1.refs_3_.refs_1_), channel_id=1, source_target_pairs={{0,4},{4,0},{8,12},{12,8},{16,20},{20,16},{24,28},{28,24},{1,5},{5... | collective-permute-start | bytes 1769480 | tf_op jit(solution)/shard_map/ppermute | solution.py:107
  45.8 9.2 %collective-permute-start.9 = (bf16[96,1536]{1,0:T(8,128)(2,1)S(1)}, bf16[96,1536]{1,0:T(8,128)(2,1)S(1)}, u32[]{:S(2)}, u32[]{:S(2)}) collective-permute-start(bf16[96,1536]{1,0:T(8,128)(2,1)S(1)} %copy-done.16), channel_id=1, source_target_pairs={{0,1},{1,0},{2,3},{3,2},{4,5},{5,4},{6,7},{7,6},{8,9},{9,8},{10,11... | collective-permute-start | bytes 884744 | tf_op jit(solution)/shard_map/ppermute | solution.py:107
  62.2 2.7 collective-permute-start.12
  62.2 10.1 %collective-permute-start.7 = (bf16[96,3072]{1,0:T(8,128)(2,1)}, bf16[96,3072]{1,0:T(8,128)(2,1)S(1)}, u32[]{:S(2)}, u32[]{:S(2)}) collective-permute-start(bf16[96,3072]{1,0:T(8,128)(2,1)} %collective-permute-done.6.refs_5_), channel_id=1, source_target_pairs={{0,8},{4,20},{8,0},{12,28},{16,24},{20,4},{24,16},{28,12},{1,9},{5... | collective-permute-start | bytes 1769480 | tf_op jit(solution)/shard_map/ppermute | solution.py:111
  63.5 63.4 %all-gather.5.cloned.1.call-start = ((), (), s32[]{:S(2)}) async-start(), calls=%async_computation.5 | async-start | bytes 1474560 | tf_op jit(solution)/shard_map/all_gather | solution.py:195
  63.5 24.1 %copy-start.28 = (bf16[96,3072]{1,0:T(8,128)(2,1)S(1)}, bf16[96,3072]{1,0:T(8,128)(2,1)}, u32[]{:S(2)}) copy-start(bf16[96,3072]{1,0:T(8,128)(2,1)} %get-tuple-element.114.refs_2_) | copy-start | bytes 1769476
  63.5 34.2 %copy-start.57 = (f32[1,4]{1,0:T(1,128)S(1)}, f32[1,4]{1,0:T(1,128)}, u32[]{:S(2)}) copy-start(f32[1,4]{1,0:T(1,128)} %constant.39) | copy-start | bytes 52
  63.6 3.7 collective-permute-start.8
  64.1 14.5 %collective-permute-start.11 = (bf16[96,3072]{1,0:T(8,128)(2,1)}, bf16[96,3072]{1,0:T(8,128)(2,1)S(1)}, u32[]{:S(2)}, u32[]{:S(2)}) collective-permute-start(bf16[96,3072]{1,0:T(8,128)(2,1)} %get-tuple-element.106.refs_2_.refs_1_.refs_14_), channel_id=1, source_target_pairs={{0,8},{4,20},{8,0},{12,28},{16,24},{20,4},{24,16},{28,12},{1,9},{5... | collective-permute-start | bytes 1769480 | tf_op jit(solution)/shard_map/ppermute | solution.py:111
  64.9 20.1 %collective-permute-start.13 = (bf16[96,3072]{1,0:T(8,128)(2,1)}, bf16[96,3072]{1,0:T(8,128)(2,1)S(1)}, u32[]{:S(2)}, u32[]{:S(2)}) collective-permute-start(bf16[96,3072]{1,0:T(8,128)(2,1)} %collective-permute-done.12.refs_5_.refs_18_), channel_id=1, source_target_pairs={{0,8},{4,20},{8,0},{12,28},{16,24},{20,4},{24,16},{28,12},{1,9},{5... | collective-permute-start | bytes 1769480 | tf_op jit(solution)/shard_map/ppermute | solution.py:111
  73.7 12.7 %collective-permute-start.19 = (bf16[96,3072]{1,0:T(8,128)(2,1)}, bf16[96,3072]{1,0:T(8,128)(2,1)S(1)}, u32[]{:S(2)}, u32[]{:S(2)}) collective-permute-start(bf16[96,3072]{1,0:T(8,128)(2,1)} %get-tuple-element.115.refs_7_), channel_id=1, source_target_pairs={{0,4},{4,0},{8,12},{12,8},{16,20},{20,16},{24,28},{28,24},{1,5},{5... | collective-permute-start | bytes 1769480 | tf_op jit(solution)/shard_map/ppermute | solution.py:107
  74.4 4.7 %collective-permute-start.14 = (f32[8,128]{1,0:T(8,128)S(1)}, f32[8,128]{1,0:T(8,128)S(1)}, u32[]{:S(2)}, u32[]{:S(2)}) collective-permute-start(f32[8,128]{1,0:T(8,128)S(1)} %fusion.21), channel_id=1, source_target_pairs={{0,2},{1,3},{2,0},{3,1},{4,6},{5,7},{6,4},{7,5},{8,10},{9,11},{10,... | collective-permute-start | bytes 12296 | tf_op jit(solution)/shard_map/ppermute | solution.py:107
  86.4 2.3 collective-permute-start.15
  86.4 10.1 %collective-permute-start.20 = (bf16[96,3072]{1,0:T(8,128)(2,1)S(1)}, bf16[96,3072]{1,0:T(8,128)(2,1)}, u32[]{:S(2)}, u32[]{:S(2)}) collective-permute-start(bf16[96,3072]{1,0:T(8,128)(2,1)S(1)} %collective-permute-done.19.refs_3_), channel_id=1, source_target_pairs={{0,8},{4,20},{8,0},{12,28},{16,24},{20,4},{24,16},{28,12},{1,9},{5... | collective-permute-start | bytes 1769480 | tf_op jit(solution)/shard_map/ppermute | solution.py:111
  87.7 12.9 %collective-permute-start.21 = (bf16[96,3072]{1,0:T(8,128)(2,1)S(1)}, bf16[96,3072]{1,0:T(8,128)(2,1)}, u32[]{:S(2)}, u32[]{:S(2)}) collective-permute-start(bf16[96,3072]{1,0:T(8,128)(2,1)S(1)} %copy-done.28), channel_id=1, source_target_pairs={{0,4},{4,0},{8,12},{12,8},{16,20},{20,16},{24,28},{28,24},{1,5},{5... | collective-permute-start | bytes 1769480 | tf_op jit(solution)/shard_map/ppermute | solution.py:107
  88.7 14.0 %collective-permute-start.16 = (bf16[96,3072]{1,0:T(8,128)(2,1)}, bf16[96,3072]{1,0:T(8,128)(2,1)}, u32[]{:S(2)}, u32[]{:S(2)}) collective-permute-start(bf16[96,3072]{1,0:T(8,128)(2,1)} %collective-permute-done.15.refs_3_.refs_16_), channel_id=1, source_target_pairs={{0,8},{4,20},{8,0},{12,28},{16,24},{20,4},{24,16},{28,12},{1,9},{5... | collective-permute-start | bytes 1769480 | tf_op jit(solution)/shard_map/ppermute | solution.py:111
  96.4 6.3 %collective-permute-start.22 = (bf16[96,3072]{1,0:T(8,128)(2,1)}, bf16[96,3072]{1,0:T(8,128)(2,1)}, u32[]{:S(2)}, u32[]{:S(2)}) collective-permute-start(bf16[96,3072]{1,0:T(8,128)(2,1)} %collective-permute-done.20.refs_4_), channel_id=1, source_target_pairs={{0,4},{4,0},{8,12},{12,8},{16,20},{20,16},{24,28},{28,24},{1,5},{5... | collective-permute-start | bytes 1769480 | tf_op jit(solution)/shard_map/ppermute | solution.py:107
  96.4 14.8 %collective-permute-start.17 = (bf16[96,3072]{1,0:T(8,128)(2,1)}, bf16[96,3072]{1,0:T(8,128)(2,1)}, u32[]{:S(2)}, u32[]{:S(2)}) collective-permute-start(bf16[96,3072]{1,0:T(8,128)(2,1)} %get-tuple-element.111.refs_2_.refs_15_), channel_id=1, source_target_pairs={{0,4},{4,0},{8,12},{12,8},{16,20},{20,16},{24,28},{28,24},{1,5},{5... | collective-permute-start | bytes 1769480 | tf_op jit(solution)/shard_map/ppermute | solution.py:107
  100.6 9.4 %collective-permute-start.24 = (bf16[96,6144]{1,0:T(8,128)(2,1)}, bf16[96,6144]{1,0:T(8,128)(2,1)S(1)}, u32[]{:S(2)}, u32[]{:S(2)}) collective-permute-start(bf16[96,6144]{1,0:T(8,128)(2,1)} %w_up_rows.1.refs_9_.refs_1_), channel_id=1, source_target_pairs={{0,4},{4,0},{8,12},{12,8},{16,20},{20,16},{24,28},{28,24},{1,5},{5... | collective-permute-start | bytes 3538952 | tf_op jit(solution)/shard_map/ppermute | solution.py:107
  100.6 26.2 %collective-permute-start.23 = (bf16[96,6144]{1,0:T(8,128)(2,1)}, bf16[96,6144]{1,0:T(8,128)(2,1)S(1)}, u32[]{:S(2)}, u32[]{:S(2)}) collective-permute-start(bf16[96,6144]{1,0:T(8,128)(2,1)} %w_up_rows.1.refs_9_.refs_1_), channel_id=1, source_target_pairs={{0,8},{4,20},{8,0},{12,28},{16,24},{20,4},{24,16},{28,12},{1,9},{5... | collective-permute-start | bytes 3538952 | tf_op jit(solution)/shard_map/ppermute | solution.py:111
  102.7 8.5 %collective-permute-start.18 = (bf16[96,3072]{1,0:T(8,128)(2,1)}, bf16[96,3072]{1,0:T(8,128)(2,1)}, u32[]{:S(2)}, u32[]{:S(2)}) collective-permute-start(bf16[96,3072]{1,0:T(8,128)(2,1)} %collective-permute-done.16.refs_4_.refs_17_), channel_id=1, source_target_pairs={{0,4},{4,0},{8,12},{12,8},{16,20},{20,16},{24,28},{28,24},{1,5},{5... | collective-permute-start | bytes 1769480 | tf_op jit(solution)/shard_map/ppermute | solution.py:107
  110.0 19.7 %collective-permute-start.25 = (bf16[96,6144]{1,0:T(8,128)(2,1)S(1)}, bf16[96,6144]{1,0:T(8,128)(2,1)S(1)}, u32[]{:S(2)}, u32[]{:S(2)}) collective-permute-start(bf16[96,6144]{1,0:T(8,128)(2,1)S(1)} %collective-permute-done.24.refs_5_), channel_id=1, source_target_pairs={{0,8},{4,20},{8,0},{12,28},{16,24},{20,4},{24,16},{28,12},{1,9},{5... | collective-permute-start | bytes 3538952 | tf_op jit(solution)/shard_map/ppermute | solution.py:111
  131.4 3.1 collective-permute-start.27
  133.5 19.4 %collective-permute-start.26 = (bf16[96,6144]{1,0:T(8,128)(2,1)}, bf16[96,6144]{1,0:T(8,128)(2,1)S(1)}, u32[]{:S(2)}, u32[]{:S(2)}) collective-permute-start(bf16[96,6144]{1,0:T(8,128)(2,1)} %get-tuple-element.124.refs_2_), channel_id=1, source_target_pairs={{0,4},{4,0},{8,12},{12,8},{16,20},{20,16},{24,28},{28,24},{1,5},{5... | collective-permute-start | bytes 3538952 | tf_op jit(solution)/shard_map/ppermute | solution.py:107
  134.4 18.5 %collective-permute-start.28 = (bf16[96,6144]{1,0:T(8,128)(2,1)S(1)}, bf16[96,6144]{1,0:T(8,128)(2,1)S(1)}, u32[]{:S(2)}, u32[]{:S(2)}) collective-permute-start(bf16[96,6144]{1,0:T(8,128)(2,1)S(1)} %collective-permute-done.27.refs_3_), channel_id=1, source_target_pairs={{0,8},{4,20},{8,0},{12,28},{16,24},{20,4},{24,16},{28,12},{1,9},{5... | collective-permute-start | bytes 3538952 | tf_op jit(solution)/shard_map/ppermute | solution.py:111
  146.5 16.8 %collective-permute-start.30 = (bf16[96,6144]{1,0:T(8,128)(2,1)}, bf16[96,6144]{1,0:T(8,128)(2,1)}, u32[]{:S(2)}, u32[]{:S(2)}) collective-permute-start(bf16[96,6144]{1,0:T(8,128)(2,1)} %w_down_rows.1.refs_10_.refs_1_), channel_id=1, source_target_pairs={{0,8},{4,20},{8,0},{12,28},{16,24},{20,4},{24,16},{28,12},{1,9},{5... | collective-permute-start | bytes 3538952 | tf_op jit(solution)/shard_map/ppermute | solution.py:111
  147.3 13.5 %collective-permute-start.31 = (bf16[96,6144]{1,0:T(8,128)(2,1)}, bf16[96,6144]{1,0:T(8,128)(2,1)}, u32[]{:S(2)}, u32[]{:S(2)}) collective-permute-start(bf16[96,6144]{1,0:T(8,128)(2,1)} %w_down_rows.1.refs_10_.refs_1_), channel_id=1, source_target_pairs={{0,4},{4,0},{8,12},{12,8},{16,20},{20,16},{24,28},{28,24},{1,5},{5... | collective-permute-start | bytes 3538952 | tf_op jit(solution)/shard_map/ppermute | solution.py:107
  160.3 3.3 collective-permute-start.29
  160.9 22.4 %collective-permute-start.32 = (bf16[96,6144]{1,0:T(8,128)(2,1)}, bf16[96,6144]{1,0:T(8,128)(2,1)S(1)}, u32[]{:S(2)}, u32[]{:S(2)}) collective-permute-start(bf16[96,6144]{1,0:T(8,128)(2,1)} %collective-permute-done.31.refs_5_), channel_id=1, source_target_pairs={{0,8},{4,20},{8,0},{12,28},{16,24},{20,4},{24,16},{28,12},{1,9},{5... | collective-permute-start | bytes 3538952 | tf_op jit(solution)/shard_map/ppermute | solution.py:111
  184.9 3.1 collective-permute-start.33
  187.9 20.1 %copy-start.49 = (bf16[96,6144]{1,0:T(8,128)(2,1)}, bf16[96,6144]{1,0:T(8,128)(2,1)S(1)}, u32[]{:S(2)}) copy-start(bf16[96,6144]{1,0:T(8,128)(2,1)S(1)} %collective-permute-done.33.refs_3_) | copy-start | bytes 3538948
  187.9 16.2 %collective-permute-start.34 = (bf16[96,6144]{1,0:T(8,128)(2,1)S(1)}, bf16[96,6144]{1,0:T(8,128)(2,1)S(1)}, u32[]{:S(2)}, u32[]{:S(2)}) collective-permute-start(bf16[96,6144]{1,0:T(8,128)(2,1)S(1)} %collective-permute-done.33.refs_3_), channel_id=1, source_target_pairs={{0,8},{4,20},{8,0},{12,28},{16,24},{20,4},{24,16},{28,12},{1,9},{5... | collective-permute-start | bytes 3538952 | tf_op jit(solution)/shard_map/ppermute | solution.py:111
  189.2 15.0 %collective-permute-start.35 = (bf16[96,6144]{1,0:T(8,128)(2,1)}, bf16[96,6144]{1,0:T(8,128)(2,1)S(1)}, u32[]{:S(2)}, u32[]{:S(2)}) collective-permute-start(bf16[96,6144]{1,0:T(8,128)(2,1)} %get-tuple-element.136.refs_2_), channel_id=1, source_target_pairs={{0,4},{4,0},{8,12},{12,8},{16,20},{20,16},{24,28},{28,24},{1,5},{5... | collective-permute-start | bytes 3538952 | tf_op jit(solution)/shard_map/ppermute | solution.py:107
  204.2 2.8 collective-permute-start.36
  218.8 32.6 %all-to-all-start = ((bf16[4,192,768]{2,1,0:T(8,128)(2,1)}), bf16[4,192,768]{2,1,0:T(8,128)(2,1)S(1)}, u32[]{:S(2)}, u32[]{:S(2)}) async-start(bf16[4,192,768]{2,1,0:T(8,128)(2,1)} %bitcast.97), calls=%async_computation | async-start | bytes 2359296 | tf_op jit(solution)/shard_map/all_to_all | solution.py:368
  240.8 21.3 %collective-permute-start.38 = (bf16[384,3072]{1,0:T(8,128)(2,1)}, bf16[384,3072]{1,0:T(8,128)(2,1)S(1)}, u32[]{:S(2)}, u32[]{:S(2)}) collective-permute-start(bf16[384,3072]{1,0:T(8,128)(2,1)} %g_down_far.1.refs_11_), channel_id=1, source_target_pairs={{0,4},{4,0},{8,12},{12,8},{16,20},{20,16},{24,28},{28,24},{1,5},{5... | collective-permute-start | bytes 7077896 | tf_op jit(solution)/shard_map/ppermute | solution.py:107
  257.6 12.6 %collective-permute-start.37 = (bf16[384,3072]{1,0:T(8,128)(2,1)}, bf16[384,3072]{1,0:T(8,128)(2,1)}, u32[]{:S(2)}, u32[]{:S(2)}) collective-permute-start(bf16[384,3072]{1,0:T(8,128)(2,1)} %get-tuple-element.147.refs_3_), channel_id=1, source_target_pairs={{0,4},{4,0},{8,12},{12,8},{16,20},{20,16},{24,28},{28,24},{1,5},{5... | collective-permute-start | bytes 7077896 | tf_op jit(solution)/shard_map/ppermute | solution.py:107
  257.6 33.4 %all-to-all-start.1 = ((bf16[4,192,768]{2,1,0:T(8,128)(2,1)}), bf16[4,192,768]{2,1,0:T(8,128)(2,1)S(1)}, u32[]{:S(2)}, u32[]{:S(2)}) async-start(bf16[4,192,768]{2,1,0:T(8,128)(2,1)} %bitcast.26), calls=%async_computation.1 | async-start | bytes 2359296 | tf_op jit(solution)/shard_map/all_to_all | solution.py:368
  269.0 34.5 %collective-permute-start.40 = (bf16[192,3072]{1,0:T(8,128)(2,1)}, bf16[192,3072]{1,0:T(8,128)(2,1)S(1)}, u32[]{:S(2)}, u32[]{:S(2)}) collective-permute-start(bf16[192,3072]{1,0:T(8,128)(2,1)} %get-tuple-element.158), channel_id=1, source_target_pairs={{0,8},{4,20},{8,0},{12,28},{16,24},{20,4},{24,16},{28,12},{1,9},{5... | collective-permute-start | bytes 3538952 | tf_op jit(solution)/shard_map/ppermute | solution.py:111
  275.7 38.2 %collective-permute-start.39 = (bf16[192,3072]{1,0:T(8,128)(2,1)}, bf16[192,3072]{1,0:T(8,128)(2,1)S(1)}, u32[]{:S(2)}, u32[]{:S(2)}) collective-permute-start(bf16[192,3072]{1,0:T(8,128)(2,1)} %get-tuple-element.156), channel_id=1, source_target_pairs={{0,8},{4,20},{8,0},{12,28},{16,24},{20,4},{24,16},{28,12},{1,9},{5... | collective-permute-start | bytes 3538952 | tf_op jit(solution)/shard_map/ppermute | solution.py:111
  311.8 18.8 %collective-permute-start.43 = (bf16[384,2304]{1,0:T(8,128)(2,1)}, bf16[384,2304]{1,0:T(8,128)(2,1)}, u32[]{:S(2)}, u32[]{:S(2)}) collective-permute-start(bf16[384,2304]{1,0:T(8,128)(2,1)} %g_qkv_far.1.refs_2_), channel_id=1, source_target_pairs={{0,4},{4,0},{8,12},{12,8},{16,20},{20,16},{24,28},{28,24},{1,5},{5... | collective-permute-start | bytes 5308424 | tf_op jit(solution)/shard_map/ppermute | solution.py:107
  312.3 24.5 %collective-permute-start.42 = (bf16[96,3072]{1,0:T(8,128)(2,1)S(1)}, bf16[96,3072]{1,0:T(8,128)(2,1)S(1)}, u32[]{:S(2)}, u32[]{:S(2)}) collective-permute-start(bf16[96,3072]{1,0:T(8,128)(2,1)S(1)} %copy-done.56), channel_id=1, source_target_pairs={{0,16},{4,12},{8,24},{12,4},{16,0},{20,28},{24,8},{28,20},{1,17},{... | collective-permute-start | bytes 1769480 | tf_op jit(solution)/shard_map/ppermute | solution.py:115
  317.7 22.1 %collective-permute-start.41 = (bf16[96,3072]{1,0:T(8,128)(2,1)}, bf16[96,3072]{1,0:T(8,128)(2,1)S(1)}, u32[]{:S(2)}, u32[]{:S(2)}) collective-permute-start(bf16[96,3072]{1,0:T(8,128)(2,1)} %get-tuple-element.161), channel_id=1, source_target_pairs={{0,16},{4,12},{8,24},{12,4},{16,0},{20,28},{24,8},{28,20},{1,17},{... | collective-permute-start | bytes 1769480 | tf_op jit(solution)/shard_map/ppermute | solution.py:115
  327.0 62.0 %all-to-all-start.2 = ((bf16[4,192,768]{2,1,0:T(8,128)(2,1)}), bf16[4,192,768]{2,1,0:T(8,128)(2,1)S(1)}, u32[]{:S(2)}, u32[]{:S(2)}) async-start(bf16[4,192,768]{2,1,0:T(8,128)(2,1)} %bitcast.96), calls=%async_computation.2 | async-start | bytes 2359296 | tf_op jit(solution)/shard_map/all_to_all | solution.py:368
  330.5 58.5 %reduce-scatter.2.cloned.1.call-start = ((), (), s32[]{:S(2)}) async-start(), calls=%async_computation.6 | async-start | bytes 737280 | tf_op jit(solution)/shard_map/reduce_scatter | solution.py:337
  335.6 16.0 %collective-permute-start.46 = (bf16[192,2304]{1,0:T(8,128)(2,1)}, bf16[192,2304]{1,0:T(8,128)(2,1)}, u32[]{:S(2)}, u32[]{:S(2)}) collective-permute-start(bf16[192,2304]{1,0:T(8,128)(2,1)} %get-tuple-element.167), channel_id=1, source_target_pairs={{0,8},{4,20},{8,0},{12,28},{16,24},{20,4},{24,16},{28,12},{1,9},{5... | collective-permute-start | bytes 2654216 | tf_op jit(solution)/shard_map/ppermute | solution.py:111
  346.1 5.5 %collective-permute-start.45 = (bf16[384,1024]{1,0:T(8,128)(2,1)}, bf16[384,1024]{1,0:T(8,128)(2,1)}, u32[]{:S(2)}, u32[]{:S(2)}) collective-permute-start(bf16[384,1024]{1,0:T(8,128)(2,1)} %g_out_far.1.refs_1_), channel_id=1, source_target_pairs={{0,4},{4,0},{8,12},{12,8},{16,20},{20,16},{24,28},{28,24},{1,5},{5... | collective-permute-start | bytes 2359304 | tf_op jit(solution)/shard_map/ppermute | solution.py:107
  346.2 19.2 %collective-permute-start.44 = (bf16[2,96,768]{2,1,0:T(8,128)(2,1)S(1)}, bf16[2,96,768]{2,1,0:T(8,128)(2,1)S(1)}, u32[]{:S(2)}, u32[]{:S(2)}) collective-permute-start(bf16[2,96,768]{2,1,0:T(8,128)(2,1)S(1)} %bitcast.105), channel_id=1, source_target_pairs={{0,1},{1,0},{2,3},{3,2},{4,5},{5,4},{6,7},{7,6},{8,9},{9,8},{10,11... | collective-permute-start | bytes 884744 | tf_op jit(solution)/shard_map/ppermute | solution.py:107
  357.4 31.6 %collective-permute-start.47 = (bf16[96,2304]{1,0:T(8,128)(2,1)}, bf16[96,2304]{1,0:T(8,128)(2,1)S(1)}, u32[]{:S(2)}, u32[]{:S(2)}) collective-permute-start(bf16[96,2304]{1,0:T(8,128)(2,1)} %get-tuple-element.173), channel_id=1, source_target_pairs={{0,16},{4,12},{8,24},{12,4},{16,0},{20,28},{24,8},{28,20},{1,17},{... | collective-permute-start | bytes 1327112 | tf_op jit(solution)/shard_map/ppermute | solution.py:115
  370.6 13.4 %collective-permute-start.54 = (bf16[1,96,768]{2,1,0:T(8,128)(2,1)S(1)}, bf16[1,96,768]{2,1,0:T(8,128)(2,1)S(1)}, u32[]{:S(2)}, u32[]{:S(2)}) collective-permute-start(bf16[1,96,768]{2,1,0:T(8,128)(2,1)S(1)} %slice.146), channel_id=1, source_target_pairs={{0,2},{1,3},{2,0},{3,1},{4,6},{5,7},{6,4},{7,5},{8,10},{9,11},{10,... | collective-permute-start | bytes 442376 | tf_op jit(solution)/shard_map/ppermute | solution.py:107
  377.8 8.0 %collective-permute-start.48 = (bf16[192,1024]{1,0:T(8,128)(2,1)}, bf16[192,1024]{1,0:T(8,128)(2,1)S(1)}, u32[]{:S(2)}, u32[]{:S(2)}) collective-permute-start(bf16[192,1024]{1,0:T(8,128)(2,1)} %get-tuple-element.174), channel_id=1, source_target_pairs={{0,8},{4,20},{8,0},{12,28},{16,24},{20,4},{24,16},{28,12},{1,9},{5... | collective-permute-start | bytes 1179656 | tf_op jit(solution)/shard_map/ppermute | solution.py:111
  388.4 12.6 %collective-permute-start.51 = (bf16[96,1024]{1,0:T(8,128)(2,1)}, bf16[96,1024]{1,0:T(8,128)(2,1)S(1)}, u32[]{:S(2)}, u32[]{:S(2)}) collective-permute-start(bf16[96,1024]{1,0:T(8,128)(2,1)} %get-tuple-element.180), channel_id=1, source_target_pairs={{0,16},{4,12},{8,24},{12,4},{16,0},{20,28},{24,8},{28,20},{1,17},{... | collective-permute-start | bytes 589832 | tf_op jit(solution)/shard_map/ppermute | solution.py:115
  398.3 11.4 %collective-permute-start.49 = (bf16[2,96,576]{1,2,0:T(8,128)(2,1)S(1)}, bf16[2,96,576]{1,2,0:T(8,128)(2,1)S(1)}, u32[]{:S(2)}, u32[]{:S(2)}) collective-permute-start(bf16[2,96,576]{1,2,0:T(8,128)(2,1)S(1)} %bitcast.104), channel_id=1, source_target_pairs={{0,1},{1,0},{2,3},{3,2},{4,5},{5,4},{6,7},{7,6},{8,9},{9,8},{10,11... | collective-permute-start | bytes 663560 | tf_op jit(solution)/shard_map/ppermute | solution.py:107
  404.5 5.0 %collective-permute-start.52 = (bf16[2,96,256]{1,2,0:T(8,128)(2,1)S(1)}, bf16[2,96,256]{1,2,0:T(8,128)(2,1)S(1)}, u32[]{:S(2)}, u32[]{:S(2)}) collective-permute-start(bf16[2,96,256]{1,2,0:T(8,128)(2,1)S(1)} %bitcast.109), channel_id=1, source_target_pairs={{0,1},{1,0},{2,3},{3,2},{4,5},{5,4},{6,7},{7,6},{8,9},{9,8},{10,11... | collective-permute-start | bytes 294920 | tf_op jit(solution)/shard_map/ppermute | solution.py:107
  409.6 8.3 %collective-permute-start.53 = (bf16[1,96,256]{1,2,0:T(8,128)(2,1)S(1)}, bf16[1,96,256]{1,2,0:T(8,128)(2,1)S(1)}, u32[]{:S(2)}, u32[]{:S(2)}) collective-permute-start(bf16[1,96,256]{1,2,0:T(8,128)(2,1)S(1)} %slice.143), channel_id=1, source_target_pairs={{0,2},{1,3},{2,0},{3,1},{4,6},{5,7},{6,4},{7,5},{8,10},{9,11},{10,... | collective-permute-start | bytes 147464 | tf_op jit(solution)/shard_map/ppermute | solution.py:107
  409.8 10.4 %collective-permute-start.50 = (bf16[1,96,576]{1,2,0:T(8,128)(2,1)S(1)}, bf16[1,96,576]{1,2,0:T(8,128)(2,1)S(1)}, u32[]{:S(2)}, u32[]{:S(2)}) collective-permute-start(bf16[1,96,576]{1,2,0:T(8,128)(2,1)S(1)} %slice.141), channel_id=1, source_target_pairs={{0,2},{1,3},{2,0},{3,1},{4,6},{5,7},{6,4},{7,5},{8,10},{9,11},{10,... | collective-permute-start | bytes 331784 | tf_op jit(solution)/shard_map/ppermute | solution.py:107
  (55 other events, 242.7 us)
Sparse Core Ops, SparseCore 0:
  63.6 28.2 all-gather.2
  96.6 27.8 all-gather.4
  346.3 27.7 reduce-scatter.1

commit v2 on v1

--- a/solution.py
+++ b/solution.py
@@ -200,10 +200,10 @@
         (got,) = yield [swap(value, TENSOR, 1)]
         mine = finish(name + "_rows", value, got)
     if two_links(mine.shape[0]):
-        sibling = swap(mine, FSDP, 1)
-        first, first_other = yield [swap_first(mine), swap_first(sibling)]
-        second = swap(first_other, FSDP, 1)
-        second_other, both = yield [swap(first, FSDP, 1), swap_first(second)]
+        sibling, first = yield [swap(mine, FSDP, 1), swap_first(mine)]
+        first, first_other = yield [first, swap_first(sibling)]
+        second_other, second = yield [swap(first, FSDP, 1), swap(first_other, FSDP, 1)]
+        (both,) = yield [swap_first(second)]
         both_other = swap(both, FSDP, 1)
         store((mine, first, second, both, sibling, second_other, first_other, both_other))
     else:
@@ -216,7 +216,7 @@
     return (left.astype(WIDE) + right.astype(WIDE)).astype(LOW)
 
 
-def scatter_weight(run, name, left, right, split, store, beside=None, swaps=False):
+def scatter_weight(run, name, left, right, split, store, beside=None, triple=False):
     rows, width = left.shape
     fsdp = lax.axis_size(FSDP)
     depth = width // fsdp
@@ -283,12 +283,27 @@
                 lanes = slice(k * n, (k + 1) * n)
                 out[...] = add_low(own[:, lanes], got[:, lanes])
 
-        def third_rows(where, own, got, out):
+        def third_split(own, got, keep, send):
+            n = columns // 12
+            for p in range(4):
+                out = keep if p < 2 else send
+                for k in range(3):
+                    lanes = slice((4 * k + p) * n, (4 * k + p + 1) * n)
+                    out[at[p % 2], k * n : (k + 1) * n] = add_low(own[:, lanes], got[:, lanes])
+
+        def third_rows(where, own, got, keep, send):
             n = columns // 4
             for k in range(4):
                 lanes = slice(k * n, (k + 1) * n)
-                row = pl.multiple_of(where[k] * depth, depth)
-                out[pl.ds(row, depth)] = add_low(own[:, lanes], got[:, lanes])
+                row = pl.multiple_of((where[k] & 1) * depth, depth)
+
+                @pl.when(where[k] < 2)
+                def _():
+                    keep[pl.ds(row, depth)] = add_low(own[:, lanes], got[:, lanes])
+
+                @pl.when(where[k] >= 2)
+                def _():
+                    send[pl.ds(row, depth)] = add_low(own[:, lanes], got[:, lanes])
 
         pair = ((2 * depth, columns), LOW, pl.BlockSpec((2 * depth, out_step), lambda j: (0, j)))
         keep, send = run.call(name + "_near", near_kernel, near_ins, [pair] * 2, grid=(2 * steps,), **cost)
@@ -298,14 +313,19 @@
         (got,) = yield [swap_second(onward)]
         ins = [(own, one[2]), (got, one[2])]
         if split is None:
-            shape = (4 * depth, columns // 4)
+            shape = (2 * depth, columns // 4)
             m = jnp.arange(4, dtype=jnp.int32) ^ lax.axis_index(TENSOR)
-            places = (m & 1) * 2 + (m >> 1) if swaps else jnp.arange(4, dtype=jnp.int32)
-            ins = [(places, SCALARS)] + ins
-            here = run.call(name + "_add3", third_rows, ins, [(shape, LOW, whole(*shape))], moved=6 * depth * columns)[0]
+            ins = [((m & 1) * 2 + (m >> 1), SCALARS)] + ins
+            here = run.call(
+                name + "_add3", third_rows, ins, [(shape, LOW, whole(*shape))] * 2, moved=6 * depth * columns
+            )
+            split = lambda *parts: tuple(value.reshape(2, depth, -1) for value in parts)
         else:
-            shape = (depth, half)
-            here = run.call(name + "_add3", third, ins, [(shape, LOW, whole(*shape))] * 2, moved=6 * depth * columns)
+            shape = (2 * depth, columns // 4) if triple else (depth, half)
+            work = third_split if triple else third
+            here = run.call(name + "_add3", work, ins, [(shape, LOW, whole(*shape))] * 2, moved=6 * depth * columns)
+            if triple:
+                split = lambda *parts: tuple(value.reshape(2, depth, -1) for value in parts)
     else:
 
         def near_kernel(left_ref, right_ref, got_ref, *refs):
@@ -327,12 +347,8 @@
             here = add_low(here[:count], got)
         if split is None:
             here = here[0].reshape(depth, 4, -1).transpose(1, 0, 2).reshape(4 * depth, -1)
-            swaps = False
         else:
             here = (here[0, :, :half], here[0, :, half:])
-    if split is None and swaps:
-        split = lambda blocks: tuple(blocks.reshape(2, 2, depth, -1))
-        here = (here,)
     if split is None:
         (here,) = yield [lax.psum_scatter(here, TENSOR, scatter_dimension=0, tiled=True)]
         store(here.astype(WIDE))
@@ -363,24 +379,24 @@
     store(gains, sums[0])
 
 
-def leave_columns(run, name, value, dtype, store):
+def leave_columns(run, name, value, dtype, count, store):
     size = lax.axis_size(TENSOR)
     (got,) = yield [lax.all_to_all(value, TENSOR, 0, 0, tiled=True)]
-    columns, rows = got.shape[0] // size, got.shape[1]
-
-    def kernel(ref, out):
-        out[...] = ref[...].astype(dtype)
-
-    store(
-        run.call(
-            name,
-            kernel,
-            [(got, pl.BlockSpec((columns, rows), lambda i: (i, 0)))],
-            [((columns, size * rows), dtype, pl.BlockSpec((columns, rows), lambda i: (0, i)))],
-            grid=(size,),
-            moved=8 * columns * rows,
-        )[0].T
+    columns, rows = got.shape[0] // size, got.shape[1] // count
+
+    def kernel(ref, *outs):
+        for k, out in enumerate(outs):
+            out[...] = ref[:, k * rows : (k + 1) * rows].astype(dtype)
+
+    results = run.call(
+        name,
+        kernel,
+        [(got, pl.BlockSpec((columns, count * rows), lambda i: (i, 0)))],
+        [((columns, size * rows), dtype, pl.BlockSpec((columns, rows), lambda i: (0, i)))] * count,
+        grid=(size,),
+        moved=8 * columns * rows,
     )
+    store(*[result.T for result in results])
 
 
 def put_turned(value, natural, out, tile):
@@ -692,9 +708,10 @@
     have = types.SimpleNamespace()
     run = Order()
 
-    def keep(name):
-        def store(value):
-            setattr(have, name, value)
+    def keep(*names):
+        def store(*values):
+            for name, value in zip(names, values):
+                setattr(have, name, value)
 
         return store
 
@@ -928,40 +945,91 @@
             [(have.betas, SCALARS)], [LOW, LOW],
         )
 
-    def down_teacher():
-        def work(product, refs, outs, tile):
-            here = rows_at(tile)
-            normed, _ = norm_parts(refs[0][here] + product)
-            outs[0][here] = normed
-            put_turned(normed.astype(LOW), refs[1], outs[1], tile)
-
-        have.t_result, have.t_leave = times_turned(
-            run, "down_teacher", have.t_hidden, have.w_down, wide_tiles(0), work,
-            [], [have.t_first, have.leave], [square, packed],
-        )
-
-    def down_student():
-        def work(product, refs, outs, tile):
-            betas, first_gain, second_gain, n_first, t_result, live_rows, leave = refs
-            here = rows_at(tile)
-            normed, size = norm_parts(n_first[here] * first_gain[...] + betas[3] * product)
-            result = normed * second_gain[...]
-            d_result = jnp.where(live_rows[here][:, 0:1] > 0, result - t_result[here], 0.0)
-            add_column_sums(outs[2], d_result * normed, tile)
-            d_second = norm_back(d_result * second_gain[...], normed, size)
-            outs[0][here] = d_second
-            outs[1][here] = (betas[3] * d_second).astype(LOW)
-            put_turned(result.astype(LOW), leave, outs[3], tile)
-
-        have.d_second, have.grad_z, have.sums_second, have.s_leave = times_turned(
-            run, "down_student", have.hidden, have.w_down, wide_tiles(1), work,
-            [
+    def down_both():
+        parts = have.w_down
+        count = len(parts)
+        late = [have.t_first, have.n_first, have.live_rows, have.leave]
+
+        def kernel(t_left, s_left, *refs):
+            blocks, refs = refs[:count], refs[count:]
+            betas, first_gain, second_gain = refs[:3]
+            sources = refs[3:7]
+            d_second, grad_z, sums, packed = refs[7:11]
+            t_total, s_total, weight, t_first, n_first, live_rows, leave, sems = refs[11:]
+            j = pl.program_id(0)
+            copies = [
+                pltpu.make_async_copy(source, to, sems.at[k])
+                for k, (source, to) in enumerate(zip(sources, (t_first, n_first, live_rows, leave)))
+            ]
+
+            @pl.when(j == 0)
+            def _():
+                for copy in copies:
+                    copy.start()
+
+            row = 0
+            for block in blocks:
+                weight[pl.ds(row, block.shape[0])] = block[...]
+                row += block.shape[0]
+
+            def add(total, left, first):
+                product = kernel_nt(left[...], weight[...])
+
+                @pl.when(j == first)
+                def _():
+                    total[...] = product
+
+                @pl.when(j > first)
+                def _():
+                    total[...] = total[...] + product
+
+            pl.when(j < tensor)(lambda: add(t_total, t_left, 0))
+            pl.when(j >= tensor)(lambda: add(s_total, s_left, tensor))
+
+            @pl.when(j == 2 * tensor - 1)
+            def _():
+                for copy in copies:
+                    copy.wait()
+                for tile in range(rows // TILE):
+                    here = rows_at(tile)
+                    t_result, _ = norm_parts(t_first[here] + t_total[here])
+                    normed, size = norm_parts(n_first[here] * first_gain[...] + betas[3] * s_total[here])
+                    result = normed * second_gain[...]
+                    d_result = jnp.where(live_rows[here][:, 0:1] > 0, result - t_result, 0.0)
+                    add_column_sums(sums, d_result * normed, tile)
+                    value = norm_back(d_result * second_gain[...], normed, size)
+                    d_second[here] = value
+                    grad_z[here] = (betas[3] * value).astype(LOW)
+                    put_turned(t_result.astype(LOW), leave, packed, tile)
+                    put_turned(result.astype(LOW), leave, packed, rows // TILE + tile)
+
+        tiles = pl.BlockSpec((rows, width), lambda j: (0, jnp.clip(j, 0, tensor - 1)))
+        later = pl.BlockSpec((rows, width), lambda j: (0, jnp.clip(j - tensor, 0, tensor - 1)))
+
+        def place(j):
+            return (0, jnp.where(j < tensor, 2 * j, 2 * (j - tensor) + 1))
+
+        have.d_second, have.grad_z, have.sums_second, have.leaving = run.call(
+            "down_both",
+            kernel,
+            [(have.t_hidden, tiles), (have.hidden, later)]
+            + [(part, pl.BlockSpec((part.shape[0], width), place)) for part in parts]
+            + [
                 (have.betas, SCALARS),
                 (have.first_gain, whole(1, width)),
                 (have.second_gain, whole(1, width)),
+            ]
+            + [(value, IN_PLACE) for value in late],
+            [
+                (shape, dtype, whole(*shape))
+                for shape, dtype in (square, square_low, ((8, width), WIDE), ((width, 2 * rows), LOW))
             ],
-            [have.n_first, have.t_result, have.live_rows, have.leave],
-            [square, square_low, ((8, width), WIDE), packed],
+            grid=(2 * tensor,),
+            scratch=[pltpu.VMEM((rows, width), WIDE), pltpu.VMEM((rows, width), WIDE), pltpu.VMEM((width, width), LOW)]
+            + [pltpu.VMEM(value.shape, value.dtype) for value in late]
+            + [pltpu.SemaphoreType.DMA((4,))],
+            flops=4 * rows * width * hidden_width,
+            moved=4 * (rows * hidden_width + width * hidden_width),
         )
 
 
@@ -987,7 +1055,7 @@
         )[0]
 
     def share_up():
-        return Task(scatter_weight(run, "g_up", have.middle, have.grad_u, None, keep("grad_up"), swaps=True))
+        return Task(scatter_weight(run, "g_up", have.middle, have.grad_u, None, keep("grad_up")))
 
     def back_up():
         def work(product, refs, outs, tile):
@@ -1021,7 +1089,7 @@
         )
 
     def share_qkv():
-        return Task(scatter_weight(run, "g_qkv", have.entry, have.g_all, split_qkv, keep("grad_qkv")))
+        return Task(scatter_weight(run, "g_qkv", have.entry, have.g_all, split_qkv, keep("grad_qkv"), triple=True))
 
     def back_entry():
         def work(product, refs, outs, tile):
@@ -1056,22 +1124,33 @@
     run.land(small)
     go_on(sa)
     go_on(ta)
+    run.land(ta, only=0)
+    run.fence()
+    go_on(ta)
     run.land(sa)
     go_on(c)
+    run.land(ta)
+    go_on(sa)
     go_on(d)
-    run.land(ta, only=0)
+    go_on(small)
+    go_on(ta)
+    run.land(ta, only=1)
+    run.land(sa, only=0)
+    run.fence()
+    go_on(ta)
     go_on(sa)
-    go_on(small)
-    run.land(ta, only=1)
+    run.land(sa)
     run.land(small)
     run.fence()
-    go_on(ta)
     go_on(small)
-    run.land(sa, small)
+    go_on(sa)
+    run.land(sa, only=1)
+    run.land(small)
     run.fence()
     finish(small)
+    go_on(sa)
     finish(ta)
-    go_on(sa)
+    go_on(c)
     go_on(c)
     project_teacher()
     finish(sa)
@@ -1080,7 +1159,9 @@
     run.land(c, d)
     run.fence()
     go_on(c)
+    go_on(c)
     attend(1)
+    go_on(d)
     go_on(d)
     close_teacher()
     run.land(c)
@@ -1088,50 +1169,48 @@
     finish(c)
     run.land(d, only=0)
     up_teacher()
-    up_student()
     run.land(d, only=1)
     run.fence()
+    go_on(d)
+    go_on(d)
+    up_student()
+    run.land(d)
+    run.fence()
     finish(d)
-    down_teacher()
-    t_leave = Task(leave_columns(run, "arrive_teacher", have.t_leave, LOW, keep("teacher_out")))
-    go_on(t_leave)
-    down_student()
-    s_leave = Task(leave_columns(run, "arrive_student", have.s_leave, LOW, keep("student_out")))
+    down_both()
+    leaving = Task(leave_columns(run, "arrive", have.leaving, LOW, 2, keep("teacher_out", "student_out")))
+    go_on(leaving)
     down = share_down()
     go_on(down)
     back_down()
-    run.land(t_leave)
     up = share_up()
     go_on(up)
-    go_on(s_leave)
     go_on(down)
     go_on(up)
     back_up()
-    run.land(s_leave)
+    go_on(down)
     back_attend()
     go_on(down)
+    go_on(up)
     qkv = share_qkv()
     go_on(qkv)
+    run.land(down, leaving)
     go_on(up)
+    go_on(down)
     back_entry()
-    g_leave = Task(leave_columns(run, "arrive_grad", have.g_leave, WIDE, keep("input_grad")))
+    g_leave = Task(leave_columns(run, "arrive_grad", have.g_leave, WIDE, 1, keep("input_grad")))
     go_on(g_leave)
+    run.land(down, up)
     go_on(qkv)
-    go_on(down)
     go_on(up)
     out = share_out()
     go_on(out)
-    finish(t_leave)
-    run.land(qkv)
     go_on(out)
     go_on(qkv)
-    run.land(up)
-    finish(s_leave)
-    go_on(up)
+    finish(leaving)
+    go_on(qkv)
     go_on(out)
-    run.land(qkv, down)
     finish(g_leave)
-    go_on(qkv)
     go_on(out)
     finish(qkv)
     finish(out)

time: 435 us -> 406 us (0.933)
  waiting for transfers between devices: 87.3 us -> 69.8 us
  starting transfers between devices: 62.1 us -> 55.9 us
    ppermute x16, waiting for transfers between devices: 41.2 us -> 28.3 us  [swap_first(): lax.ppermute(value, FSDP, [(i, i ^ (4 if i % 2 else 2)) for i in range(8)])]
    pallas_call x48 -> x49, Pallas kernels: 221 us -> 217 us  [call(): pl.pallas_call(wrapped, grid=grid, in_specs=[spec for _, spec in ins] + [...]
    all_to_all x3 -> x2, starting transfers between devices: 11.6 us -> 7.68 us  [leave_columns(): got, = (yield [lax.all_to_all(value, TENSOR, 0, 0, tiled=True)])]
    ppermute x35 -> x37, waiting for transfers between devices: 42.9 us -> 40.9 us  [swap(): return lax.ppermute(value, axis, [(i, i ^ bit) for i in range(size)])]
    ppermute x35 -> x37, starting transfers between devices: 29.2 us -> 27.7 us  [swap(): return lax.ppermute(value, axis, [(i, i ^ bit) for i in range(size)])]
    unnamed x121 -> x143, local copies, waits for them, and re-layouts: 24.3 us -> 25.6 us
  transfers between devices with their start and end apart: 61 -> 61, of which waited for: 26 -> 23; matrix products, arithmetic and copies ran while one was open for 4% -> 4% of each run, Pallas kernels for 48% -> 47%
where the time goes in v2:
time: 406 us; the launch traced here: 399 us
  Pallas kernels  217 us (53%)
  waiting for transfers between devices  69.8 us (17%)
  starting transfers between devices  55.9 us (14%)
  local copies, waits for them, and re-layouts  31.5 us (8%)
  between operations  15 us (4%)
  other arithmetic  9.79 us (2%)
    pallas_call x49, Pallas kernels, call(): pl.pallas_call(wrapped, grid=grid, in_specs=[spec for _, spec in ins] + [...  217 us
    ppermute x37, waiting for transfers between devices, swap(): return lax.ppermute(value, axis, [(i, i ^ bit) for i in range(size)])  40.9 us
    ppermute x16, waiting for transfers between devices, swap_first(): lax.ppermute(value, FSDP, [(i, i ^ (4 if i % 2 else 2)) for i in range(8)])  28.3 us
    ppermute x37, starting transfers between devices, swap(): return lax.ppermute(value, axis, [(i, i ^ bit) for i in range(size)])  27.7 us
    unnamed x143, local copies, waits for them, and re-layouts  25.6 us
    ppermute x16, starting transfers between devices, swap_first(): lax.ppermute(value, FSDP, [(i, i ^ (4 if i % 2 else 2)) for i in range(8)])  16.4 us
  transfers between devices with their start and end apart: 61, of which 23 were waited for; matrix products, arithmetic and copies ran while one was open for 4% of the time, Pallas kernels for 47%

profile of v2, /device:TPU:0, one launch (start us, length us, event | category | flops | bytes accessed | tf_op | source)
XLA Modules:
  0.0 399.4 jit_solution(12628557931324945111)
XLA Ops:
  9.6 4.1 %collective-permute-start.1 = (bf16[96,768]{1,0:T(8,128)(2,1)S(1)}, bf16[96,768]{1,0:T(8,128)(2,1)S(1)}, u32[]{:S(2)}, u32[]{:S(2)}) collective-permute-start(bf16[96,768]{1,0:T(8,128)(2,1)S(1)} %pad_maximum_fusion.refs_4_.refs_0_), channel_id=1, source_target_pairs={{0,2},{1,3},{2,0},{3,1},{4,6},{5,7},{6,4},{7,5},{8,10},{9,11},{10,... | collective-permute-start | bytes 442376 | tf_op jit(solution)/shard_map/ppermute | solution.py:107
  14.6 2.1 magnitudes.1.refs_4_
  26.1 1.7 collective-permute-done.2.refs_2_
  28.5 1.7 w_tqkv_join.1
  33.1 5.8 %place_rows.1 = (bf16[768,768]{1,0:T(8,128)(2,1)}, bf16[768,768]{1,0:T(8,128)(2,1)}, bf16[768,768]{1,0:T(8,128)(2,1)}, bf16[768,768]{1,0:T(8,128)(2,1)}) custom-call(s32[9]{0:T(128)} %pad_add_fusion.refs_0_, bf16[3072,768]{1,0:T(8,128)(2,1)} %refs_1_.6, bf16[3072,768]{1,0:T(8,128)(2,1)} %refs_2_.5, bf16[96,1536]{1,0:T(8,128)(2,1)} %get-tuple-element.105.refs_3_.refs_0_), custom_call_target="tpu_custom_call" | custom-call | tf_op jit(solution)/shard_map/place_rows/pallas_call | solution.py:80
  39.6 1.7 w_qkv_join.1
  42.1 2.1 w_tqkv_rows.1.refs_1_
  49.8 8.6 %collective-permute-done.5.refs_2_ = bf16[96,1536]{1,0:T(8,128)(2,1)S(1)} collective-permute-done((bf16[96,1536]{1,0:T(8,128)(2,1)S(1)}, bf16[96,1536]{1,0:T(8,128)(2,1)S(1)}, u32[]{:S(2)}, u32[]{:S(2)}) %collective-permute-start.5) | collective-permute-done | bytes 294944 | tf_op jit(solution)/shard_map/ppermute | solution.py:107
  59.1 1.8 pack_up.1
  62.0 2.1 w_qkv_rows.1
  66.1 1.8 pack_down.1.refs_2_
  71.3 3.9 collective-permute-done.14.refs_2_
  75.2 5.9 %collective-permute-done.13.refs_1_ = bf16[96,3072]{1,0:T(8,128)(2,1)S(1)} collective-permute-done((bf16[96,3072]{1,0:T(8,128)(2,1)}, bf16[96,3072]{1,0:T(8,128)(2,1)S(1)}, u32[]{:S(2)}, u32[]{:S(2)}) %collective-permute-start.13) | collective-permute-done | bytes 589856 | tf_op jit(solution)/shard_map/ppermute | solution.py:111
  85.5 3.8 collective-permute-done.16.refs_1_
  93.6 2.3 w_up_rows.1.refs_9_.refs_1_
  97.4 3.4 collective-permute-done.17.refs_4_.refs_17_
  101.7 7.3 %project_teacher.1.refs_10_.refs_5_.refs_6_.refs_7_ = bf16[768,2304]{1,0:T(8,128)(2,1)} custom-call(bf16[768,768]{1,0:T(8,128)(2,1)} %get-tuple-element.125.refs_0_.refs_9_, bf16[96,3072]{1,0:T(8,128)(2,1)} %w_tqkv_rows.1.refs_1_, bf16[96,3072]{1,0:T(8,128)(2,1)} %get-tuple-element.126.refs_2_, bf16[96,3072]{1,0:T(8,128)(2,1)} %get-tuple-element.127.refs_3_, ...), custom_call_target="tpu_custom_call" | custom-call | flops 13589544960 | bytes 41287680 | tf_op jit(solution)/shard_map/project_teacher/pallas_call | solution.py:80
  111.2 7.0 %project_student.1.refs_2_.refs_3_.refs_4_.refs_8_.refs_1_ = bf16[768,2304]{1,0:T(8,128)(2,1)} custom-call(bf16[768,768]{1,0:T(8,128)(2,1)} %get-tuple-element.106.refs_0_, bf16[96,3072]{1,0:T(8,128)(2,1)} %get-tuple-element.114.refs_2_.refs_1_.refs_14_, bf16[96,3072]{1,0:T(8,128)(2,1)} %get-tuple-element.119.refs_2_.refs_15_, ...), custom_call_target="tpu_custom_call" | custom-call | flops 13589544960 | bytes 41287680 | tf_op jit(solution)/shard_map/project_student/pallas_call | solution.py:80
  118.2 8.5 %attend_forward.2 = (bf16[768,768]{1,0:T(8,128)(2,1)}, bf16[768,768]{1,0:T(8,128)(2,1)}, bf16[3,6,256,512]{3,2,1,0:T(8,128)(2,1)}, bf16[3,6,256,512]{3,2,1,0:T(8,128)(2,1)}) custom-call(s32[8,768]{1,0:T(8,128)} %get-tuple-element.102.refs_3_.refs_0_, s32[768,128]{1,0:T(8,128)} %get-tuple-element.103.refs_1_, ...), custom_call_target="tpu_custom_call" | custom-call | flops 12079595520 | bytes 35389440 | tf_op jit(solution)/shard_map/attend_forward/pallas_call | solution.py:80
  133.1 8.4 %attend_forward.3 = (bf16[768,768]{1,0:T(8,128)(2,1)}, bf16[768,768]{1,0:T(8,128)(2,1)}, bf16[3,6,256,512]{3,2,1,0:T(8,128)(2,1)}, bf16[3,6,256,512]{3,2,1,0:T(8,128)(2,1)}) custom-call(s32[8,768]{1,0:T(8,128)} %get-tuple-element.102.refs_3_.refs_0_, ...), custom_call_target="tpu_custom_call", output_to_operand_aliasing={{0}: (8, {}), {1}: (9, {}), {2}: (10, {}), {3}: (11, {})} | custom-call | flops 12079595520 | bytes 35389440 | tf_op jit(solution)/shard_map/attend_forward/pallas_call | solution.py:80
  141.6 2.4 w_down_rows.1.refs_10_.refs_2_.refs_1_
  145.9 5.5 %close_teacher.1 = (f32[768,768]{1,0:T(8,128)}, bf16[768,768]{1,0:T(8,128)(2,1)}) custom-call(bf16[768,768]{1,0:T(8,128)(2,1)} %get-tuple-element.136.refs_0_, bf16[96,3072]{1,0:T(8,128)(2,1)} %w_tqkv_rows.1.refs_1_, bf16[96,3072]{1,0:T(8,128)(2,1)} %get-tuple-element.126.refs_2_, bf16[96,3072]{1,0:T(8,128)(2,1)} %get-tuple-element.127.refs_3_, ...), custom_call_target="tpu_custom_call" | custom-call | flops 4529848320 | bytes 11796480 | tf_op jit(solution)/shard_map/close_teacher/pallas_call | solution.py:80
  152.4 6.0 %close_student.1 = (f32[768,768]{1,0:T(8,128)}, f32[768,128]{1,0:T(8,128)}, bf16[768,768]{1,0:T(8,128)(2,1)}, bf16[96,6144]{1,0:T(8,128)(2,1)}) custom-call(bf16[768,768]{1,0:T(8,128)(2,1)} %get-tuple-element.134.refs_1_.refs_0_, bf16[96,3072]{1,0:T(8,128)(2,1)} %get-tuple-element.114.refs_2_.refs_1_.refs_14_, ...), custom_call_target="tpu_custom_call", output_to_operand_aliasing={{3}: (12, {})} | custom-call | flops 4529848320 | bytes 11796480 | tf_op jit(solution)/shard_map/close_student/pallas_call | solution.py:80
  159.3 2.0 collective-permute-done.30.refs_9_
  162.6 8.3 %up_teacher.1 = (bf16[768,3072]{1,0:T(8,128)(2,1)}, bf16[96,6144]{1,0:T(8,128)(2,1)}) custom-call(bf16[768,768]{1,0:T(8,128)(2,1)} %get-tuple-element.140.refs_0_, bf16[96,6144]{1,0:T(8,128)(2,1)} %w_up_rows.1.refs_9_.refs_1_, bf16[96,6144]{1,0:T(8,128)(2,1)} %get-tuple-element.141.refs_2_, ...), custom_call_target="tpu_custom_call", output_to_operand_aliasing={{1}: (9, {})} | custom-call | flops 18119393280 | bytes 53084160 | tf_op jit(solution)/shard_map/up_teacher/pallas_call | solution.py:80
  170.9 4.1 %collective-permute-done.32.refs_0_ = bf16[96,6144]{1,0:T(8,128)(2,1)S(1)} collective-permute-done((bf16[96,6144]{1,0:T(8,128)(2,1)}, bf16[96,6144]{1,0:T(8,128)(2,1)S(1)}, u32[]{:S(2)}, u32[]{:S(2)}) %collective-permute-start.32) | collective-permute-done | bytes 1179680 | tf_op jit(solution)/shard_map/ppermute | solution.py:111
  177.1 2.5 collective-permute-done.33.refs_4_.refs_3_
  180.4 10.3 %up_student.1 = (bf16[768,3072]{1,0:T(8,128)(2,1)}, bf16[768,3072]{1,0:T(8,128)(2,1)}) custom-call(bf16[768,768]{1,0:T(8,128)(2,1)} %get-tuple-element.139.refs_0_, bf16[96,6144]{1,0:T(8,128)(2,1)} %w_up_rows.1.refs_9_.refs_1_, bf16[96,6144]{1,0:T(8,128)(2,1)} %get-tuple-element.141.refs_2_, bf16[96,6144]{1,0:T(8,128)(2,1)} %copy-done.58, ...), custom_call_target="tpu_custom_call" | custom-call | flops 18119393280 | bytes 76677120 | tf_op jit(solution)/shard_map/up_student/pallas_call | solution.py:80
  190.8 5.1 %collective-permute-done.34.refs_0_ = bf16[96,6144]{1,0:T(8,128)(2,1)S(1)} collective-permute-done((bf16[96,6144]{1,0:T(8,128)(2,1)S(1)}, bf16[96,6144]{1,0:T(8,128)(2,1)S(1)}, u32[]{:S(2)}, u32[]{:S(2)}) %collective-permute-start.34) | collective-permute-done | bytes 1179680 | tf_op jit(solution)/shard_map/ppermute | solution.py:111
  197.5 3.0 collective-permute-done.36.refs_9_.refs_8_
  201.6 21.1 %down_both.1 = (f32[768,768]{1,0:T(8,128)}, bf16[768,768]{1,0:T(8,128)(2,1)}, f32[8,768]{1,0:T(8,128)}, bf16[768,1536]{1,0:T(8,128)(2,1)}) custom-call(bf16[768,3072]{1,0:T(8,128)(2,1)} %get-tuple-element.144.refs_1_.refs_0_, bf16[768,3072]{1,0:T(8,128)(2,1)} %get-tuple-element.146.refs_1_, bf16[96,6144]{1,0:T(8,128)(2,1)} %w_down_rows.1.refs_10_.refs_2_.refs_1_, ...), custom_call_target="tpu_custom_call" | custom-call | flops 36238786560 | bytes 94371840 | tf_op jit(solution)/shard_map/down_both/pallas_call | solution.py:80
  222.7 5.0 %g_down_far.1.refs_11_ = bf16[384,3072]{1,0:T(8,128)(2,1)} custom-call(bf16[768,768]{1,0:T(8,128)(2,1)} %get-tuple-element.153.refs_0_, bf16[768,3072]{1,0:T(8,128)(2,1)} %get-tuple-element.146.refs_1_, f32[768,768]{1,0:T(8,128)} %get-tuple-element.155.refs_2_.refs_11_), custom_call_target="tpu_custom_call" | custom-call | flops 9059696640 | bytes 47185920 | tf_op jit(solution)/shard_map/g_down_far/pallas_call | solution.py:80
  227.9 9.3 %back_down.1.refs_1_.refs_2_.refs_0_ = bf16[768,3072]{1,0:T(8,128)(2,1)} custom-call(bf16[768,768]{1,0:T(8,128)(2,1)} %get-tuple-element.153.refs_0_, bf16[96,6144]{1,0:T(8,128)(2,1)} %w_down_rows.1.refs_10_.refs_2_.refs_1_, bf16[96,6144]{1,0:T(8,128)(2,1)} %get-tuple-element.147.refs_3_.refs_2_, bf16[96,6144]{1,0:T(8,128)(2,1)} %copy-done.60, ...), custom_call_target="tpu_custom_call" | custom-call | flops 18119393280 | bytes 53084160 | tf_op jit(solution)/shard_map/back_down/pallas_call | solution.py:80
  237.1 5.1 %g_up_far.1.refs_3_ = bf16[384,3072]{1,0:T(8,128)(2,1)} custom-call(bf16[768,768]{1,0:T(8,128)(2,1)} %get-tuple-element.139.refs_0_, bf16[768,3072]{1,0:T(8,128)(2,1)} %back_down.1.refs_1_.refs_2_.refs_0_, bf16[768,3072]{1,0:T(8,128)(2,1)} %back_down.1.refs_1_.refs_2_.refs_0_), custom_call_target="tpu_custom_call" | custom-call | flops 9059696640 | bytes 47185920 | tf_op jit(solution)/shard_map/g_up_far/pallas_call | solution.py:80
  243.1 4.0 %all-to-all-start = ((bf16[4,192,1536]{2,1,0:T(8,128)(2,1)}), bf16[4,192,1536]{2,1,0:T(8,128)(2,1)S(1)}, u32[]{:S(2)}, u32[]{:S(2)}) async-start(bf16[4,192,1536]{2,1,0:T(8,128)(2,1)} %bitcast.99), calls=%async_computation | async-start | bytes 4718592 | tf_op jit(solution)/shard_map/all_to_all | solution.py:384
  247.2 5.5 %g_down_near.1 = (bf16[192,3072]{1,0:T(8,128)(2,1)}, bf16[192,3072]{1,0:T(8,128)(2,1)}) custom-call(bf16[768,768]{1,0:T(8,128)(2,1)} %get-tuple-element.153.refs_0_, bf16[768,3072]{1,0:T(8,128)(2,1)} %get-tuple-element.146.refs_1_, bf16[384,3072]{1,0:T(8,128)(2,1)} %collective-permute-done.38.refs_2_, bf16[384,3072]{1,0:T(8,128)(2,1)} %g_up_far.1.refs_3_), custom_call_target="tpu_custom_call" | custom-call | flops 9059696640 | bytes 47185920 | tf_op jit(solution)/shard_map/g_down_near/pallas_call | solution.py:80
  253.4 5.4 %g_up_near.1 = (bf16[192,3072]{1,0:T(8,128)(2,1)}, bf16[192,3072]{1,0:T(8,128)(2,1)}) custom-call(bf16[768,768]{1,0:T(8,128)(2,1)} %get-tuple-element.139.refs_0_, bf16[768,3072]{1,0:T(8,128)(2,1)} %back_down.1.refs_1_.refs_2_.refs_0_, bf16[384,3072]{1,0:T(8,128)(2,1)} %collective-permute-done.37.refs_2_, bf16[192,3072]{1,0:T(8,128)(2,1)} %get-tuple-element.156.refs_3_.refs_0_), custom_call_target="tpu_custom_call" | custom-call | flops 9059696640 | bytes 47185920 | tf_op jit(solution)/shard_map/g_up_near/pallas_call | solution.py:80
  260.1 12.7 %back_up.1 = (f32[768,768]{1,0:T(8,128)}, bf16[768,768]{1,0:T(8,128)(2,1)}, bf16[768,768]{1,0:T(8,128)(2,1)}, f32[8,768]{1,0:T(8,128)}) custom-call(bf16[768,3072]{1,0:T(8,128)(2,1)} %back_down.1.refs_1_.refs_2_.refs_0_, bf16[96,6144]{1,0:T(8,128)(2,1)} %w_up_rows.1.refs_9_.refs_1_, bf16[96,6144]{1,0:T(8,128)(2,1)} %get-tuple-element.141.refs_2_, ...), custom_call_target="tpu_custom_call" | custom-call | flops 18119393280 | bytes 47185920 | tf_op jit(solution)/shard_map/back_up/pallas_call | solution.py:80
  272.8 2.8 g_down_add2.1
  276.4 11.5 %attend_backward.1.refs_3_.refs_1_.refs_0_ = bf16[768,2304]{1,0:T(8,128)(2,1)} custom-call(f32[4]{0:T(128)} %multiply_bitcast_fusion.refs_9_.refs_10_.refs_0_, bf16[768,2304]{1,0:T(8,128)(2,1)} %project_student.1.refs_2_.refs_3_.refs_4_.refs_8_.refs_1_, bf16[768,768]{1,0:T(8,128)(2,1)} %get-tuple-element.164.refs_2_, ...), custom_call_target="tpu_custom_call" | custom-call | flops 12079595520 | bytes 70778880 | tf_op jit(solution)/shard_map/attend_backward/pallas_call | solution.py:80
  287.9 2.3 g_down_add3.1
  291.2 2.8 g_up_add2.1
  295.2 2.0 collective-permute-start.43
  297.2 4.5 %g_qkv_far.1.refs_5_ = bf16[384,2304]{1,0:T(8,128)(2,1)} custom-call(bf16[768,768]{1,0:T(8,128)(2,1)} %get-tuple-element.106.refs_0_, bf16[768,2304]{1,0:T(8,128)(2,1)} %attend_backward.1.refs_3_.refs_1_.refs_0_, bf16[96,3072]{1,0:T(8,128)(2,1)} %get-tuple-element.168.refs_2_.refs_1_), custom_call_target="tpu_custom_call" | custom-call | flops 6794772480 | bytes 35389440 | tf_op jit(solution)/shard_map/g_qkv_far/pallas_call | solution.py:80
  301.7 6.2 %collective-permute-done.43.refs_3_ = bf16[2,96,768]{2,1,0:T(8,128)(2,1)S(1)} collective-permute-done((bf16[2,96,768]{2,1,0:T(8,128)(2,1)}, bf16[2,96,768]{2,1,0:T(8,128)(2,1)S(1)}, u32[]{:S(2)}, u32[]{:S(2)}) %collective-permute-start.43) | collective-permute-done | bytes 294944 | tf_op jit(solution)/shard_map/ppermute | solution.py:107
  308.8 2.3 g_up_add3.1
  312.3 2.0 collective-permute-start.46
  314.3 8.9 %back_entry.1.refs_5_ = bf16[768,768]{1,0:T(8,128)(2,1)} custom-call(bf16[768,2304]{1,0:T(8,128)(2,1)} %attend_backward.1.refs_3_.refs_1_.refs_0_, bf16[96,3072]{1,0:T(8,128)(2,1)} %get-tuple-element.114.refs_2_.refs_1_.refs_14_, bf16[96,3072]{1,0:T(8,128)(2,1)} %get-tuple-element.119.refs_2_.refs_15_, bf16[96,3072]{1,0:T(8,128)(2,1)} %get-tuple-element.123.refs_3_.refs_16_, ...), custom_call_target="tpu_custom_call" | custom-call | flops 13589544960 | bytes 35389440 | tf_op jit(solution)/shard_map/back_entry/pallas_call | solution.py:80
  323.2 3.6 all-to-all-start.1
  327.6 4.7 %g_qkv_near.1 = (bf16[192,2304]{1,0:T(8,128)(2,1)}, bf16[192,2304]{1,0:T(8,128)(2,1)}, bf16[1,96,768]{2,1,0:T(8,128)(2,1)}, bf16[2,96,768]{2,1,0:T(8,128)(2,1)}) custom-call(bf16[768,768]{1,0:T(8,128)(2,1)} %get-tuple-element.106.refs_0_, bf16[768,2304]{1,0:T(8,128)(2,1)} %attend_backward.1.refs_3_.refs_1_.refs_0_, ...), custom_call_target="tpu_custom_call", output_to_operand_aliasing={{2}: (3, {}), {3}: (4, {})} | custom-call | flops 6794772480 | bytes 35389440 | tf_op jit(solution)/shard_map/g_qkv_near/pallas_call | solution.py:80
  332.3 3.2 g_out_far.1.refs_5_
  336.4 1.8 collective-permute-done.48.refs_2_
  338.2 3.4 g_out_near.1
  342.3 6.5 %collective-permute-done.47.refs_1_ = bf16[192,2304]{1,0:T(8,128)(2,1)S(1)} collective-permute-done((bf16[192,2304]{1,0:T(8,128)(2,1)}, bf16[192,2304]{1,0:T(8,128)(2,1)S(1)}, u32[]{:S(2)}, u32[]{:S(2)}) %collective-permute-start.47) | collective-permute-done | bytes 884768 | tf_op jit(solution)/shard_map/ppermute | solution.py:111
  349.7 2.5 g_qkv_add2.1
  353.8 2.9 collective-permute-start.56
  357.5 3.9 arrive.1
  362.1 2.1 g_qkv_add3.1
  364.2 2.0 g_out_add2.1
  371.1 3.6 arrive_grad.1.refs_2_
  375.5 1.7 g_out_add3.1
  379.9 2.0 collective-permute-start.52
  381.9 3.1 collective-permute-done.54
  386.6 3.6 collective-permute-done.52
  (297 shorter events, 86.9 us)
Async XLA Ops:
  7.2 86.4 %all-gather.3.cloned.1.call-start = ((), (), s32[]{:S(2)}) async-start(), calls=%async_computation.2 | async-start | bytes 1474560 | tf_op jit(solution)/shard_map/all_gather | solution.py:195
  9.6 18.2 %collective-permute-start.1 = (bf16[96,768]{1,0:T(8,128)(2,1)S(1)}, bf16[96,768]{1,0:T(8,128)(2,1)S(1)}, u32[]{:S(2)}, u32[]{:S(2)}) collective-permute-start(bf16[96,768]{1,0:T(8,128)(2,1)S(1)} %pad_maximum_fusion.refs_4_.refs_0_), channel_id=1, source_target_pairs={{0,2},{1,3},{2,0},{3,1},{4,6},{5,7},{6,4},{7,5},{8,10},{9,11},{10,... | collective-permute-start | bytes 442376 | tf_op jit(solution)/shard_map/ppermute | solution.py:107
  16.7 15.0 %copy-start.56 = (s32[8]{0:T(128)S(1)}, s32[8]{0:T(128)}, u32[]{:S(2)}) copy-start(s32[8]{0:T(128)} %constant.34.clone) | copy-start | bytes 100
  16.7 15.0 %copy-start.57 = (s32[8]{0:T(128)S(1)}, s32[8]{0:T(128)}, u32[]{:S(2)}) copy-start(s32[8]{0:T(128)} %constant.35.clone) | copy-start | bytes 100
  17.5 3.7 collective-permute-start
  24.1 3.7 collective-permute-start.2
  25.7 13.3 %collective-permute-start.3 = (bf16[96,768]{1,0:T(8,128)(2,1)S(1)}, bf16[96,768]{1,0:T(8,128)(2,1)S(1)}, u32[]{:S(2)}, u32[]{:S(2)}) collective-permute-start(bf16[96,768]{1,0:T(8,128)(2,1)S(1)} %pad_maximum_fusion.1.refs_0_), channel_id=1, source_target_pairs={{0,2},{1,3},{2,0},{3,1},{4,6},{5,7},{6,4},{7,5},{8,10},{9,11},{10,... | collective-permute-start | bytes 442376 | tf_op jit(solution)/shard_map/ppermute | solution.py:107
  30.2 11.2 %collective-permute-start.6 = (bf16[96,1536]{1,0:T(8,128)(2,1)}, bf16[96,1536]{1,0:T(8,128)(2,1)S(1)}, u32[]{:S(2)}, u32[]{:S(2)}) collective-permute-start(bf16[96,1536]{1,0:T(8,128)(2,1)} %get-tuple-element.105.refs_3_.refs_0_), channel_id=1, source_target_pairs={{0,1},{1,0},{2,3},{3,2},{4,5},{5,4},{6,7},{7,6},{8,9},{9,8},{10,11... | collective-permute-start | bytes 884744 | tf_op jit(solution)/shard_map/ppermute | solution.py:107
  32.5 6.5 %collective-permute-start.4 = (f32[4,16,128]{2,1,0:T(8,128)S(1)}, f32[4,16,128]{2,1,0:T(8,128)S(1)}, u32[]{:S(2)}, u32[]{:S(2)}) collective-permute-start(f32[4,16,128]{2,1,0:T(8,128)S(1)} %pad_maximum_fusion.2), channel_id=1, source_target_pairs={{0,4},{4,0},{8,12},{12,8},{16,20},{20,16},{24,28},{28,24},{1,5},{5... | collective-permute-start | bytes 98312 | tf_op jit(solution)/shard_map/ppermute | solution.py:107
  44.2 2.3 collective-permute-start.7
  44.7 16.3 %collective-permute-start.8 = (bf16[96,3072]{1,0:T(8,128)(2,1)}, bf16[96,3072]{1,0:T(8,128)(2,1)S(1)}, u32[]{:S(2)}, u32[]{:S(2)}) collective-permute-start(bf16[96,3072]{1,0:T(8,128)(2,1)} %w_tqkv_rows.1.refs_1_), channel_id=1, source_target_pairs={{0,8},{4,20},{8,0},{12,28},{16,24},{20,4},{24,16},{28,12},{1,9},{5... | collective-permute-start | bytes 1769480 | tf_op jit(solution)/shard_map/ppermute | solution.py:111
  47.9 13.2 %collective-permute-start.9 = (bf16[96,3072]{1,0:T(8,128)(2,1)}, bf16[96,3072]{1,0:T(8,128)(2,1)S(1)}, u32[]{:S(2)}, u32[]{:S(2)}) collective-permute-start(bf16[96,3072]{1,0:T(8,128)(2,1)} %get-tuple-element.112.refs_5_), channel_id=1, source_target_pairs={{0,8},{4,20},{8,0},{12,28},{16,24},{20,4},{24,16},{28,12},{1,9},{5... | collective-permute-start | bytes 1769480 | tf_op jit(solution)/shard_map/ppermute | solution.py:111
  49.4 9.0 %collective-permute-start.5 = (bf16[96,1536]{1,0:T(8,128)(2,1)S(1)}, bf16[96,1536]{1,0:T(8,128)(2,1)S(1)}, u32[]{:S(2)}, u32[]{:S(2)}) collective-permute-start(bf16[96,1536]{1,0:T(8,128)(2,1)S(1)} %copy-done.16), channel_id=1, source_target_pairs={{0,1},{1,0},{2,3},{3,2},{4,5},{5,4},{6,7},{7,6},{8,9},{9,8},{10,11... | collective-permute-start | bytes 884744 | tf_op jit(solution)/shard_map/ppermute | solution.py:107
  64.0 3.9 collective-permute-start.11
  64.0 3.9 collective-permute-start.12
  64.6 62.1 %all-gather.5.cloned.1.call-start = ((), (), s32[]{:S(2)}) async-start(), calls=%async_computation.3 | async-start | bytes 1474560 | tf_op jit(solution)/shard_map/all_gather | solution.py:195
  64.6 10.6 %collective-permute-start.10 = (bf16[96,3072]{1,0:T(8,128)(2,1)}, bf16[96,3072]{1,0:T(8,128)(2,1)S(1)}, u32[]{:S(2)}, u32[]{:S(2)}) collective-permute-start(bf16[96,3072]{1,0:T(8,128)(2,1)} %get-tuple-element.114.refs_2_.refs_1_.refs_14_), channel_id=1, source_target_pairs={{0,8},{4,20},{8,0},{12,28},{16,24},{20,4},{24,16},{28,12},{1,9},{5... | collective-permute-start | bytes 1769480 | tf_op jit(solution)/shard_map/ppermute | solution.py:111
  67.9 17.6 %copy-start.29 = (bf16[96,3072]{1,0:T(8,128)(2,1)S(1)}, bf16[96,3072]{1,0:T(8,128)(2,1)}, u32[]{:S(2)}) copy-start(bf16[96,3072]{1,0:T(8,128)(2,1)} %get-tuple-element.126.refs_2_) | copy-start | bytes 1769476
  70.1 11.0 %collective-permute-start.13 = (bf16[96,3072]{1,0:T(8,128)(2,1)}, bf16[96,3072]{1,0:T(8,128)(2,1)S(1)}, u32[]{:S(2)}, u32[]{:S(2)}) collective-permute-start(bf16[96,3072]{1,0:T(8,128)(2,1)} %get-tuple-element.116.refs_5_.refs_18_), channel_id=1, source_target_pairs={{0,8},{4,20},{8,0},{12,28},{16,24},{20,4},{24,16},{28,12},{1,9},{5... | collective-permute-start | bytes 1769480 | tf_op jit(solution)/shard_map/ppermute | solution.py:111
  70.8 4.4 %collective-permute-start.14 = (f32[8,128]{1,0:T(8,128)S(1)}, f32[8,128]{1,0:T(8,128)S(1)}, u32[]{:S(2)}, u32[]{:S(2)}) collective-permute-start(f32[8,128]{1,0:T(8,128)S(1)} %fusion.11), channel_id=1, source_target_pairs={{0,1},{1,0},{2,3},{3,2},{4,5},{5,4},{6,7},{7,6},{8,9},{9,8},{10,11... | collective-permute-start | bytes 12296 | tf_op jit(solution)/shard_map/ppermute | solution.py:107
  82.5 6.8 %collective-permute-start.15 = (bf16[96,3072]{1,0:T(8,128)(2,1)}, bf16[96,3072]{1,0:T(8,128)(2,1)S(1)}, u32[]{:S(2)}, u32[]{:S(2)}) collective-permute-start(bf16[96,3072]{1,0:T(8,128)(2,1)} %get-tuple-element.120.refs_7_.refs_20_), channel_id=1, source_target_pairs={{0,4},{4,0},{8,12},{12,8},{16,20},{20,16},{24,28},{28,24},{1,5},{5... | collective-permute-start | bytes 1769480 | tf_op jit(solution)/shard_map/ppermute | solution.py:107
  82.5 10.0 %collective-permute-start.20 = (bf16[96,3072]{1,0:T(8,128)(2,1)S(1)}, bf16[96,3072]{1,0:T(8,128)(2,1)}, u32[]{:S(2)}, u32[]{:S(2)}) collective-permute-start(bf16[96,3072]{1,0:T(8,128)(2,1)S(1)} %copy-done.31), channel_id=1, source_target_pairs={{0,8},{4,20},{8,0},{12,28},{16,24},{20,4},{24,16},{28,12},{1,9},{5... | collective-permute-start | bytes 1769480 | tf_op jit(solution)/shard_map/ppermute | solution.py:111
  84.6 4.7 %collective-permute-start.16 = (f32[8,128]{1,0:T(8,128)S(1)}, f32[8,128]{1,0:T(8,128)S(1)}, u32[]{:S(2)}, u32[]{:S(2)}) collective-permute-start(f32[8,128]{1,0:T(8,128)S(1)} %fusion.21), channel_id=1, source_target_pairs={{0,2},{1,3},{2,0},{3,1},{4,6},{5,7},{6,4},{7,5},{8,10},{9,11},{10,... | collective-permute-start | bytes 12296 | tf_op jit(solution)/shard_map/ppermute | solution.py:107
  85.5 10.4 %collective-permute-start.21 = (bf16[96,3072]{1,0:T(8,128)(2,1)S(1)}, bf16[96,3072]{1,0:T(8,128)(2,1)}, u32[]{:S(2)}, u32[]{:S(2)}) collective-permute-start(bf16[96,3072]{1,0:T(8,128)(2,1)S(1)} %copy-done.29), channel_id=1, source_target_pairs={{0,4},{4,0},{8,12},{12,8},{16,20},{20,16},{24,28},{28,24},{1,5},{5... | collective-permute-start | bytes 1769480 | tf_op jit(solution)/shard_map/ppermute | solution.py:107
  90.7 10.1 %collective-permute-start.17 = (bf16[96,3072]{1,0:T(8,128)(2,1)}, bf16[96,3072]{1,0:T(8,128)(2,1)S(1)}, u32[]{:S(2)}, u32[]{:S(2)}) collective-permute-start(bf16[96,3072]{1,0:T(8,128)(2,1)} %get-tuple-element.123.refs_3_.refs_16_), channel_id=1, source_target_pairs={{0,8},{4,20},{8,0},{12,28},{16,24},{20,4},{24,16},{28,12},{1,9},{5... | collective-permute-start | bytes 1769480 | tf_op jit(solution)/shard_map/ppermute | solution.py:111
  92.5 8.3 %collective-permute-start.22 = (bf16[96,3072]{1,0:T(8,128)(2,1)}, bf16[96,3072]{1,0:T(8,128)(2,1)S(1)}, u32[]{:S(2)}, u32[]{:S(2)}) collective-permute-start(bf16[96,3072]{1,0:T(8,128)(2,1)} %collective-permute-done.20.refs_4_), channel_id=1, source_target_pairs={{0,4},{4,0},{8,12},{12,8},{16,20},{20,16},{24,28},{28,24},{1,5},{5... | collective-permute-start | bytes 1769480 | tf_op jit(solution)/shard_map/ppermute | solution.py:107
  92.5 17.8 %collective-permute-start.18 = (bf16[96,3072]{1,0:T(8,128)(2,1)}, bf16[96,3072]{1,0:T(8,128)(2,1)S(1)}, u32[]{:S(2)}, u32[]{:S(2)}) collective-permute-start(bf16[96,3072]{1,0:T(8,128)(2,1)} %get-tuple-element.119.refs_2_.refs_15_), channel_id=1, source_target_pairs={{0,4},{4,0},{8,12},{12,8},{16,20},{20,16},{24,28},{28,24},{1,5},{5... | collective-permute-start | bytes 1769480 | tf_op jit(solution)/shard_map/ppermute | solution.py:107
  95.9 13.7 %collective-permute-start.24 = (bf16[96,6144]{1,0:T(8,128)(2,1)}, bf16[96,6144]{1,0:T(8,128)(2,1)}, u32[]{:S(2)}, u32[]{:S(2)}) collective-permute-start(bf16[96,6144]{1,0:T(8,128)(2,1)} %w_up_rows.1.refs_9_.refs_1_), channel_id=1, source_target_pairs={{0,4},{4,0},{8,12},{12,8},{16,20},{20,16},{24,28},{28,24},{1,5},{5... | collective-permute-start | bytes 3538952 | tf_op jit(solution)/shard_map/ppermute | solution.py:107
  95.9 30.8 %collective-permute-start.23 = (bf16[96,6144]{1,0:T(8,128)(2,1)}, bf16[96,6144]{1,0:T(8,128)(2,1)S(1)}, u32[]{:S(2)}, u32[]{:S(2)}) collective-permute-start(bf16[96,6144]{1,0:T(8,128)(2,1)} %w_up_rows.1.refs_9_.refs_1_), channel_id=1, source_target_pairs={{0,8},{4,20},{8,0},{12,28},{16,24},{20,4},{24,16},{28,12},{1,9},{5... | collective-permute-start | bytes 3538952 | tf_op jit(solution)/shard_map/ppermute | solution.py:111
  100.8 9.5 %collective-permute-start.19 = (bf16[96,3072]{1,0:T(8,128)(2,1)S(1)}, bf16[96,3072]{1,0:T(8,128)(2,1)}, u32[]{:S(2)}, u32[]{:S(2)}) collective-permute-start(bf16[96,3072]{1,0:T(8,128)(2,1)S(1)} %collective-permute-done.17.refs_4_.refs_17_), channel_id=1, source_target_pairs={{0,4},{4,0},{8,12},{12,8},{16,20},{20,16},{24,28},{28,24},{1,5},{5... | collective-permute-start | bytes 1769480 | tf_op jit(solution)/shard_map/ppermute | solution.py:107
  109.6 17.1 %collective-permute-start.25 = (bf16[96,6144]{1,0:T(8,128)(2,1)}, bf16[96,6144]{1,0:T(8,128)(2,1)S(1)}, u32[]{:S(2)}, u32[]{:S(2)}) collective-permute-start(bf16[96,6144]{1,0:T(8,128)(2,1)} %collective-permute-done.24.refs_5_), channel_id=1, source_target_pairs={{0,8},{4,20},{8,0},{12,28},{16,24},{20,4},{24,16},{28,12},{1,9},{5... | collective-permute-start | bytes 3538952 | tf_op jit(solution)/shard_map/ppermute | solution.py:111
  128.8 3.6 collective-permute-start.26
  132.4 19.0 %collective-permute-start.27 = (bf16[96,6144]{1,0:T(8,128)(2,1)S(1)}, bf16[96,6144]{1,0:T(8,128)(2,1)S(1)}, u32[]{:S(2)}, u32[]{:S(2)}) collective-permute-start(bf16[96,6144]{1,0:T(8,128)(2,1)S(1)} %collective-permute-done.26.refs_3_), channel_id=1, source_target_pairs={{0,8},{4,20},{8,0},{12,28},{16,24},{20,4},{24,16},{28,12},{1,9},{5... | collective-permute-start | bytes 3538952 | tf_op jit(solution)/shard_map/ppermute | solution.py:111
  144.0 17.3 %collective-permute-start.30 = (bf16[96,6144]{1,0:T(8,128)(2,1)}, bf16[96,6144]{1,0:T(8,128)(2,1)}, u32[]{:S(2)}, u32[]{:S(2)}) collective-permute-start(bf16[96,6144]{1,0:T(8,128)(2,1)} %w_down_rows.1.refs_10_.refs_2_.refs_1_), channel_id=1, source_target_pairs={{0,8},{4,20},{8,0},{12,28},{16,24},{20,4},{24,16},{28,12},{1,9},{5... | collective-permute-start | bytes 3538952 | tf_op jit(solution)/shard_map/ppermute | solution.py:111
  145.4 13.2 %collective-permute-start.31 = (bf16[96,6144]{1,0:T(8,128)(2,1)}, bf16[96,6144]{1,0:T(8,128)(2,1)}, u32[]{:S(2)}, u32[]{:S(2)}) collective-permute-start(bf16[96,6144]{1,0:T(8,128)(2,1)} %w_down_rows.1.refs_10_.refs_2_.refs_1_), channel_id=1, source_target_pairs={{0,4},{4,0},{8,12},{12,8},{16,20},{20,16},{24,28},{28,24},{1,5},{5... | collective-permute-start | bytes 3538952 | tf_op jit(solution)/shard_map/ppermute | solution.py:107
  145.4 16.0 %collective-permute-start.28 = (bf16[96,6144]{1,0:T(8,128)(2,1)S(1)}, bf16[96,6144]{1,0:T(8,128)(2,1)}, u32[]{:S(2)}, u32[]{:S(2)}) collective-permute-start(bf16[96,6144]{1,0:T(8,128)(2,1)S(1)} %copy-done.12), channel_id=1, source_target_pairs={{0,4},{4,0},{8,12},{12,8},{16,20},{20,16},{24,28},{28,24},{1,5},{5... | collective-permute-start | bytes 3538952 | tf_op jit(solution)/shard_map/ppermute | solution.py:107
  158.4 3.1 collective-permute-start.29
  158.5 16.5 %collective-permute-start.32 = (bf16[96,6144]{1,0:T(8,128)(2,1)}, bf16[96,6144]{1,0:T(8,128)(2,1)S(1)}, u32[]{:S(2)}, u32[]{:S(2)}) collective-permute-start(bf16[96,6144]{1,0:T(8,128)(2,1)} %collective-permute-done.31.refs_6_.refs_5_), channel_id=1, source_target_pairs={{0,8},{4,20},{8,0},{12,28},{16,24},{20,4},{24,16},{28,12},{1,9},{5... | collective-permute-start | bytes 3538952 | tf_op jit(solution)/shard_map/ppermute | solution.py:111
  176.6 3.1 collective-permute-start.33
  176.6 20.9 %collective-permute-start.35 = (bf16[96,6144]{1,0:T(8,128)(2,1)}, bf16[96,6144]{1,0:T(8,128)(2,1)S(1)}, u32[]{:S(2)}, u32[]{:S(2)}) collective-permute-start(bf16[96,6144]{1,0:T(8,128)(2,1)} %get-tuple-element.147.refs_3_.refs_2_), channel_id=1, source_target_pairs={{0,4},{4,0},{8,12},{12,8},{16,20},{20,16},{24,28},{28,24},{1,5},{5... | collective-permute-start | bytes 3538952 | tf_op jit(solution)/shard_map/ppermute | solution.py:107
  179.7 16.2 %collective-permute-start.34 = (bf16[96,6144]{1,0:T(8,128)(2,1)S(1)}, bf16[96,6144]{1,0:T(8,128)(2,1)S(1)}, u32[]{:S(2)}, u32[]{:S(2)}) collective-permute-start(bf16[96,6144]{1,0:T(8,128)(2,1)S(1)} %collective-permute-done.33.refs_4_.refs_3_), channel_id=1, source_target_pairs={{0,8},{4,20},{8,0},{12,28},{16,24},{20,4},{24,16},{28,12},{1,9},{5... | collective-permute-start | bytes 3538952 | tf_op jit(solution)/shard_map/ppermute | solution.py:111
  197.5 3.1 collective-permute-start.36
  227.7 19.5 %collective-permute-start.38 = (bf16[384,3072]{1,0:T(8,128)(2,1)}, bf16[384,3072]{1,0:T(8,128)(2,1)}, u32[]{:S(2)}, u32[]{:S(2)}) collective-permute-start(bf16[384,3072]{1,0:T(8,128)(2,1)} %g_down_far.1.refs_11_), channel_id=1, source_target_pairs={{0,4},{4,0},{8,12},{12,8},{16,20},{20,16},{24,28},{28,24},{1,5},{5... | collective-permute-start | bytes 7077896 | tf_op jit(solution)/shard_map/ppermute | solution.py:107
  242.3 11.1 %collective-permute-start.37 = (bf16[384,3072]{1,0:T(8,128)(2,1)}, bf16[384,3072]{1,0:T(8,128)(2,1)}, u32[]{:S(2)}, u32[]{:S(2)}) collective-permute-start(bf16[384,3072]{1,0:T(8,128)(2,1)} %g_up_far.1.refs_3_), channel_id=1, source_target_pairs={{0,4},{4,0},{8,12},{12,8},{16,20},{20,16},{24,28},{28,24},{1,5},{5... | collective-permute-start | bytes 7077896 | tf_op jit(solution)/shard_map/ppermute | solution.py:107
  243.1 58.5 %all-to-all-start = ((bf16[4,192,1536]{2,1,0:T(8,128)(2,1)}), bf16[4,192,1536]{2,1,0:T(8,128)(2,1)S(1)}, u32[]{:S(2)}, u32[]{:S(2)}) async-start(bf16[4,192,1536]{2,1,0:T(8,128)(2,1)} %bitcast.99), calls=%async_computation | async-start | bytes 4718592 | tf_op jit(solution)/shard_map/all_to_all | solution.py:384
  252.7 20.1 %collective-permute-start.40 = (bf16[192,3072]{1,0:T(8,128)(2,1)}, bf16[192,3072]{1,0:T(8,128)(2,1)}, u32[]{:S(2)}, u32[]{:S(2)}) collective-permute-start(bf16[192,3072]{1,0:T(8,128)(2,1)} %get-tuple-element.159), channel_id=1, source_target_pairs={{0,8},{4,20},{8,0},{12,28},{16,24},{20,4},{24,16},{28,12},{1,9},{5... | collective-permute-start | bytes 3538952 | tf_op jit(solution)/shard_map/ppermute | solution.py:111
  258.8 31.3 %collective-permute-start.39 = (bf16[192,3072]{1,0:T(8,128)(2,1)}, bf16[192,3072]{1,0:T(8,128)(2,1)S(1)}, u32[]{:S(2)}, u32[]{:S(2)}) collective-permute-start(bf16[192,3072]{1,0:T(8,128)(2,1)} %get-tuple-element.158), channel_id=1, source_target_pairs={{0,8},{4,20},{8,0},{12,28},{16,24},{20,4},{24,16},{28,12},{1,9},{5... | collective-permute-start | bytes 3538952 | tf_op jit(solution)/shard_map/ppermute | solution.py:111
  275.6 12.3 %collective-permute-start.41 = (bf16[96,3072]{1,0:T(8,128)(2,1)}, bf16[96,3072]{1,0:T(8,128)(2,1)}, u32[]{:S(2)}, u32[]{:S(2)}) collective-permute-start(bf16[96,3072]{1,0:T(8,128)(2,1)} %get-tuple-element.163), channel_id=1, source_target_pairs={{0,16},{4,12},{8,24},{12,4},{16,0},{20,28},{24,8},{28,20},{1,17},{... | collective-permute-start | bytes 1769480 | tf_op jit(solution)/shard_map/ppermute | solution.py:115
  294.0 13.9 %collective-permute-start.42 = (bf16[96,3072]{1,0:T(8,128)(2,1)}, bf16[96,3072]{1,0:T(8,128)(2,1)S(1)}, u32[]{:S(2)}, u32[]{:S(2)}) collective-permute-start(bf16[96,3072]{1,0:T(8,128)(2,1)} %get-tuple-element.169), channel_id=1, source_target_pairs={{0,16},{4,12},{8,24},{12,4},{16,0},{20,28},{24,8},{28,20},{1,17},{... | collective-permute-start | bytes 1769480 | tf_op jit(solution)/shard_map/ppermute | solution.py:115
  295.2 12.7 %collective-permute-start.43 = (bf16[2,96,768]{2,1,0:T(8,128)(2,1)}, bf16[2,96,768]{2,1,0:T(8,128)(2,1)S(1)}, u32[]{:S(2)}, u32[]{:S(2)}) collective-permute-start(bf16[2,96,768]{2,1,0:T(8,128)(2,1)} %bitcast.24), channel_id=1, source_target_pairs={{0,1},{1,0},{2,3},{3,2},{4,5},{5,4},{6,7},{7,6},{8,9},{9,8},{10,11... | collective-permute-start | bytes 884744 | tf_op jit(solution)/shard_map/ppermute | solution.py:107
  301.7 25.2 %collective-permute-start.44 = (bf16[384,2304]{1,0:T(8,128)(2,1)}, bf16[384,2304]{1,0:T(8,128)(2,1)}, u32[]{:S(2)}, u32[]{:S(2)}) collective-permute-start(bf16[384,2304]{1,0:T(8,128)(2,1)} %g_qkv_far.1.refs_5_), channel_id=1, source_target_pairs={{0,4},{4,0},{8,12},{12,8},{16,20},{20,16},{24,28},{28,24},{1,5},{5... | collective-permute-start | bytes 5308424 | tf_op jit(solution)/shard_map/ppermute | solution.py:107
  312.2 14.6 %collective-permute-start.45 = (bf16[1,96,768]{2,1,0:T(8,128)(2,1)S(1)}, bf16[1,96,768]{2,1,0:T(8,128)(2,1)S(1)}, u32[]{:S(2)}, u32[]{:S(2)}) collective-permute-start(bf16[1,96,768]{2,1,0:T(8,128)(2,1)S(1)} %slice.131), channel_id=1, source_target_pairs={{0,2},{1,3},{2,0},{3,1},{4,6},{5,7},{6,4},{7,5},{8,10},{9,11},{10,... | collective-permute-start | bytes 442376 | tf_op jit(solution)/shard_map/ppermute | solution.py:107
  312.3 14.6 %collective-permute-start.46 = (bf16[2,96,768]{2,1,0:T(8,128)(2,1)S(1)}, bf16[2,96,768]{2,1,0:T(8,128)(2,1)S(1)}, u32[]{:S(2)}, u32[]{:S(2)}) collective-permute-start(bf16[2,96,768]{2,1,0:T(8,128)(2,1)S(1)} %bitcast.117), channel_id=1, source_target_pairs={{0,1},{1,0},{2,3},{3,2},{4,5},{5,4},{6,7},{7,6},{8,9},{9,8},{10,11... | collective-permute-start | bytes 884744 | tf_op jit(solution)/shard_map/ppermute | solution.py:107
  323.2 47.0 %all-to-all-start.1 = ((bf16[4,192,768]{2,1,0:T(8,128)(2,1)}), bf16[4,192,768]{2,1,0:T(8,128)(2,1)S(1)}, u32[]{:S(2)}, u32[]{:S(2)}) async-start(bf16[4,192,768]{2,1,0:T(8,128)(2,1)} %bitcast.100), calls=%async_computation.1 | async-start | bytes 2359296 | tf_op jit(solution)/shard_map/all_to_all | solution.py:384
  335.5 2.6 collective-permute-start.48
  335.6 13.3 %collective-permute-start.47 = (bf16[192,2304]{1,0:T(8,128)(2,1)}, bf16[192,2304]{1,0:T(8,128)(2,1)S(1)}, u32[]{:S(2)}, u32[]{:S(2)}) collective-permute-start(bf16[192,2304]{1,0:T(8,128)(2,1)} %get-tuple-element.177), channel_id=1, source_target_pairs={{0,8},{4,20},{8,0},{12,28},{16,24},{20,4},{24,16},{28,12},{1,9},{5... | collective-permute-start | bytes 2654216 | tf_op jit(solution)/shard_map/ppermute | solution.py:111
  341.6 22.7 %collective-permute-start.49 = (bf16[192,1024]{1,0:T(8,128)(2,1)}, bf16[192,1024]{1,0:T(8,128)(2,1)}, u32[]{:S(2)}, u32[]{:S(2)}) collective-permute-start(bf16[192,1024]{1,0:T(8,128)(2,1)} %get-tuple-element.185), channel_id=1, source_target_pairs={{0,8},{4,20},{8,0},{12,28},{16,24},{20,4},{24,16},{28,12},{1,9},{5... | collective-permute-start | bytes 1179656 | tf_op jit(solution)/shard_map/ppermute | solution.py:111
  352.2 9.1 %collective-permute-start.50 = (bf16[96,2304]{1,0:T(8,128)(2,1)}, bf16[96,2304]{1,0:T(8,128)(2,1)S(1)}, u32[]{:S(2)}, u32[]{:S(2)}) collective-permute-start(bf16[96,2304]{1,0:T(8,128)(2,1)} %get-tuple-element.186), channel_id=1, source_target_pairs={{0,16},{4,12},{8,24},{12,4},{16,0},{20,28},{24,8},{28,20},{1,17},{... | collective-permute-start | bytes 1327112 | tf_op jit(solution)/shard_map/ppermute | solution.py:115
  353.8 15.4 %collective-permute-start.56 = (bf16[1,96,768]{2,1,0:T(8,128)(2,1)}, bf16[1,96,768]{2,1,0:T(8,128)(2,1)S(1)}, u32[]{:S(2)}, u32[]{:S(2)}) collective-permute-start(bf16[1,96,768]{2,1,0:T(8,128)(2,1)} %slice.138), channel_id=1, source_target_pairs={{0,2},{1,3},{2,0},{3,1},{4,6},{5,7},{6,4},{7,5},{8,10},{9,11},{10,... | collective-permute-start | bytes 442376 | tf_op jit(solution)/shard_map/ppermute | solution.py:107
  366.2 8.6 %collective-permute-start.53 = (bf16[96,1024]{1,0:T(8,128)(2,1)}, bf16[96,1024]{1,0:T(8,128)(2,1)S(1)}, u32[]{:S(2)}, u32[]{:S(2)}) collective-permute-start(bf16[96,1024]{1,0:T(8,128)(2,1)} %get-tuple-element.190), channel_id=1, source_target_pairs={{0,16},{4,12},{8,24},{12,4},{16,0},{20,28},{24,8},{28,20},{1,17},{... | collective-permute-start | bytes 589832 | tf_op jit(solution)/shard_map/ppermute | solution.py:115
  367.7 12.2 %collective-permute-start.51 = (bf16[2,96,576]{1,2,0:T(8,128)(2,1)S(1)}, bf16[2,96,576]{1,2,0:T(8,128)(2,1)S(1)}, u32[]{:S(2)}, u32[]{:S(2)}) collective-permute-start(bf16[2,96,576]{1,2,0:T(8,128)(2,1)S(1)} %copy.70), channel_id=1, source_target_pairs={{0,1},{1,0},{2,3},{3,2},{4,5},{5,4},{6,7},{7,6},{8,9},{9,8},{10,11... | collective-permute-start | bytes 663560 | tf_op jit(solution)/shard_map/ppermute | solution.py:107
  378.2 6.8 %collective-permute-start.54 = (bf16[2,96,256]{1,2,0:T(8,128)(2,1)S(1)}, bf16[2,96,256]{1,2,0:T(8,128)(2,1)S(1)}, u32[]{:S(2)}, u32[]{:S(2)}) collective-permute-start(bf16[2,96,256]{1,2,0:T(8,128)(2,1)S(1)} %bitcast.113), channel_id=1, source_target_pairs={{0,1},{1,0},{2,3},{3,2},{4,5},{5,4},{6,7},{7,6},{8,9},{9,8},{10,11... | collective-permute-start | bytes 294920 | tf_op jit(solution)/shard_map/ppermute | solution.py:107
  379.9 10.2 %collective-permute-start.52 = (bf16[1,96,576]{1,2,0:T(8,128)(2,1)S(1)}, bf16[1,96,576]{1,2,0:T(8,128)(2,1)S(1)}, u32[]{:S(2)}, u32[]{:S(2)}) collective-permute-start(bf16[1,96,576]{1,2,0:T(8,128)(2,1)S(1)} %slice.133), channel_id=1, source_target_pairs={{0,2},{1,3},{2,0},{3,1},{4,6},{5,7},{6,4},{7,5},{8,10},{9,11},{10,... | collective-permute-start | bytes 331784 | tf_op jit(solution)/shard_map/ppermute | solution.py:107
  385.0 6.1 %collective-permute-start.55 = (bf16[1,96,256]{1,2,0:T(8,128)(2,1)S(1)}, bf16[1,96,256]{1,2,0:T(8,128)(2,1)S(1)}, u32[]{:S(2)}, u32[]{:S(2)}) collective-permute-start(bf16[1,96,256]{1,2,0:T(8,128)(2,1)S(1)} %slice.135), channel_id=1, source_target_pairs={{0,2},{1,3},{2,0},{3,1},{4,6},{5,7},{6,4},{7,5},{8,10},{9,11},{10,... | collective-permute-start | bytes 147464 | tf_op jit(solution)/shard_map/ppermute | solution.py:107
  (66 other events, 255.2 us)
Sparse Core Ops, SparseCore 0:
  64.7 28.8 all-gather.2
  95.7 29.3 all-gather.4

commit v3 on v2

--- a/solution.py
+++ b/solution.py
@@ -175,16 +175,22 @@
     return join_columns(run, name, [left, right], [(0, 0, 0, n), (1, 0, n, n)], 2 * n)
 
 
-def rows_side_by_side(run, name, value, rows):
-    total, n = value.shape
-    count = total // rows
-
-    def kernel(ref, out):
-        for k in range(count):
-            out[:, k * n : (k + 1) * n] = ref[k * rows : (k + 1) * rows]
+def rows_in_order(run, name, near, far):
+    rows, wide = near.shape
+    n = wide // 2
+    places = lax.axis_index(TENSOR) ^ jnp.array([0, 2, 1, 3], jnp.int32)
+
+    def kernel(where, near_ref, far_ref, out):
+        for k in range(4):
+            ref = near_ref if k < 2 else far_ref
+            start = pl.multiple_of(where[k] * n, 128)
+            out[:, pl.ds(start, n)] = ref[:, (k % 2) * n : (k % 2 + 1) * n]
 
     return run.call(
-        name, kernel, [(value, whole(total, n))], [((rows, count * n), LOW, whole(rows, count * n))], moved=4 * total * n
+        name,
+        kernel,
+        [(places, SCALARS), (near, whole(rows, wide)), (far, whole(rows, wide))],
+        [((rows, 2 * wide), LOW, whole(rows, 2 * wide))],
     )[0]
 
 
@@ -192,8 +198,10 @@
     value = shard()
     run.shards.append(value)
     if finish is None:
-        (got,) = yield [lax.all_gather(value, TENSOR, axis=0, tiled=True)]
-        mine = rows_side_by_side(run, name + "_rows", got, value.shape[0])
+        (got,) = yield [swap(value, TENSOR, 2)]
+        value = side_by_side(run, name + "_join", value, got)
+        (got,) = yield [swap(value, TENSOR, 1)]
+        mine = rows_in_order(run, name + "_rows", value, got)
     else:
         (got,) = yield [swap(value, TENSOR, 2)]
         value = side_by_side(run, name + "_join", value, got)
@@ -1116,6 +1124,7 @@
     go_on(small)
     run.land(small)
     prepare_slots()
+    go_on(c)
     go_on(small)
     run.land(small)
     go_on(ta)
@@ -1131,7 +1140,6 @@
     go_on(c)
     run.land(ta)
     go_on(sa)
-    go_on(d)
     go_on(small)
     go_on(ta)
     run.land(ta, only=1)
@@ -1141,9 +1149,11 @@
     go_on(sa)
     run.land(sa)
     run.land(small)
+    run.land(c)
     run.fence()
     go_on(small)
     go_on(sa)
+    go_on(d)
     run.land(sa, only=1)
     run.land(small)
     run.fence()
@@ -1153,6 +1163,7 @@
     go_on(c)
     go_on(c)
     project_teacher()
+    go_on(d)
     finish(sa)
     project_student()
     attend(0)
@@ -1200,11 +1211,11 @@
     back_entry()
     g_leave = Task(leave_columns(run, "arrive_grad", have.g_leave, WIDE, 1, keep("input_grad")))
     go_on(g_leave)
+    out = share_out()
+    go_on(out)
     run.land(down, up)
     go_on(qkv)
     go_on(up)
-    out = share_out()
-    go_on(out)
     go_on(out)
     go_on(qkv)
     finish(leaving)

time: 406 us -> 403 us (level)
  between operations: 15 us -> 1.62 us
  starting transfers between devices: 55.9 us -> 66.1 us
  waiting for transfers between devices: 69.8 us -> 64.7 us
    ppermute x37 -> x41, starting transfers between devices: 27.7 us -> 35 us  [swap(): return lax.ppermute(value, axis, [(i, i ^ bit) for i in range(size)])]
    ppermute x16, waiting for transfers between devices: 28.3 us -> 23.5 us  [swap_first(): lax.ppermute(value, FSDP, [(i, i ^ (4 if i % 2 else 2)) for i in range(8)])]
    pallas_call x49 -> x51, Pallas kernels: 217 us -> 221 us  [call(): pl.pallas_call(wrapped, grid=grid, in_specs=[spec for _, spec in ins] + [...]
    ppermute x37 -> x41, waiting for transfers between devices: 40.9 us -> 41.2 us  [swap(): return lax.ppermute(value, axis, [(i, i ^ bit) for i in range(size)])]
    unnamed x143 -> x159, local copies, waits for them, and re-layouts: 25.6 us -> 25.5 us
  transfers between devices with their start and end apart: 61 -> 63, of which waited for: 23 -> 23; matrix products, arithmetic and copies ran while one was open for 4% -> 4% of each run, Pallas kernels for 47% -> 48%
where the time goes in v3:
time: 403 us; the launch traced here: 396 us
  Pallas kernels  221 us (55%)
  starting transfers between devices  66.1 us (16%)
  waiting for transfers between devices  64.7 us (16%)
  local copies, waits for them, and re-layouts  32 us (8%)
  other arithmetic  10.4 us (3%)
    pallas_call x51, Pallas kernels, call(): pl.pallas_call(wrapped, grid=grid, in_specs=[spec for _, spec in ins] + [...  221 us
    ppermute x41, waiting for transfers between devices, swap(): return lax.ppermute(value, axis, [(i, i ^ bit) for i in range(size)])  41.2 us
    ppermute x41, starting transfers between devices, swap(): return lax.ppermute(value, axis, [(i, i ^ bit) for i in range(size)])  35 us
    unnamed x159, local copies, waits for them, and re-layouts  25.5 us
    ppermute x16, waiting for transfers between devices, swap_first(): lax.ppermute(value, FSDP, [(i, i ^ (4 if i % 2 else 2)) for i in range(8)])  23.5 us
    ppermute x16, starting transfers between devices, swap_first(): lax.ppermute(value, FSDP, [(i, i ^ (4 if i % 2 else 2)) for i in range(8)])  19.4 us
  transfers between devices with their start and end apart: 63, of which 23 were waited for; matrix products, arithmetic and copies ran while one was open for 4% of the time, Pallas kernels for 48%

profile of v3, /device:TPU:0, one launch (start us, length us, event | category | flops | bytes accessed | tf_op | source)
XLA Modules:
  0.0 396.1 jit_solution(13283819836675989342)
XLA Ops:
  3.0 4.1 %collective-permute-start.1 = (bf16[96,768]{1,0:T(8,128)(2,1)S(1)}, bf16[96,768]{1,0:T(8,128)(2,1)S(1)}, u32[]{:S(2)}, u32[]{:S(2)}) collective-permute-start(bf16[96,768]{1,0:T(8,128)(2,1)S(1)} %pad_maximum_fusion.refs_4_.refs_0_), channel_id=1, source_target_pairs={{0,2},{1,3},{2,0},{3,1},{4,6},{5,7},{6,4},{7,5},{8,10},{9,11},{10,... | collective-permute-start | bytes 442376 | tf_op jit(solution)/shard_map/ppermute | solution.py:107
  8.1 2.1 magnitudes.1.refs_4_
  15.1 1.7 slots.1
  19.6 1.8 pack_up.1.refs_3_.refs_0_
  22.7 1.7 w_tqkv_join.1
  27.3 5.8 %place_rows.1 = (bf16[768,768]{1,0:T(8,128)(2,1)}, bf16[768,768]{1,0:T(8,128)(2,1)}, bf16[768,768]{1,0:T(8,128)(2,1)}, bf16[768,768]{1,0:T(8,128)(2,1)}) custom-call(s32[9]{0:T(128)} %pad_add_fusion.refs_0_, bf16[3072,768]{1,0:T(8,128)(2,1)} %refs_1_.7, bf16[3072,768]{1,0:T(8,128)(2,1)} %refs_2_.5, bf16[96,1536]{1,0:T(8,128)(2,1)} %get-tuple-element.106.refs_3_.refs_0_), custom_call_target="tpu_custom_call" | custom-call | tf_op jit(solution)/shard_map/place_rows/pallas_call | solution.py:80
  33.8 1.7 w_qkv_join.1
  36.2 2.1 w_tqkv_rows.1.refs_1_
  43.6 2.6 collective-permute-start.5
  46.6 13.1 %collective-permute-done.5.refs_1_ = bf16[96,1536]{1,0:T(8,128)(2,1)S(1)} collective-permute-done((bf16[96,1536]{1,0:T(8,128)(2,1)S(1)}, bf16[96,1536]{1,0:T(8,128)(2,1)S(1)}, u32[]{:S(2)}, u32[]{:S(2)}) %collective-permute-start.5) | collective-permute-done | bytes 294944 | tf_op jit(solution)/shard_map/ppermute | solution.py:107
  60.9 1.9 w_up_join.1
  63.9 2.1 w_qkv_rows.1
  74.4 7.5 %collective-permute-done.15.refs_2_ = f32[8,128]{1,0:T(8,128)S(1)} collective-permute-done((f32[8,128]{1,0:T(8,128)S(1)}, f32[8,128]{1,0:T(8,128)S(1)}, u32[]{:S(2)}, u32[]{:S(2)}) %collective-permute-start.15) | collective-permute-done | bytes 4128 | tf_op jit(solution)/shard_map/ppermute | solution.py:107
  87.0 1.8 pack_down.1.refs_2_.refs_0_
  95.4 2.4 w_up_rows.1.refs_9_.refs_1_
  98.8 3.4 collective-permute-done.19.refs_4_.refs_17_
  102.2 7.2 %project_teacher.1.refs_2_.refs_5_.refs_6_.refs_7_ = bf16[768,2304]{1,0:T(8,128)(2,1)} custom-call(bf16[768,768]{1,0:T(8,128)(2,1)} %get-tuple-element.126.refs_0_.refs_9_, bf16[96,3072]{1,0:T(8,128)(2,1)} %w_tqkv_rows.1.refs_1_, bf16[96,3072]{1,0:T(8,128)(2,1)} %get-tuple-element.127.refs_2_, bf16[96,3072]{1,0:T(8,128)(2,1)} %get-tuple-element.128.refs_3_, ...), custom_call_target="tpu_custom_call" | custom-call | flops 13589544960 | bytes 41287680 | tf_op jit(solution)/shard_map/project_teacher/pallas_call | solution.py:80
  110.9 1.9 w_down_join.1.refs_10_.refs_1_
  115.8 7.0 %project_student.1.refs_2_.refs_3_.refs_4_.refs_8_.refs_1_ = bf16[768,2304]{1,0:T(8,128)(2,1)} custom-call(bf16[768,768]{1,0:T(8,128)(2,1)} %get-tuple-element.107.refs_0_, bf16[96,3072]{1,0:T(8,128)(2,1)} %get-tuple-element.115.refs_2_.refs_1_.refs_14_, bf16[96,3072]{1,0:T(8,128)(2,1)} %get-tuple-element.120.refs_2_.refs_15_, ...), custom_call_target="tpu_custom_call" | custom-call | flops 13589544960 | bytes 41287680 | tf_op jit(solution)/shard_map/project_student/pallas_call | solution.py:80
  122.8 8.5 %attend_forward.2 = (bf16[768,768]{1,0:T(8,128)(2,1)}, bf16[768,768]{1,0:T(8,128)(2,1)}, bf16[3,6,256,512]{3,2,1,0:T(8,128)(2,1)}, bf16[3,6,256,512]{3,2,1,0:T(8,128)(2,1)}) custom-call(s32[8,768]{1,0:T(8,128)} %get-tuple-element.103.refs_2_.refs_0_, s32[768,128]{1,0:T(8,128)} %get-tuple-element.104.refs_1_, ...), custom_call_target="tpu_custom_call" | custom-call | flops 12079595520 | bytes 35389440 | tf_op jit(solution)/shard_map/attend_forward/pallas_call | solution.py:80
  137.7 8.5 %attend_forward.3 = (bf16[768,768]{1,0:T(8,128)(2,1)}, bf16[768,768]{1,0:T(8,128)(2,1)}, bf16[3,6,256,512]{3,2,1,0:T(8,128)(2,1)}, bf16[3,6,256,512]{3,2,1,0:T(8,128)(2,1)}) custom-call(s32[8,768]{1,0:T(8,128)} %get-tuple-element.103.refs_2_.refs_0_, ...), custom_call_target="tpu_custom_call", output_to_operand_aliasing={{0}: (8, {}), {1}: (9, {}), {2}: (10, {}), {3}: (11, {})} | custom-call | flops 12079595520 | bytes 35389440 | tf_op jit(solution)/shard_map/attend_forward/pallas_call | solution.py:80
  146.2 2.4 w_down_rows.1.refs_10_.refs_2_.refs_1_
  150.0 5.5 %close_teacher.1 = (f32[768,768]{1,0:T(8,128)}, bf16[768,768]{1,0:T(8,128)(2,1)}) custom-call(bf16[768,768]{1,0:T(8,128)(2,1)} %get-tuple-element.138.refs_0_, bf16[96,3072]{1,0:T(8,128)(2,1)} %w_tqkv_rows.1.refs_1_, bf16[96,3072]{1,0:T(8,128)(2,1)} %get-tuple-element.127.refs_2_, bf16[96,3072]{1,0:T(8,128)(2,1)} %get-tuple-element.128.refs_3_, ...), custom_call_target="tpu_custom_call" | custom-call | flops 4529848320 | bytes 11796480 | tf_op jit(solution)/shard_map/close_teacher/pallas_call | solution.py:80
  156.6 6.0 %close_student.1 = (f32[768,768]{1,0:T(8,128)}, f32[768,128]{1,0:T(8,128)}, bf16[768,768]{1,0:T(8,128)(2,1)}, bf16[96,6144]{1,0:T(8,128)(2,1)}) custom-call(bf16[768,768]{1,0:T(8,128)(2,1)} %get-tuple-element.136.refs_3_.refs_0_.refs_1_, bf16[96,3072]{1,0:T(8,128)(2,1)} %get-tuple-element.115.refs_2_.refs_1_.refs_14_, ...), custom_call_target="tpu_custom_call", output_to_operand_aliasing={{3}: (12, {})} | custom-call | flops 4529848320 | bytes 11796480 | tf_op jit(solution)/shard_map/close_student/pallas_call | solution.py:80
  166.8 8.3 %up_teacher.1 = (bf16[768,3072]{1,0:T(8,128)(2,1)}, bf16[96,6144]{1,0:T(8,128)(2,1)}) custom-call(bf16[768,768]{1,0:T(8,128)(2,1)} %get-tuple-element.142.refs_0_, bf16[96,6144]{1,0:T(8,128)(2,1)} %w_up_rows.1.refs_9_.refs_1_, bf16[96,6144]{1,0:T(8,128)(2,1)} %get-tuple-element.143.refs_2_, ...), custom_call_target="tpu_custom_call", output_to_operand_aliasing={{1}: (9, {})} | custom-call | flops 18119393280 | bytes 53084160 | tf_op jit(solution)/shard_map/up_teacher/pallas_call | solution.py:80
  175.1 4.1 %collective-permute-done.36.refs_0_ = bf16[96,6144]{1,0:T(8,128)(2,1)S(1)} collective-permute-done((bf16[96,6144]{1,0:T(8,128)(2,1)}, bf16[96,6144]{1,0:T(8,128)(2,1)S(1)}, u32[]{:S(2)}, u32[]{:S(2)}) %collective-permute-start.36) | collective-permute-done | bytes 1179680 | tf_op jit(solution)/shard_map/ppermute | solution.py:111
  181.4 2.5 collective-permute-done.37.refs_4_.refs_3_
  185.1 10.4 %up_student.1 = (bf16[768,3072]{1,0:T(8,128)(2,1)}, bf16[768,3072]{1,0:T(8,128)(2,1)}) custom-call(bf16[768,768]{1,0:T(8,128)(2,1)} %get-tuple-element.141.refs_0_, bf16[96,6144]{1,0:T(8,128)(2,1)} %w_up_rows.1.refs_9_.refs_1_, bf16[96,6144]{1,0:T(8,128)(2,1)} %get-tuple-element.143.refs_2_, bf16[96,6144]{1,0:T(8,128)(2,1)} %copy-done.66, ...), custom_call_target="tpu_custom_call" | custom-call | flops 18119393280 | bytes 76677120 | tf_op jit(solution)/shard_map/up_student/pallas_call | solution.py:80
  195.4 4.7 %collective-permute-done.38.refs_0_ = bf16[96,6144]{1,0:T(8,128)(2,1)S(1)} collective-permute-done((bf16[96,6144]{1,0:T(8,128)(2,1)S(1)}, bf16[96,6144]{1,0:T(8,128)(2,1)S(1)}, u32[]{:S(2)}, u32[]{:S(2)}) %collective-permute-start.38) | collective-permute-done | bytes 1179680 | tf_op jit(solution)/shard_map/ppermute | solution.py:111
  201.7 3.0 collective-permute-done.40.refs_9_.refs_8_
  205.8 21.1 %down_both.1 = (f32[768,768]{1,0:T(8,128)}, bf16[768,768]{1,0:T(8,128)(2,1)}, f32[8,768]{1,0:T(8,128)}, bf16[768,1536]{1,0:T(8,128)(2,1)}) custom-call(bf16[768,3072]{1,0:T(8,128)(2,1)} %get-tuple-element.146.refs_1_.refs_0_, bf16[768,3072]{1,0:T(8,128)(2,1)} %get-tuple-element.148.refs_1_, bf16[96,6144]{1,0:T(8,128)(2,1)} %w_down_rows.1.refs_10_.refs_2_.refs_1_, ...), custom_call_target="tpu_custom_call" | custom-call | flops 36238786560 | bytes 94371840 | tf_op jit(solution)/shard_map/down_both/pallas_call | solution.py:80
  226.9 5.0 %g_down_far.1.refs_11_ = bf16[384,3072]{1,0:T(8,128)(2,1)} custom-call(bf16[768,768]{1,0:T(8,128)(2,1)} %get-tuple-element.155.refs_0_, bf16[768,3072]{1,0:T(8,128)(2,1)} %get-tuple-element.148.refs_1_, f32[768,768]{1,0:T(8,128)} %get-tuple-element.157.refs_2_.refs_11_), custom_call_target="tpu_custom_call" | custom-call | flops 9059696640 | bytes 47185920 | tf_op jit(solution)/shard_map/g_down_far/pallas_call | solution.py:80
  232.1 9.2 %back_down.1.refs_1_.refs_2_.refs_0_ = bf16[768,3072]{1,0:T(8,128)(2,1)} custom-call(bf16[768,768]{1,0:T(8,128)(2,1)} %get-tuple-element.155.refs_0_, bf16[96,6144]{1,0:T(8,128)(2,1)} %w_down_rows.1.refs_10_.refs_2_.refs_1_, bf16[96,6144]{1,0:T(8,128)(2,1)} %get-tuple-element.149.refs_3_.refs_2_, bf16[96,6144]{1,0:T(8,128)(2,1)} %copy-done.68, ...), custom_call_target="tpu_custom_call" | custom-call | flops 18119393280 | bytes 53084160 | tf_op jit(solution)/shard_map/back_down/pallas_call | solution.py:80
  241.3 5.1 %g_up_far.1.refs_3_ = bf16[384,3072]{1,0:T(8,128)(2,1)} custom-call(bf16[768,768]{1,0:T(8,128)(2,1)} %get-tuple-element.141.refs_0_, bf16[768,3072]{1,0:T(8,128)(2,1)} %back_down.1.refs_1_.refs_2_.refs_0_, bf16[768,3072]{1,0:T(8,128)(2,1)} %back_down.1.refs_1_.refs_2_.refs_0_), custom_call_target="tpu_custom_call" | custom-call | flops 9059696640 | bytes 47185920 | tf_op jit(solution)/shard_map/g_up_far/pallas_call | solution.py:80
  247.4 4.0 %all-to-all-start = ((bf16[4,192,1536]{2,1,0:T(8,128)(2,1)}), bf16[4,192,1536]{2,1,0:T(8,128)(2,1)S(1)}, u32[]{:S(2)}, u32[]{:S(2)}) async-start(bf16[4,192,1536]{2,1,0:T(8,128)(2,1)} %bitcast.99), calls=%async_computation | async-start | bytes 4718592 | tf_op jit(solution)/shard_map/all_to_all | solution.py:392
  251.4 5.5 %g_down_near.1 = (bf16[192,3072]{1,0:T(8,128)(2,1)}, bf16[192,3072]{1,0:T(8,128)(2,1)}) custom-call(bf16[768,768]{1,0:T(8,128)(2,1)} %get-tuple-element.155.refs_0_, bf16[768,3072]{1,0:T(8,128)(2,1)} %get-tuple-element.148.refs_1_, bf16[384,3072]{1,0:T(8,128)(2,1)} %collective-permute-done.42.refs_2_, bf16[384,3072]{1,0:T(8,128)(2,1)} %g_up_far.1.refs_3_), custom_call_target="tpu_custom_call" | custom-call | flops 9059696640 | bytes 47185920 | tf_op jit(solution)/shard_map/g_down_near/pallas_call | solution.py:80
  258.0 5.4 %g_up_near.1 = (bf16[192,3072]{1,0:T(8,128)(2,1)}, bf16[192,3072]{1,0:T(8,128)(2,1)}) custom-call(bf16[768,768]{1,0:T(8,128)(2,1)} %get-tuple-element.141.refs_0_, bf16[768,3072]{1,0:T(8,128)(2,1)} %back_down.1.refs_1_.refs_2_.refs_0_, bf16[384,3072]{1,0:T(8,128)(2,1)} %collective-permute-done.41.refs_2_, bf16[192,3072]{1,0:T(8,128)(2,1)} %get-tuple-element.158.refs_3_.refs_0_), custom_call_target="tpu_custom_call" | custom-call | flops 9059696640 | bytes 47185920 | tf_op jit(solution)/shard_map/g_up_near/pallas_call | solution.py:80
  264.3 12.6 %back_up.1 = (f32[768,768]{1,0:T(8,128)}, bf16[768,768]{1,0:T(8,128)(2,1)}, bf16[768,768]{1,0:T(8,128)(2,1)}, f32[8,768]{1,0:T(8,128)}) custom-call(bf16[768,3072]{1,0:T(8,128)(2,1)} %back_down.1.refs_1_.refs_2_.refs_0_, bf16[96,6144]{1,0:T(8,128)(2,1)} %w_up_rows.1.refs_9_.refs_1_, bf16[96,6144]{1,0:T(8,128)(2,1)} %get-tuple-element.143.refs_2_, ...), custom_call_target="tpu_custom_call" | custom-call | flops 18119393280 | bytes 47185920 | tf_op jit(solution)/shard_map/back_up/pallas_call | solution.py:80
  277.0 2.8 g_down_add2.1
  281.3 11.5 %attend_backward.1.refs_3_.refs_1_.refs_0_ = bf16[768,2304]{1,0:T(8,128)(2,1)} custom-call(f32[4]{0:T(128)} %multiply_bitcast_fusion.refs_9_.refs_10_.refs_0_, bf16[768,2304]{1,0:T(8,128)(2,1)} %project_student.1.refs_2_.refs_3_.refs_4_.refs_8_.refs_1_, bf16[768,768]{1,0:T(8,128)(2,1)} %get-tuple-element.166.refs_2_, ...), custom_call_target="tpu_custom_call" | custom-call | flops 12079595520 | bytes 70778880 | tf_op jit(solution)/shard_map/attend_backward/pallas_call | solution.py:80
  292.8 2.3 g_down_add3.1
  296.1 2.8 g_up_add2.1
  299.4 2.0 collective-permute-start.47
  301.4 4.5 %g_qkv_far.1.refs_5_ = bf16[384,2304]{1,0:T(8,128)(2,1)} custom-call(bf16[768,768]{1,0:T(8,128)(2,1)} %get-tuple-element.107.refs_0_, bf16[768,2304]{1,0:T(8,128)(2,1)} %attend_backward.1.refs_3_.refs_1_.refs_0_, bf16[96,3072]{1,0:T(8,128)(2,1)} %get-tuple-element.170.refs_2_.refs_1_), custom_call_target="tpu_custom_call" | custom-call | flops 6794772480 | bytes 35389440 | tf_op jit(solution)/shard_map/g_qkv_far/pallas_call | solution.py:80
  306.0 6.1 %collective-permute-done.47.refs_3_ = bf16[2,96,768]{2,1,0:T(8,128)(2,1)S(1)} collective-permute-done((bf16[2,96,768]{2,1,0:T(8,128)(2,1)}, bf16[2,96,768]{2,1,0:T(8,128)(2,1)S(1)}, u32[]{:S(2)}, u32[]{:S(2)}) %collective-permute-start.47) | collective-permute-done | bytes 294944 | tf_op jit(solution)/shard_map/ppermute | solution.py:107
  313.0 2.3 g_up_add3.1
  316.5 2.0 collective-permute-start.50
  318.5 8.9 %back_entry.1.refs_4_ = bf16[768,768]{1,0:T(8,128)(2,1)} custom-call(bf16[768,2304]{1,0:T(8,128)(2,1)} %attend_backward.1.refs_3_.refs_1_.refs_0_, bf16[96,3072]{1,0:T(8,128)(2,1)} %get-tuple-element.115.refs_2_.refs_1_.refs_14_, bf16[96,3072]{1,0:T(8,128)(2,1)} %get-tuple-element.120.refs_2_.refs_15_, bf16[96,3072]{1,0:T(8,128)(2,1)} %get-tuple-element.124.refs_3_.refs_16_, ...), custom_call_target="tpu_custom_call" | custom-call | flops 13589544960 | bytes 35389440 | tf_op jit(solution)/shard_map/back_entry/pallas_call | solution.py:80
  327.4 3.2 g_out_far.1.refs_5_
  330.7 3.6 all-to-all-start.1
  335.1 4.7 %g_qkv_near.1 = (bf16[192,2304]{1,0:T(8,128)(2,1)}, bf16[192,2304]{1,0:T(8,128)(2,1)}, bf16[1,96,768]{2,1,0:T(8,128)(2,1)}, bf16[2,96,768]{2,1,0:T(8,128)(2,1)}) custom-call(bf16[768,768]{1,0:T(8,128)(2,1)} %get-tuple-element.107.refs_0_, bf16[768,2304]{1,0:T(8,128)(2,1)} %attend_backward.1.refs_3_.refs_1_.refs_0_, ...), custom_call_target="tpu_custom_call", output_to_operand_aliasing={{2}: (3, {}), {3}: (4, {})} | custom-call | flops 6794772480 | bytes 35389440 | tf_op jit(solution)/shard_map/g_qkv_near/pallas_call | solution.py:80
  341.1 3.4 g_out_near.1
  345.4 7.6 %collective-permute-done.51.refs_1_ = bf16[192,2304]{1,0:T(8,128)(2,1)S(1)} collective-permute-done((bf16[192,2304]{1,0:T(8,128)(2,1)}, bf16[192,2304]{1,0:T(8,128)(2,1)S(1)}, u32[]{:S(2)}, u32[]{:S(2)}) %collective-permute-start.51) | collective-permute-done | bytes 884768 | tf_op jit(solution)/shard_map/ppermute | solution.py:111
  354.0 2.5 g_qkv_add2.1
  358.7 2.9 collective-permute-start.60
  362.4 3.9 arrive.1
  367.1 2.1 g_qkv_add3.1
  369.2 2.0 g_out_add2.1
  371.9 1.7 collective-permute-start.55
  375.6 3.6 arrive_grad.1.refs_2_
  380.0 1.7 g_out_add3.1
  384.2 2.6 collective-permute-start.56
  388.0 2.9 collective-permute-start.59
  390.9 2.4 collective-permute-done.56
  (318 shorter events, 94.3 us)
Async XLA Ops:
  3.0 18.4 %collective-permute-start.1 = (bf16[96,768]{1,0:T(8,128)(2,1)S(1)}, bf16[96,768]{1,0:T(8,128)(2,1)S(1)}, u32[]{:S(2)}, u32[]{:S(2)}) collective-permute-start(bf16[96,768]{1,0:T(8,128)(2,1)S(1)} %pad_maximum_fusion.refs_4_.refs_0_), channel_id=1, source_target_pairs={{0,2},{1,3},{2,0},{3,1},{4,6},{5,7},{6,4},{7,5},{8,10},{9,11},{10,... | collective-permute-start | bytes 442376 | tf_op jit(solution)/shard_map/ppermute | solution.py:107
  10.9 3.7 collective-permute-start
  17.6 3.8 collective-permute-start.2
  19.2 14.0 %collective-permute-start.3 = (bf16[96,768]{1,0:T(8,128)(2,1)S(1)}, bf16[96,768]{1,0:T(8,128)(2,1)S(1)}, u32[]{:S(2)}, u32[]{:S(2)}) collective-permute-start(bf16[96,768]{1,0:T(8,128)(2,1)S(1)} %pad_maximum_fusion.1.refs_0_), channel_id=1, source_target_pairs={{0,2},{1,3},{2,0},{3,1},{4,6},{5,7},{6,4},{7,5},{8,10},{9,11},{10,... | collective-permute-start | bytes 442376 | tf_op jit(solution)/shard_map/ppermute | solution.py:107
  24.4 11.2 %collective-permute-start.7 = (bf16[96,1536]{1,0:T(8,128)(2,1)}, bf16[96,1536]{1,0:T(8,128)(2,1)S(1)}, u32[]{:S(2)}, u32[]{:S(2)}) collective-permute-start(bf16[96,1536]{1,0:T(8,128)(2,1)} %get-tuple-element.106.refs_3_.refs_0_), channel_id=1, source_target_pairs={{0,1},{1,0},{2,3},{3,2},{4,5},{5,4},{6,7},{7,6},{8,9},{9,8},{10,11... | collective-permute-start | bytes 884744 | tf_op jit(solution)/shard_map/ppermute | solution.py:107
  26.7 6.5 %collective-permute-start.4 = (f32[4,16,128]{2,1,0:T(8,128)S(1)}, f32[4,16,128]{2,1,0:T(8,128)S(1)}, u32[]{:S(2)}, u32[]{:S(2)}) collective-permute-start(f32[4,16,128]{2,1,0:T(8,128)S(1)} %pad_maximum_fusion.2), channel_id=1, source_target_pairs={{0,4},{4,0},{8,12},{12,8},{16,20},{20,16},{24,28},{28,24},{1,5},{5... | collective-permute-start | bytes 98312 | tf_op jit(solution)/shard_map/ppermute | solution.py:107
  38.4 2.3 collective-permute-start.8
  38.9 24.0 %collective-permute-start.9 = (bf16[96,3072]{1,0:T(8,128)(2,1)}, bf16[96,3072]{1,0:T(8,128)(2,1)S(1)}, u32[]{:S(2)}, u32[]{:S(2)}) collective-permute-start(bf16[96,3072]{1,0:T(8,128)(2,1)} %w_tqkv_rows.1.refs_1_), channel_id=1, source_target_pairs={{0,8},{4,20},{8,0},{12,28},{16,24},{20,4},{24,16},{28,12},{1,9},{5... | collective-permute-start | bytes 1769480 | tf_op jit(solution)/shard_map/ppermute | solution.py:111
  42.1 20.7 %collective-permute-start.10 = (bf16[96,3072]{1,0:T(8,128)(2,1)}, bf16[96,3072]{1,0:T(8,128)(2,1)S(1)}, u32[]{:S(2)}, u32[]{:S(2)}) collective-permute-start(bf16[96,3072]{1,0:T(8,128)(2,1)} %get-tuple-element.113.refs_5_), channel_id=1, source_target_pairs={{0,8},{4,20},{8,0},{12,28},{16,24},{20,4},{24,16},{28,12},{1,9},{5... | collective-permute-start | bytes 1769480 | tf_op jit(solution)/shard_map/ppermute | solution.py:111
  43.6 16.1 %collective-permute-start.5 = (bf16[96,1536]{1,0:T(8,128)(2,1)S(1)}, bf16[96,1536]{1,0:T(8,128)(2,1)S(1)}, u32[]{:S(2)}, u32[]{:S(2)}) collective-permute-start(bf16[96,1536]{1,0:T(8,128)(2,1)S(1)} %copy-done.2), channel_id=1, source_target_pairs={{0,2},{1,3},{2,0},{3,1},{4,6},{5,7},{6,4},{7,5},{8,10},{9,11},{10,... | collective-permute-start | bytes 884744 | tf_op jit(solution)/shard_map/ppermute | solution.py:107
  46.2 14.0 %collective-permute-start.6 = (bf16[96,1536]{1,0:T(8,128)(2,1)S(1)}, bf16[96,1536]{1,0:T(8,128)(2,1)S(1)}, u32[]{:S(2)}, u32[]{:S(2)}) collective-permute-start(bf16[96,1536]{1,0:T(8,128)(2,1)S(1)} %copy-done.14), channel_id=1, source_target_pairs={{0,1},{1,0},{2,3},{3,2},{4,5},{5,4},{6,7},{7,6},{8,9},{9,8},{10,11... | collective-permute-start | bytes 884744 | tf_op jit(solution)/shard_map/ppermute | solution.py:107
  66.0 2.4 collective-permute-start.12
  66.0 3.1 collective-permute-start.13
  66.5 15.4 %collective-permute-start.16 = (bf16[96,3072]{1,0:T(8,128)(2,1)S(1)}, bf16[96,3072]{1,0:T(8,128)(2,1)S(1)}, u32[]{:S(2)}, u32[]{:S(2)}) collective-permute-start(bf16[96,3072]{1,0:T(8,128)(2,1)S(1)} %copy-done.9), channel_id=1, source_target_pairs={{0,1},{1,0},{2,3},{3,2},{4,5},{5,4},{6,7},{7,6},{8,9},{9,8},{10,11... | collective-permute-start | bytes 1769480 | tf_op jit(solution)/shard_map/ppermute | solution.py:107
  66.9 15.0 %collective-permute-start.11 = (bf16[96,3072]{1,0:T(8,128)(2,1)}, bf16[96,3072]{1,0:T(8,128)(2,1)S(1)}, u32[]{:S(2)}, u32[]{:S(2)}) collective-permute-start(bf16[96,3072]{1,0:T(8,128)(2,1)} %get-tuple-element.115.refs_2_.refs_1_.refs_14_), channel_id=1, source_target_pairs={{0,8},{4,20},{8,0},{12,28},{16,24},{20,4},{24,16},{28,12},{1,9},{5... | collective-permute-start | bytes 1769480 | tf_op jit(solution)/shard_map/ppermute | solution.py:111
  70.6 16.3 %copy-start.36 = (bf16[96,3072]{1,0:T(8,128)(2,1)S(1)}, bf16[96,3072]{1,0:T(8,128)(2,1)}, u32[]{:S(2)}) copy-start(bf16[96,3072]{1,0:T(8,128)(2,1)} %get-tuple-element.127.refs_2_) | copy-start | bytes 1769476
  70.6 12.7 %collective-permute-start.14 = (bf16[96,3072]{1,0:T(8,128)(2,1)}, bf16[96,3072]{1,0:T(8,128)(2,1)S(1)}, u32[]{:S(2)}, u32[]{:S(2)}) collective-permute-start(bf16[96,3072]{1,0:T(8,128)(2,1)} %get-tuple-element.117.refs_5_.refs_18_), channel_id=1, source_target_pairs={{0,8},{4,20},{8,0},{12,28},{16,24},{20,4},{24,16},{28,12},{1,9},{5... | collective-permute-start | bytes 1769480 | tf_op jit(solution)/shard_map/ppermute | solution.py:111
  72.0 9.9 %collective-permute-start.15 = (f32[8,128]{1,0:T(8,128)S(1)}, f32[8,128]{1,0:T(8,128)S(1)}, u32[]{:S(2)}, u32[]{:S(2)}) collective-permute-start(f32[8,128]{1,0:T(8,128)S(1)} %fusion.11), channel_id=1, source_target_pairs={{0,1},{1,0},{2,3},{3,2},{4,5},{5,4},{6,7},{7,6},{8,9},{9,8},{10,11... | collective-permute-start | bytes 12296 | tf_op jit(solution)/shard_map/ppermute | solution.py:107
  72.9 16.7 %collective-permute-start.23 = (bf16[96,3072]{1,0:T(8,128)(2,1)}, bf16[96,3072]{1,0:T(8,128)(2,1)S(1)}, u32[]{:S(2)}, u32[]{:S(2)}) collective-permute-start(bf16[96,3072]{1,0:T(8,128)(2,1)} %get-tuple-element.128.refs_3_), channel_id=1, source_target_pairs={{0,8},{4,20},{8,0},{12,28},{16,24},{20,4},{24,16},{28,12},{1,9},{5... | collective-permute-start | bytes 1769480 | tf_op jit(solution)/shard_map/ppermute | solution.py:111
  84.7 5.3 %collective-permute-start.17 = (bf16[96,3072]{1,0:T(8,128)(2,1)}, bf16[96,3072]{1,0:T(8,128)(2,1)S(1)}, u32[]{:S(2)}, u32[]{:S(2)}) collective-permute-start(bf16[96,3072]{1,0:T(8,128)(2,1)} %get-tuple-element.121.refs_7_.refs_20_), channel_id=1, source_target_pairs={{0,4},{4,0},{8,12},{12,8},{16,20},{20,16},{24,28},{28,24},{1,5},{5... | collective-permute-start | bytes 1769480 | tf_op jit(solution)/shard_map/ppermute | solution.py:107
  85.5 4.5 %collective-permute-start.18 = (f32[8,128]{1,0:T(8,128)S(1)}, f32[8,128]{1,0:T(8,128)S(1)}, u32[]{:S(2)}, u32[]{:S(2)}) collective-permute-start(f32[8,128]{1,0:T(8,128)S(1)} %fusion.21), channel_id=1, source_target_pairs={{0,2},{1,3},{2,0},{3,1},{4,6},{5,7},{6,4},{7,5},{8,10},{9,11},{10,... | collective-permute-start | bytes 12296 | tf_op jit(solution)/shard_map/ppermute | solution.py:107
  86.9 10.9 %collective-permute-start.24 = (bf16[96,3072]{1,0:T(8,128)(2,1)S(1)}, bf16[96,3072]{1,0:T(8,128)(2,1)S(1)}, u32[]{:S(2)}, u32[]{:S(2)}) collective-permute-start(bf16[96,3072]{1,0:T(8,128)(2,1)S(1)} %copy-done.36), channel_id=1, source_target_pairs={{0,4},{4,0},{8,12},{12,8},{16,20},{20,16},{24,28},{28,24},{1,5},{5... | collective-permute-start | bytes 1769480 | tf_op jit(solution)/shard_map/ppermute | solution.py:107
  89.6 8.6 %collective-permute-start.25 = (bf16[96,3072]{1,0:T(8,128)(2,1)S(1)}, bf16[96,3072]{1,0:T(8,128)(2,1)}, u32[]{:S(2)}, u32[]{:S(2)}) collective-permute-start(bf16[96,3072]{1,0:T(8,128)(2,1)S(1)} %collective-permute-done.23.refs_4_), channel_id=1, source_target_pairs={{0,4},{4,0},{8,12},{12,8},{16,20},{20,16},{24,28},{28,24},{1,5},{5... | collective-permute-start | bytes 1769480 | tf_op jit(solution)/shard_map/ppermute | solution.py:107
  92.0 10.2 %collective-permute-start.19 = (bf16[96,3072]{1,0:T(8,128)(2,1)}, bf16[96,3072]{1,0:T(8,128)(2,1)}, u32[]{:S(2)}, u32[]{:S(2)}) collective-permute-start(bf16[96,3072]{1,0:T(8,128)(2,1)} %get-tuple-element.124.refs_3_.refs_16_), channel_id=1, source_target_pairs={{0,8},{4,20},{8,0},{12,28},{16,24},{20,4},{24,16},{28,12},{1,9},{5... | collective-permute-start | bytes 1769480 | tf_op jit(solution)/shard_map/ppermute | solution.py:111
  94.0 16.3 %collective-permute-start.22 = (bf16[96,1536]{1,0:T(8,128)(2,1)}, bf16[96,1536]{1,0:T(8,128)(2,1)S(1)}, u32[]{:S(2)}, u32[]{:S(2)}) collective-permute-start(bf16[96,1536]{1,0:T(8,128)(2,1)} %pack_down.1.refs_2_.refs_0_), channel_id=1, source_target_pairs={{0,2},{1,3},{2,0},{3,1},{4,6},{5,7},{6,4},{7,5},{8,10},{9,11},{10,... | collective-permute-start | bytes 884744 | tf_op jit(solution)/shard_map/ppermute | solution.py:107
  95.4 20.4 %collective-permute-start.20 = (bf16[96,3072]{1,0:T(8,128)(2,1)S(1)}, bf16[96,3072]{1,0:T(8,128)(2,1)}, u32[]{:S(2)}, u32[]{:S(2)}) collective-permute-start(bf16[96,3072]{1,0:T(8,128)(2,1)S(1)} %copy-done.29), channel_id=1, source_target_pairs={{0,4},{4,0},{8,12},{12,8},{16,20},{20,16},{24,28},{28,24},{1,5},{5... | collective-permute-start | bytes 1769480 | tf_op jit(solution)/shard_map/ppermute | solution.py:107
  97.7 16.5 %collective-permute-start.27 = (bf16[96,6144]{1,0:T(8,128)(2,1)}, bf16[96,6144]{1,0:T(8,128)(2,1)}, u32[]{:S(2)}, u32[]{:S(2)}) collective-permute-start(bf16[96,6144]{1,0:T(8,128)(2,1)} %w_up_rows.1.refs_9_.refs_1_), channel_id=1, source_target_pairs={{0,4},{4,0},{8,12},{12,8},{16,20},{20,16},{24,28},{28,24},{1,5},{5... | collective-permute-start | bytes 3538952 | tf_op jit(solution)/shard_map/ppermute | solution.py:107
  98.3 33.0 %collective-permute-start.26 = (bf16[96,6144]{1,0:T(8,128)(2,1)}, bf16[96,6144]{1,0:T(8,128)(2,1)S(1)}, u32[]{:S(2)}, u32[]{:S(2)}) collective-permute-start(bf16[96,6144]{1,0:T(8,128)(2,1)} %w_up_rows.1.refs_9_.refs_1_), channel_id=1, source_target_pairs={{0,8},{4,20},{8,0},{12,28},{16,24},{20,4},{24,16},{28,12},{1,9},{5... | collective-permute-start | bytes 3538952 | tf_op jit(solution)/shard_map/ppermute | solution.py:111
  102.2 13.6 %collective-permute-start.21 = (bf16[96,3072]{1,0:T(8,128)(2,1)}, bf16[96,3072]{1,0:T(8,128)(2,1)}, u32[]{:S(2)}, u32[]{:S(2)}) collective-permute-start(bf16[96,3072]{1,0:T(8,128)(2,1)} %collective-permute-done.19.refs_4_.refs_17_), channel_id=1, source_target_pairs={{0,4},{4,0},{8,12},{12,8},{16,20},{20,16},{24,28},{28,24},{1,5},{5... | collective-permute-start | bytes 1769480 | tf_op jit(solution)/shard_map/ppermute | solution.py:107
  112.8 18.4 %collective-permute-start.29 = (bf16[96,3072]{1,0:T(8,128)(2,1)}, bf16[96,3072]{1,0:T(8,128)(2,1)S(1)}, u32[]{:S(2)}, u32[]{:S(2)}) collective-permute-start(bf16[96,3072]{1,0:T(8,128)(2,1)} %w_down_join.1.refs_10_.refs_1_), channel_id=1, source_target_pairs={{0,1},{1,0},{2,3},{3,2},{4,5},{5,4},{6,7},{7,6},{8,9},{9,8},{10,11... | collective-permute-start | bytes 1769480 | tf_op jit(solution)/shard_map/ppermute | solution.py:107
  114.3 17.0 %collective-permute-start.28 = (bf16[96,6144]{1,0:T(8,128)(2,1)}, bf16[96,6144]{1,0:T(8,128)(2,1)S(1)}, u32[]{:S(2)}, u32[]{:S(2)}) collective-permute-start(bf16[96,6144]{1,0:T(8,128)(2,1)} %collective-permute-done.27.refs_5_), channel_id=1, source_target_pairs={{0,8},{4,20},{8,0},{12,28},{16,24},{20,4},{24,16},{28,12},{1,9},{5... | collective-permute-start | bytes 3538952 | tf_op jit(solution)/shard_map/ppermute | solution.py:111
  133.5 3.1 collective-permute-start.30
  136.5 19.0 %collective-permute-start.31 = (bf16[96,6144]{1,0:T(8,128)(2,1)S(1)}, bf16[96,6144]{1,0:T(8,128)(2,1)S(1)}, u32[]{:S(2)}, u32[]{:S(2)}) collective-permute-start(bf16[96,6144]{1,0:T(8,128)(2,1)S(1)} %collective-permute-done.30.refs_3_), channel_id=1, source_target_pairs={{0,8},{4,20},{8,0},{12,28},{16,24},{20,4},{24,16},{28,12},{1,9},{5... | collective-permute-start | bytes 3538952 | tf_op jit(solution)/shard_map/ppermute | solution.py:111
  148.6 16.8 %collective-permute-start.34 = (bf16[96,6144]{1,0:T(8,128)(2,1)}, bf16[96,6144]{1,0:T(8,128)(2,1)}, u32[]{:S(2)}, u32[]{:S(2)}) collective-permute-start(bf16[96,6144]{1,0:T(8,128)(2,1)} %w_down_rows.1.refs_10_.refs_2_.refs_1_), channel_id=1, source_target_pairs={{0,8},{4,20},{8,0},{12,28},{16,24},{20,4},{24,16},{28,12},{1,9},{5... | collective-permute-start | bytes 3538952 | tf_op jit(solution)/shard_map/ppermute | solution.py:111
  149.5 13.2 %collective-permute-start.35 = (bf16[96,6144]{1,0:T(8,128)(2,1)}, bf16[96,6144]{1,0:T(8,128)(2,1)}, u32[]{:S(2)}, u32[]{:S(2)}) collective-permute-start(bf16[96,6144]{1,0:T(8,128)(2,1)} %w_down_rows.1.refs_10_.refs_2_.refs_1_), channel_id=1, source_target_pairs={{0,4},{4,0},{8,12},{12,8},{16,20},{20,16},{24,28},{28,24},{1,5},{5... | collective-permute-start | bytes 3538952 | tf_op jit(solution)/shard_map/ppermute | solution.py:107
  149.5 16.0 %collective-permute-start.32 = (bf16[96,6144]{1,0:T(8,128)(2,1)S(1)}, bf16[96,6144]{1,0:T(8,128)(2,1)}, u32[]{:S(2)}, u32[]{:S(2)}) collective-permute-start(bf16[96,6144]{1,0:T(8,128)(2,1)S(1)} %copy-done.17), channel_id=1, source_target_pairs={{0,4},{4,0},{8,12},{12,8},{16,20},{20,16},{24,28},{28,24},{1,5},{5... | collective-permute-start | bytes 3538952 | tf_op jit(solution)/shard_map/ppermute | solution.py:107
  162.7 3.1 collective-permute-start.33
  162.7 16.5 %collective-permute-start.36 = (bf16[96,6144]{1,0:T(8,128)(2,1)}, bf16[96,6144]{1,0:T(8,128)(2,1)S(1)}, u32[]{:S(2)}, u32[]{:S(2)}) collective-permute-start(bf16[96,6144]{1,0:T(8,128)(2,1)} %collective-permute-done.35.refs_6_.refs_5_), channel_id=1, source_target_pairs={{0,8},{4,20},{8,0},{12,28},{16,24},{20,4},{24,16},{28,12},{1,9},{5... | collective-permute-start | bytes 3538952 | tf_op jit(solution)/shard_map/ppermute | solution.py:111
  180.9 3.1 collective-permute-start.37
  180.9 20.9 %collective-permute-start.39 = (bf16[96,6144]{1,0:T(8,128)(2,1)}, bf16[96,6144]{1,0:T(8,128)(2,1)S(1)}, u32[]{:S(2)}, u32[]{:S(2)}) collective-permute-start(bf16[96,6144]{1,0:T(8,128)(2,1)} %get-tuple-element.149.refs_3_.refs_2_), channel_id=1, source_target_pairs={{0,4},{4,0},{8,12},{12,8},{16,20},{20,16},{24,28},{28,24},{1,5},{5... | collective-permute-start | bytes 3538952 | tf_op jit(solution)/shard_map/ppermute | solution.py:107
  183.9 16.2 %collective-permute-start.38 = (bf16[96,6144]{1,0:T(8,128)(2,1)S(1)}, bf16[96,6144]{1,0:T(8,128)(2,1)S(1)}, u32[]{:S(2)}, u32[]{:S(2)}) collective-permute-start(bf16[96,6144]{1,0:T(8,128)(2,1)S(1)} %collective-permute-done.37.refs_4_.refs_3_), channel_id=1, source_target_pairs={{0,8},{4,20},{8,0},{12,28},{16,24},{20,4},{24,16},{28,12},{1,9},{5... | collective-permute-start | bytes 3538952 | tf_op jit(solution)/shard_map/ppermute | solution.py:111
  201.7 3.1 collective-permute-start.40
  232.0 19.4 %collective-permute-start.42 = (bf16[384,3072]{1,0:T(8,128)(2,1)}, bf16[384,3072]{1,0:T(8,128)(2,1)}, u32[]{:S(2)}, u32[]{:S(2)}) collective-permute-start(bf16[384,3072]{1,0:T(8,128)(2,1)} %g_down_far.1.refs_11_), channel_id=1, source_target_pairs={{0,4},{4,0},{8,12},{12,8},{16,20},{20,16},{24,28},{28,24},{1,5},{5... | collective-permute-start | bytes 7077896 | tf_op jit(solution)/shard_map/ppermute | solution.py:107
  246.5 11.6 %collective-permute-start.41 = (bf16[384,3072]{1,0:T(8,128)(2,1)}, bf16[384,3072]{1,0:T(8,128)(2,1)}, u32[]{:S(2)}, u32[]{:S(2)}) collective-permute-start(bf16[384,3072]{1,0:T(8,128)(2,1)} %g_up_far.1.refs_3_), channel_id=1, source_target_pairs={{0,4},{4,0},{8,12},{12,8},{16,20},{20,16},{24,28},{28,24},{1,5},{5... | collective-permute-start | bytes 7077896 | tf_op jit(solution)/shard_map/ppermute | solution.py:107
  247.4 58.6 %all-to-all-start = ((bf16[4,192,1536]{2,1,0:T(8,128)(2,1)}), bf16[4,192,1536]{2,1,0:T(8,128)(2,1)S(1)}, u32[]{:S(2)}, u32[]{:S(2)}) async-start(bf16[4,192,1536]{2,1,0:T(8,128)(2,1)} %bitcast.99), calls=%async_computation | async-start | bytes 4718592 | tf_op jit(solution)/shard_map/all_to_all | solution.py:392
  256.9 20.1 %collective-permute-start.44 = (bf16[192,3072]{1,0:T(8,128)(2,1)}, bf16[192,3072]{1,0:T(8,128)(2,1)}, u32[]{:S(2)}, u32[]{:S(2)}) collective-permute-start(bf16[192,3072]{1,0:T(8,128)(2,1)} %get-tuple-element.161), channel_id=1, source_target_pairs={{0,8},{4,20},{8,0},{12,28},{16,24},{20,4},{24,16},{28,12},{1,9},{5... | collective-permute-start | bytes 3538952 | tf_op jit(solution)/shard_map/ppermute | solution.py:111
  263.5 31.6 %collective-permute-start.43 = (bf16[192,3072]{1,0:T(8,128)(2,1)}, bf16[192,3072]{1,0:T(8,128)(2,1)S(1)}, u32[]{:S(2)}, u32[]{:S(2)}) collective-permute-start(bf16[192,3072]{1,0:T(8,128)(2,1)} %get-tuple-element.160), channel_id=1, source_target_pairs={{0,8},{4,20},{8,0},{12,28},{16,24},{20,4},{24,16},{28,12},{1,9},{5... | collective-permute-start | bytes 3538952 | tf_op jit(solution)/shard_map/ppermute | solution.py:111
  279.8 13.0 %collective-permute-start.45 = (bf16[96,3072]{1,0:T(8,128)(2,1)}, bf16[96,3072]{1,0:T(8,128)(2,1)}, u32[]{:S(2)}, u32[]{:S(2)}) collective-permute-start(bf16[96,3072]{1,0:T(8,128)(2,1)} %get-tuple-element.165), channel_id=1, source_target_pairs={{0,16},{4,12},{8,24},{12,4},{16,0},{20,28},{24,8},{28,20},{1,17},{... | collective-permute-start | bytes 1769480 | tf_op jit(solution)/shard_map/ppermute | solution.py:115
  298.9 13.2 %collective-permute-start.46 = (bf16[96,3072]{1,0:T(8,128)(2,1)}, bf16[96,3072]{1,0:T(8,128)(2,1)S(1)}, u32[]{:S(2)}, u32[]{:S(2)}) collective-permute-start(bf16[96,3072]{1,0:T(8,128)(2,1)} %get-tuple-element.171), channel_id=1, source_target_pairs={{0,16},{4,12},{8,24},{12,4},{16,0},{20,28},{24,8},{28,20},{1,17},{... | collective-permute-start | bytes 1769480 | tf_op jit(solution)/shard_map/ppermute | solution.py:115
  299.4 12.6 %collective-permute-start.47 = (bf16[2,96,768]{2,1,0:T(8,128)(2,1)}, bf16[2,96,768]{2,1,0:T(8,128)(2,1)S(1)}, u32[]{:S(2)}, u32[]{:S(2)}) collective-permute-start(bf16[2,96,768]{2,1,0:T(8,128)(2,1)} %bitcast.24), channel_id=1, source_target_pairs={{0,1},{1,0},{2,3},{3,2},{4,5},{5,4},{6,7},{7,6},{8,9},{9,8},{10,11... | collective-permute-start | bytes 884744 | tf_op jit(solution)/shard_map/ppermute | solution.py:107
  306.0 28.4 %collective-permute-start.48 = (bf16[384,2304]{1,0:T(8,128)(2,1)}, bf16[384,2304]{1,0:T(8,128)(2,1)}, u32[]{:S(2)}, u32[]{:S(2)}) collective-permute-start(bf16[384,2304]{1,0:T(8,128)(2,1)} %g_qkv_far.1.refs_5_), channel_id=1, source_target_pairs={{0,4},{4,0},{8,12},{12,8},{16,20},{20,16},{24,28},{28,24},{1,5},{5... | collective-permute-start | bytes 5308424 | tf_op jit(solution)/shard_map/ppermute | solution.py:107
  316.4 17.9 %collective-permute-start.49 = (bf16[1,96,768]{2,1,0:T(8,128)(2,1)S(1)}, bf16[1,96,768]{2,1,0:T(8,128)(2,1)S(1)}, u32[]{:S(2)}, u32[]{:S(2)}) collective-permute-start(bf16[1,96,768]{2,1,0:T(8,128)(2,1)S(1)} %slice.131), channel_id=1, source_target_pairs={{0,2},{1,3},{2,0},{3,1},{4,6},{5,7},{6,4},{7,5},{8,10},{9,11},{10,... | collective-permute-start | bytes 442376 | tf_op jit(solution)/shard_map/ppermute | solution.py:107
  316.5 17.8 %collective-permute-start.50 = (bf16[2,96,768]{2,1,0:T(8,128)(2,1)S(1)}, bf16[2,96,768]{2,1,0:T(8,128)(2,1)S(1)}, u32[]{:S(2)}, u32[]{:S(2)}) collective-permute-start(bf16[2,96,768]{2,1,0:T(8,128)(2,1)S(1)} %bitcast.116), channel_id=1, source_target_pairs={{0,1},{1,0},{2,3},{3,2},{4,5},{5,4},{6,7},{7,6},{8,9},{9,8},{10,11... | collective-permute-start | bytes 884744 | tf_op jit(solution)/shard_map/ppermute | solution.py:107
  330.6 10.5 %collective-permute-start.52 = (bf16[384,1024]{1,0:T(8,128)(2,1)}, bf16[384,1024]{1,0:T(8,128)(2,1)}, u32[]{:S(2)}, u32[]{:S(2)}) collective-permute-start(bf16[384,1024]{1,0:T(8,128)(2,1)} %g_out_far.1.refs_5_), channel_id=1, source_target_pairs={{0,4},{4,0},{8,12},{12,8},{16,20},{20,16},{24,28},{28,24},{1,5},{5... | collective-permute-start | bytes 2359304 | tf_op jit(solution)/shard_map/ppermute | solution.py:107
  330.7 44.0 %all-to-all-start.1 = ((bf16[4,192,768]{2,1,0:T(8,128)(2,1)}), bf16[4,192,768]{2,1,0:T(8,128)(2,1)S(1)}, u32[]{:S(2)}, u32[]{:S(2)}) async-start(bf16[4,192,768]{2,1,0:T(8,128)(2,1)} %bitcast.31), calls=%async_computation.1 | async-start | bytes 2359296 | tf_op jit(solution)/shard_map/all_to_all | solution.py:392
  339.8 13.3 %collective-permute-start.51 = (bf16[192,2304]{1,0:T(8,128)(2,1)}, bf16[192,2304]{1,0:T(8,128)(2,1)S(1)}, u32[]{:S(2)}, u32[]{:S(2)}) collective-permute-start(bf16[192,2304]{1,0:T(8,128)(2,1)} %get-tuple-element.182), channel_id=1, source_target_pairs={{0,8},{4,20},{8,0},{12,28},{16,24},{20,4},{24,16},{28,12},{1,9},{5... | collective-permute-start | bytes 2654216 | tf_op jit(solution)/shard_map/ppermute | solution.py:111
  344.5 24.7 %collective-permute-start.53 = (bf16[192,1024]{1,0:T(8,128)(2,1)}, bf16[192,1024]{1,0:T(8,128)(2,1)}, u32[]{:S(2)}, u32[]{:S(2)}) collective-permute-start(bf16[192,1024]{1,0:T(8,128)(2,1)} %get-tuple-element.187), channel_id=1, source_target_pairs={{0,8},{4,20},{8,0},{12,28},{16,24},{20,4},{24,16},{28,12},{1,9},{5... | collective-permute-start | bytes 1179656 | tf_op jit(solution)/shard_map/ppermute | solution.py:111
  356.5 9.8 %collective-permute-start.54 = (bf16[96,2304]{1,0:T(8,128)(2,1)}, bf16[96,2304]{1,0:T(8,128)(2,1)S(1)}, u32[]{:S(2)}, u32[]{:S(2)}) collective-permute-start(bf16[96,2304]{1,0:T(8,128)(2,1)} %get-tuple-element.188), channel_id=1, source_target_pairs={{0,16},{4,12},{8,24},{12,4},{16,0},{20,28},{24,8},{28,20},{1,17},{... | collective-permute-start | bytes 1327112 | tf_op jit(solution)/shard_map/ppermute | solution.py:115
  358.7 14.9 %collective-permute-start.60 = (bf16[1,96,768]{2,1,0:T(8,128)(2,1)}, bf16[1,96,768]{2,1,0:T(8,128)(2,1)S(1)}, u32[]{:S(2)}, u32[]{:S(2)}) collective-permute-start(bf16[1,96,768]{2,1,0:T(8,128)(2,1)} %slice.138), channel_id=1, source_target_pairs={{0,2},{1,3},{2,0},{3,1},{4,6},{5,7},{6,4},{7,5},{8,10},{9,11},{10,... | collective-permute-start | bytes 442376 | tf_op jit(solution)/shard_map/ppermute | solution.py:107
  371.2 8.1 %collective-permute-start.57 = (bf16[96,1024]{1,0:T(8,128)(2,1)}, bf16[96,1024]{1,0:T(8,128)(2,1)S(1)}, u32[]{:S(2)}, u32[]{:S(2)}) collective-permute-start(bf16[96,1024]{1,0:T(8,128)(2,1)} %get-tuple-element.192), channel_id=1, source_target_pairs={{0,16},{4,12},{8,24},{12,4},{16,0},{20,28},{24,8},{28,20},{1,17},{... | collective-permute-start | bytes 589832 | tf_op jit(solution)/shard_map/ppermute | solution.py:115
  371.9 12.2 %collective-permute-start.55 = (bf16[2,96,576]{1,2,0:T(8,128)(2,1)S(1)}, bf16[2,96,576]{1,2,0:T(8,128)(2,1)S(1)}, u32[]{:S(2)}, u32[]{:S(2)}) collective-permute-start(bf16[2,96,576]{1,2,0:T(8,128)(2,1)S(1)} %copy.73), channel_id=1, source_target_pairs={{0,1},{1,0},{2,3},{3,2},{4,5},{5,4},{6,7},{7,6},{8,9},{9,8},{10,11... | collective-permute-start | bytes 663560 | tf_op jit(solution)/shard_map/ppermute | solution.py:107
  382.7 5.3 %collective-permute-start.58 = (bf16[2,96,256]{1,2,0:T(8,128)(2,1)S(1)}, bf16[2,96,256]{1,2,0:T(8,128)(2,1)S(1)}, u32[]{:S(2)}, u32[]{:S(2)}) collective-permute-start(bf16[2,96,256]{1,2,0:T(8,128)(2,1)S(1)} %bitcast.112), channel_id=1, source_target_pairs={{0,1},{1,0},{2,3},{3,2},{4,5},{5,4},{6,7},{7,6},{8,9},{9,8},{10,11... | collective-permute-start | bytes 294920 | tf_op jit(solution)/shard_map/ppermute | solution.py:107
  384.2 9.1 %collective-permute-start.56 = (bf16[1,96,576]{1,2,0:T(8,128)(2,1)S(1)}, bf16[1,96,576]{1,2,0:T(8,128)(2,1)S(1)}, u32[]{:S(2)}, u32[]{:S(2)}) collective-permute-start(bf16[1,96,576]{1,2,0:T(8,128)(2,1)S(1)} %slice.133), channel_id=1, source_target_pairs={{0,2},{1,3},{2,0},{3,1},{4,6},{5,7},{6,4},{7,5},{8,10},{9,11},{10,... | collective-permute-start | bytes 331784 | tf_op jit(solution)/shard_map/ppermute | solution.py:107
  388.0 6.7 %collective-permute-start.59 = (bf16[1,96,256]{1,2,0:T(8,128)(2,1)S(1)}, bf16[1,96,256]{1,2,0:T(8,128)(2,1)S(1)}, u32[]{:S(2)}, u32[]{:S(2)}) collective-permute-start(bf16[1,96,256]{1,2,0:T(8,128)(2,1)S(1)} %slice.135), channel_id=1, source_target_pairs={{0,2},{1,3},{2,0},{3,1},{4,6},{5,7},{6,4},{7,5},{8,10},{9,11},{10,... | collective-permute-start | bytes 147464 | tf_op jit(solution)/shard_map/ppermute | solution.py:107
  (76 other events, 331.5 us)

commit v4 on v3

--- a/solution.py
+++ b/solution.py
@@ -224,7 +224,7 @@
     return (left.astype(WIDE) + right.astype(WIDE)).astype(LOW)
 
 
-def scatter_weight(run, name, left, right, split, store, beside=None, triple=False):
+def scatter_weight(run, name, left, right, split, store, beside=None, kinds=0):
     rows, width = left.shape
     fsdp = lax.axis_size(FSDP)
     depth = width // fsdp
@@ -292,10 +292,10 @@
                 out[...] = add_low(own[:, lanes], got[:, lanes])
 
         def third_split(own, got, keep, send):
-            n = columns // 12
+            n = columns // (4 * kinds)
             for p in range(4):
                 out = keep if p < 2 else send
-                for k in range(3):
+                for k in range(kinds):
                     lanes = slice((4 * k + p) * n, (4 * k + p + 1) * n)
                     out[at[p % 2], k * n : (k + 1) * n] = add_low(own[:, lanes], got[:, lanes])
 
@@ -329,10 +329,10 @@
             )
             split = lambda *parts: tuple(value.reshape(2, depth, -1) for value in parts)
         else:
-            shape = (2 * depth, columns // 4) if triple else (depth, half)
-            work = third_split if triple else third
+            shape = (2 * depth, columns // 4) if kinds else (depth, half)
+            work = third_split if kinds else third
             here = run.call(name + "_add3", work, ins, [(shape, LOW, whole(*shape))] * 2, moved=6 * depth * columns)
-            if triple:
+            if kinds:
                 split = lambda *parts: tuple(value.reshape(2, depth, -1) for value in parts)
     else:
 
@@ -1088,7 +1088,7 @@
     def share_out():
         beside = (have.sums_first, have.sums_second)
         return Task(
-            scatter_weight(run, "g_out", have.grad_o, have.attended, split_one, keep("grad_out"), beside)
+            scatter_weight(run, "g_out", have.grad_o, have.attended, split_one, keep("grad_out"), beside, 1)
         )
 
     def back_attend():
@@ -1097,7 +1097,7 @@
         )
 
     def share_qkv():
-        return Task(scatter_weight(run, "g_qkv", have.entry, have.g_all, split_qkv, keep("grad_qkv"), triple=True))
+        return Task(scatter_weight(run, "g_qkv", have.entry, have.g_all, split_qkv, keep("grad_qkv"), kinds=3))
 
     def back_entry():
         def work(product, refs, outs, tile):

time: 403 us -> 403 us (level)
  no operation moved by 1% of the time
where the time goes in v4:
time: 403 us; the launch traced here: 396 us
  Pallas kernels  221 us (55%)
  starting transfers between devices  66.1 us (16%)
  waiting for transfers between devices  64.7 us (16%)
  local copies, waits for them, and re-layouts  32 us (8%)
  other arithmetic  10.4 us (3%)
    pallas_call x51, Pallas kernels, call(): pl.pallas_call(wrapped, grid=grid, in_specs=[spec for _, spec in ins] + [...  221 us
    ppermute x41, waiting for transfers between devices, swap(): return lax.ppermute(value, axis, [(i, i ^ bit) for i in range(size)])  41.2 us
    ppermute x41, starting transfers between devices, swap(): return lax.ppermute(value, axis, [(i, i ^ bit) for i in range(size)])  35 us
    unnamed x159, local copies, waits for them, and re-layouts  25.5 us
    ppermute x16, waiting for transfers between devices, swap_first(): lax.ppermute(value, FSDP, [(i, i ^ (4 if i % 2 else 2)) for i in range(8)])  23.5 us
    ppermute x16, starting transfers between devices, swap_first(): lax.ppermute(value, FSDP, [(i, i ^ (4 if i % 2 else 2)) for i in range(8)])  19.4 us
  transfers between devices with their start and end apart: 63, of which 23 were waited for; matrix products, arithmetic and copies ran while one was open for 4% of the time, Pallas kernels for 48%

profile of v4, /device:TPU:0, one launch (start us, length us, event | category | flops | bytes accessed | tf_op | source)
XLA Modules:
  0.0 396.1 jit_solution(9857359370246918629)
XLA Ops:
  3.0 4.1 %collective-permute-start.1 = (bf16[96,768]{1,0:T(8,128)(2,1)S(1)}, bf16[96,768]{1,0:T(8,128)(2,1)S(1)}, u32[]{:S(2)}, u32[]{:S(2)}) collective-permute-start(bf16[96,768]{1,0:T(8,128)(2,1)S(1)} %pad_maximum_fusion.refs_4_.refs_0_), channel_id=1, source_target_pairs={{0,2},{1,3},{2,0},{3,1},{4,6},{5,7},{6,4},{7,5},{8,10},{9,11},{10,... | collective-permute-start | bytes 442376 | tf_op jit(solution)/shard_map/ppermute | solution.py:107
  8.1 2.1 magnitudes.1.refs_4_
  15.1 1.7 slots.1
  19.6 1.8 pack_up.1.refs_3_.refs_0_
  22.7 1.7 w_tqkv_join.1
  27.3 5.8 %place_rows.1 = (bf16[768,768]{1,0:T(8,128)(2,1)}, bf16[768,768]{1,0:T(8,128)(2,1)}, bf16[768,768]{1,0:T(8,128)(2,1)}, bf16[768,768]{1,0:T(8,128)(2,1)}) custom-call(s32[9]{0:T(128)} %pad_add_fusion.refs_0_, bf16[3072,768]{1,0:T(8,128)(2,1)} %refs_1_.7, bf16[3072,768]{1,0:T(8,128)(2,1)} %refs_2_.5, bf16[96,1536]{1,0:T(8,128)(2,1)} %get-tuple-element.106.refs_3_.refs_0_), custom_call_target="tpu_custom_call" | custom-call | tf_op jit(solution)/shard_map/place_rows/pallas_call | solution.py:80
  33.8 1.7 w_qkv_join.1
  36.2 2.1 w_tqkv_rows.1.refs_1_
  43.6 2.6 collective-permute-start.5
  46.6 13.1 %collective-permute-done.5.refs_1_ = bf16[96,1536]{1,0:T(8,128)(2,1)S(1)} collective-permute-done((bf16[96,1536]{1,0:T(8,128)(2,1)S(1)}, bf16[96,1536]{1,0:T(8,128)(2,1)S(1)}, u32[]{:S(2)}, u32[]{:S(2)}) %collective-permute-start.5) | collective-permute-done | bytes 294944 | tf_op jit(solution)/shard_map/ppermute | solution.py:107
  60.9 1.9 w_up_join.1
  63.9 2.1 w_qkv_rows.1
  74.4 7.5 %collective-permute-done.15.refs_2_ = f32[8,128]{1,0:T(8,128)S(1)} collective-permute-done((f32[8,128]{1,0:T(8,128)S(1)}, f32[8,128]{1,0:T(8,128)S(1)}, u32[]{:S(2)}, u32[]{:S(2)}) %collective-permute-start.15) | collective-permute-done | bytes 4128 | tf_op jit(solution)/shard_map/ppermute | solution.py:107
  87.0 1.8 pack_down.1.refs_2_.refs_0_
  95.4 2.4 w_up_rows.1.refs_9_.refs_1_
  98.8 3.4 collective-permute-done.19.refs_4_.refs_17_
  102.2 7.2 %project_teacher.1.refs_2_.refs_5_.refs_6_.refs_7_ = bf16[768,2304]{1,0:T(8,128)(2,1)} custom-call(bf16[768,768]{1,0:T(8,128)(2,1)} %get-tuple-element.126.refs_0_.refs_9_, bf16[96,3072]{1,0:T(8,128)(2,1)} %w_tqkv_rows.1.refs_1_, bf16[96,3072]{1,0:T(8,128)(2,1)} %get-tuple-element.127.refs_2_, bf16[96,3072]{1,0:T(8,128)(2,1)} %get-tuple-element.128.refs_3_, ...), custom_call_target="tpu_custom_call" | custom-call | flops 13589544960 | bytes 41287680 | tf_op jit(solution)/shard_map/project_teacher/pallas_call | solution.py:80
  110.9 1.9 w_down_join.1.refs_10_.refs_1_
  115.8 7.0 %project_student.1.refs_2_.refs_3_.refs_4_.refs_8_.refs_1_ = bf16[768,2304]{1,0:T(8,128)(2,1)} custom-call(bf16[768,768]{1,0:T(8,128)(2,1)} %get-tuple-element.107.refs_0_, bf16[96,3072]{1,0:T(8,128)(2,1)} %get-tuple-element.115.refs_2_.refs_1_.refs_14_, bf16[96,3072]{1,0:T(8,128)(2,1)} %get-tuple-element.120.refs_2_.refs_15_, ...), custom_call_target="tpu_custom_call" | custom-call | flops 13589544960 | bytes 41287680 | tf_op jit(solution)/shard_map/project_student/pallas_call | solution.py:80
  122.8 8.5 %attend_forward.2 = (bf16[768,768]{1,0:T(8,128)(2,1)}, bf16[768,768]{1,0:T(8,128)(2,1)}, bf16[3,6,256,512]{3,2,1,0:T(8,128)(2,1)}, bf16[3,6,256,512]{3,2,1,0:T(8,128)(2,1)}) custom-call(s32[8,768]{1,0:T(8,128)} %get-tuple-element.103.refs_2_.refs_0_, s32[768,128]{1,0:T(8,128)} %get-tuple-element.104.refs_1_, ...), custom_call_target="tpu_custom_call" | custom-call | flops 12079595520 | bytes 35389440 | tf_op jit(solution)/shard_map/attend_forward/pallas_call | solution.py:80
  137.7 8.5 %attend_forward.3 = (bf16[768,768]{1,0:T(8,128)(2,1)}, bf16[768,768]{1,0:T(8,128)(2,1)}, bf16[3,6,256,512]{3,2,1,0:T(8,128)(2,1)}, bf16[3,6,256,512]{3,2,1,0:T(8,128)(2,1)}) custom-call(s32[8,768]{1,0:T(8,128)} %get-tuple-element.103.refs_2_.refs_0_, ...), custom_call_target="tpu_custom_call", output_to_operand_aliasing={{0}: (8, {}), {1}: (9, {}), {2}: (10, {}), {3}: (11, {})} | custom-call | flops 12079595520 | bytes 35389440 | tf_op jit(solution)/shard_map/attend_forward/pallas_call | solution.py:80
  146.2 2.4 w_down_rows.1.refs_10_.refs_2_.refs_1_
  150.0 5.5 %close_teacher.1 = (f32[768,768]{1,0:T(8,128)}, bf16[768,768]{1,0:T(8,128)(2,1)}) custom-call(bf16[768,768]{1,0:T(8,128)(2,1)} %get-tuple-element.138.refs_0_, bf16[96,3072]{1,0:T(8,128)(2,1)} %w_tqkv_rows.1.refs_1_, bf16[96,3072]{1,0:T(8,128)(2,1)} %get-tuple-element.127.refs_2_, bf16[96,3072]{1,0:T(8,128)(2,1)} %get-tuple-element.128.refs_3_, ...), custom_call_target="tpu_custom_call" | custom-call | flops 4529848320 | bytes 11796480 | tf_op jit(solution)/shard_map/close_teacher/pallas_call | solution.py:80
  156.6 6.0 %close_student.1 = (f32[768,768]{1,0:T(8,128)}, f32[768,128]{1,0:T(8,128)}, bf16[768,768]{1,0:T(8,128)(2,1)}, bf16[96,6144]{1,0:T(8,128)(2,1)}) custom-call(bf16[768,768]{1,0:T(8,128)(2,1)} %get-tuple-element.136.refs_3_.refs_0_.refs_1_, bf16[96,3072]{1,0:T(8,128)(2,1)} %get-tuple-element.115.refs_2_.refs_1_.refs_14_, ...), custom_call_target="tpu_custom_call", output_to_operand_aliasing={{3}: (12, {})} | custom-call | flops 4529848320 | bytes 11796480 | tf_op jit(solution)/shard_map/close_student/pallas_call | solution.py:80
  166.8 8.3 %up_teacher.1 = (bf16[768,3072]{1,0:T(8,128)(2,1)}, bf16[96,6144]{1,0:T(8,128)(2,1)}) custom-call(bf16[768,768]{1,0:T(8,128)(2,1)} %get-tuple-element.142.refs_0_, bf16[96,6144]{1,0:T(8,128)(2,1)} %w_up_rows.1.refs_9_.refs_1_, bf16[96,6144]{1,0:T(8,128)(2,1)} %get-tuple-element.143.refs_2_, ...), custom_call_target="tpu_custom_call", output_to_operand_aliasing={{1}: (9, {})} | custom-call | flops 18119393280 | bytes 53084160 | tf_op jit(solution)/shard_map/up_teacher/pallas_call | solution.py:80
  175.1 4.1 %collective-permute-done.36.refs_0_ = bf16[96,6144]{1,0:T(8,128)(2,1)S(1)} collective-permute-done((bf16[96,6144]{1,0:T(8,128)(2,1)}, bf16[96,6144]{1,0:T(8,128)(2,1)S(1)}, u32[]{:S(2)}, u32[]{:S(2)}) %collective-permute-start.36) | collective-permute-done | bytes 1179680 | tf_op jit(solution)/shard_map/ppermute | solution.py:111
  181.4 2.5 collective-permute-done.37.refs_4_.refs_3_
  185.1 10.4 %up_student.1 = (bf16[768,3072]{1,0:T(8,128)(2,1)}, bf16[768,3072]{1,0:T(8,128)(2,1)}) custom-call(bf16[768,768]{1,0:T(8,128)(2,1)} %get-tuple-element.141.refs_0_, bf16[96,6144]{1,0:T(8,128)(2,1)} %w_up_rows.1.refs_9_.refs_1_, bf16[96,6144]{1,0:T(8,128)(2,1)} %get-tuple-element.143.refs_2_, bf16[96,6144]{1,0:T(8,128)(2,1)} %copy-done.66, ...), custom_call_target="tpu_custom_call" | custom-call | flops 18119393280 | bytes 76677120 | tf_op jit(solution)/shard_map/up_student/pallas_call | solution.py:80
  195.4 4.7 %collective-permute-done.38.refs_0_ = bf16[96,6144]{1,0:T(8,128)(2,1)S(1)} collective-permute-done((bf16[96,6144]{1,0:T(8,128)(2,1)S(1)}, bf16[96,6144]{1,0:T(8,128)(2,1)S(1)}, u32[]{:S(2)}, u32[]{:S(2)}) %collective-permute-start.38) | collective-permute-done | bytes 1179680 | tf_op jit(solution)/shard_map/ppermute | solution.py:111
  201.7 3.0 collective-permute-done.40.refs_9_.refs_8_
  205.8 21.1 %down_both.1 = (f32[768,768]{1,0:T(8,128)}, bf16[768,768]{1,0:T(8,128)(2,1)}, f32[8,768]{1,0:T(8,128)}, bf16[768,1536]{1,0:T(8,128)(2,1)}) custom-call(bf16[768,3072]{1,0:T(8,128)(2,1)} %get-tuple-element.146.refs_1_.refs_0_, bf16[768,3072]{1,0:T(8,128)(2,1)} %get-tuple-element.148.refs_1_, bf16[96,6144]{1,0:T(8,128)(2,1)} %w_down_rows.1.refs_10_.refs_2_.refs_1_, ...), custom_call_target="tpu_custom_call" | custom-call | flops 36238786560 | bytes 94371840 | tf_op jit(solution)/shard_map/down_both/pallas_call | solution.py:80
  226.9 5.0 %g_down_far.1.refs_11_ = bf16[384,3072]{1,0:T(8,128)(2,1)} custom-call(bf16[768,768]{1,0:T(8,128)(2,1)} %get-tuple-element.155.refs_0_, bf16[768,3072]{1,0:T(8,128)(2,1)} %get-tuple-element.148.refs_1_, f32[768,768]{1,0:T(8,128)} %get-tuple-element.157.refs_2_.refs_11_), custom_call_target="tpu_custom_call" | custom-call | flops 9059696640 | bytes 47185920 | tf_op jit(solution)/shard_map/g_down_far/pallas_call | solution.py:80
  232.1 9.2 %back_down.1.refs_1_.refs_2_.refs_0_ = bf16[768,3072]{1,0:T(8,128)(2,1)} custom-call(bf16[768,768]{1,0:T(8,128)(2,1)} %get-tuple-element.155.refs_0_, bf16[96,6144]{1,0:T(8,128)(2,1)} %w_down_rows.1.refs_10_.refs_2_.refs_1_, bf16[96,6144]{1,0:T(8,128)(2,1)} %get-tuple-element.149.refs_3_.refs_2_, bf16[96,6144]{1,0:T(8,128)(2,1)} %copy-done.68, ...), custom_call_target="tpu_custom_call" | custom-call | flops 18119393280 | bytes 53084160 | tf_op jit(solution)/shard_map/back_down/pallas_call | solution.py:80
  241.3 5.1 %g_up_far.1.refs_3_ = bf16[384,3072]{1,0:T(8,128)(2,1)} custom-call(bf16[768,768]{1,0:T(8,128)(2,1)} %get-tuple-element.141.refs_0_, bf16[768,3072]{1,0:T(8,128)(2,1)} %back_down.1.refs_1_.refs_2_.refs_0_, bf16[768,3072]{1,0:T(8,128)(2,1)} %back_down.1.refs_1_.refs_2_.refs_0_), custom_call_target="tpu_custom_call" | custom-call | flops 9059696640 | bytes 47185920 | tf_op jit(solution)/shard_map/g_up_far/pallas_call | solution.py:80
  247.4 4.0 %all-to-all-start = ((bf16[4,192,1536]{2,1,0:T(8,128)(2,1)}), bf16[4,192,1536]{2,1,0:T(8,128)(2,1)S(1)}, u32[]{:S(2)}, u32[]{:S(2)}) async-start(bf16[4,192,1536]{2,1,0:T(8,128)(2,1)} %bitcast.96), calls=%async_computation | async-start | bytes 4718592 | tf_op jit(solution)/shard_map/all_to_all | solution.py:392
  251.4 5.5 %g_down_near.1 = (bf16[192,3072]{1,0:T(8,128)(2,1)}, bf16[192,3072]{1,0:T(8,128)(2,1)}) custom-call(bf16[768,768]{1,0:T(8,128)(2,1)} %get-tuple-element.155.refs_0_, bf16[768,3072]{1,0:T(8,128)(2,1)} %get-tuple-element.148.refs_1_, bf16[384,3072]{1,0:T(8,128)(2,1)} %collective-permute-done.42.refs_2_, bf16[384,3072]{1,0:T(8,128)(2,1)} %g_up_far.1.refs_3_), custom_call_target="tpu_custom_call" | custom-call | flops 9059696640 | bytes 47185920 | tf_op jit(solution)/shard_map/g_down_near/pallas_call | solution.py:80
  258.0 5.4 %g_up_near.1 = (bf16[192,3072]{1,0:T(8,128)(2,1)}, bf16[192,3072]{1,0:T(8,128)(2,1)}) custom-call(bf16[768,768]{1,0:T(8,128)(2,1)} %get-tuple-element.141.refs_0_, bf16[768,3072]{1,0:T(8,128)(2,1)} %back_down.1.refs_1_.refs_2_.refs_0_, bf16[384,3072]{1,0:T(8,128)(2,1)} %collective-permute-done.41.refs_2_, bf16[192,3072]{1,0:T(8,128)(2,1)} %get-tuple-element.158.refs_3_.refs_0_), custom_call_target="tpu_custom_call" | custom-call | flops 9059696640 | bytes 47185920 | tf_op jit(solution)/shard_map/g_up_near/pallas_call | solution.py:80
  264.3 12.6 %back_up.1 = (f32[768,768]{1,0:T(8,128)}, bf16[768,768]{1,0:T(8,128)(2,1)}, bf16[768,768]{1,0:T(8,128)(2,1)}, f32[8,768]{1,0:T(8,128)}) custom-call(bf16[768,3072]{1,0:T(8,128)(2,1)} %back_down.1.refs_1_.refs_2_.refs_0_, bf16[96,6144]{1,0:T(8,128)(2,1)} %w_up_rows.1.refs_9_.refs_1_, bf16[96,6144]{1,0:T(8,128)(2,1)} %get-tuple-element.143.refs_2_, ...), custom_call_target="tpu_custom_call" | custom-call | flops 18119393280 | bytes 47185920 | tf_op jit(solution)/shard_map/back_up/pallas_call | solution.py:80
  277.0 2.8 g_down_add2.1
  281.3 11.5 %attend_backward.1.refs_3_.refs_1_.refs_0_ = bf16[768,2304]{1,0:T(8,128)(2,1)} custom-call(f32[4]{0:T(128)} %multiply_bitcast_fusion.refs_9_.refs_10_.refs_0_, bf16[768,2304]{1,0:T(8,128)(2,1)} %project_student.1.refs_2_.refs_3_.refs_4_.refs_8_.refs_1_, bf16[768,768]{1,0:T(8,128)(2,1)} %get-tuple-element.166.refs_2_, ...), custom_call_target="tpu_custom_call" | custom-call | flops 12079595520 | bytes 70778880 | tf_op jit(solution)/shard_map/attend_backward/pallas_call | solution.py:80
  292.8 2.3 g_down_add3.1
  296.1 2.8 g_up_add2.1
  299.4 2.0 collective-permute-start.47
  301.4 4.5 %g_qkv_far.1.refs_5_ = bf16[384,2304]{1,0:T(8,128)(2,1)} custom-call(bf16[768,768]{1,0:T(8,128)(2,1)} %get-tuple-element.107.refs_0_, bf16[768,2304]{1,0:T(8,128)(2,1)} %attend_backward.1.refs_3_.refs_1_.refs_0_, bf16[96,3072]{1,0:T(8,128)(2,1)} %get-tuple-element.170.refs_2_.refs_1_), custom_call_target="tpu_custom_call" | custom-call | flops 6794772480 | bytes 35389440 | tf_op jit(solution)/shard_map/g_qkv_far/pallas_call | solution.py:80
  306.0 6.1 %collective-permute-done.47.refs_3_ = bf16[2,96,768]{2,1,0:T(8,128)(2,1)S(1)} collective-permute-done((bf16[2,96,768]{2,1,0:T(8,128)(2,1)}, bf16[2,96,768]{2,1,0:T(8,128)(2,1)S(1)}, u32[]{:S(2)}, u32[]{:S(2)}) %collective-permute-start.47) | collective-permute-done | bytes 294944 | tf_op jit(solution)/shard_map/ppermute | solution.py:107
  313.0 2.3 g_up_add3.1
  316.5 2.0 collective-permute-start.50
  318.5 8.9 %back_entry.1.refs_4_ = bf16[768,768]{1,0:T(8,128)(2,1)} custom-call(bf16[768,2304]{1,0:T(8,128)(2,1)} %attend_backward.1.refs_3_.refs_1_.refs_0_, bf16[96,3072]{1,0:T(8,128)(2,1)} %get-tuple-element.115.refs_2_.refs_1_.refs_14_, bf16[96,3072]{1,0:T(8,128)(2,1)} %get-tuple-element.120.refs_2_.refs_15_, bf16[96,3072]{1,0:T(8,128)(2,1)} %get-tuple-element.124.refs_3_.refs_16_, ...), custom_call_target="tpu_custom_call" | custom-call | flops 13589544960 | bytes 35389440 | tf_op jit(solution)/shard_map/back_entry/pallas_call | solution.py:80
  327.4 3.2 g_out_far.1.refs_5_
  330.7 3.6 all-to-all-start.1
  335.1 4.7 %g_qkv_near.1 = (bf16[192,2304]{1,0:T(8,128)(2,1)}, bf16[192,2304]{1,0:T(8,128)(2,1)}, bf16[1,96,768]{2,1,0:T(8,128)(2,1)}, bf16[2,96,768]{2,1,0:T(8,128)(2,1)}) custom-call(bf16[768,768]{1,0:T(8,128)(2,1)} %get-tuple-element.107.refs_0_, bf16[768,2304]{1,0:T(8,128)(2,1)} %attend_backward.1.refs_3_.refs_1_.refs_0_, ...), custom_call_target="tpu_custom_call", output_to_operand_aliasing={{2}: (3, {}), {3}: (4, {})} | custom-call | flops 6794772480 | bytes 35389440 | tf_op jit(solution)/shard_map/g_qkv_near/pallas_call | solution.py:80
  341.1 3.4 g_out_near.1
  345.4 7.6 %collective-permute-done.51.refs_1_ = bf16[192,2304]{1,0:T(8,128)(2,1)S(1)} collective-permute-done((bf16[192,2304]{1,0:T(8,128)(2,1)}, bf16[192,2304]{1,0:T(8,128)(2,1)S(1)}, u32[]{:S(2)}, u32[]{:S(2)}) %collective-permute-start.51) | collective-permute-done | bytes 884768 | tf_op jit(solution)/shard_map/ppermute | solution.py:111
  354.0 2.5 g_qkv_add2.1
  358.7 2.9 collective-permute-start.60
  362.4 3.9 arrive.1
  367.1 2.1 g_qkv_add3.1
  369.2 2.0 g_out_add2.1
  371.9 1.7 collective-permute-start.55
  375.6 3.6 arrive_grad.1.refs_2_
  380.0 1.7 g_out_add3.1
  384.2 2.6 collective-permute-start.56
  388.1 2.9 collective-permute-start.59
  390.9 2.4 collective-permute-done.56
  (318 shorter events, 94.3 us)
Async XLA Ops:
  3.0 18.4 %collective-permute-start.1 = (bf16[96,768]{1,0:T(8,128)(2,1)S(1)}, bf16[96,768]{1,0:T(8,128)(2,1)S(1)}, u32[]{:S(2)}, u32[]{:S(2)}) collective-permute-start(bf16[96,768]{1,0:T(8,128)(2,1)S(1)} %pad_maximum_fusion.refs_4_.refs_0_), channel_id=1, source_target_pairs={{0,2},{1,3},{2,0},{3,1},{4,6},{5,7},{6,4},{7,5},{8,10},{9,11},{10,... | collective-permute-start | bytes 442376 | tf_op jit(solution)/shard_map/ppermute | solution.py:107
  10.9 3.7 collective-permute-start
  17.6 3.8 collective-permute-start.2
  19.2 14.0 %collective-permute-start.3 = (bf16[96,768]{1,0:T(8,128)(2,1)S(1)}, bf16[96,768]{1,0:T(8,128)(2,1)S(1)}, u32[]{:S(2)}, u32[]{:S(2)}) collective-permute-start(bf16[96,768]{1,0:T(8,128)(2,1)S(1)} %pad_maximum_fusion.1.refs_0_), channel_id=1, source_target_pairs={{0,2},{1,3},{2,0},{3,1},{4,6},{5,7},{6,4},{7,5},{8,10},{9,11},{10,... | collective-permute-start | bytes 442376 | tf_op jit(solution)/shard_map/ppermute | solution.py:107
  24.4 11.2 %collective-permute-start.7 = (bf16[96,1536]{1,0:T(8,128)(2,1)}, bf16[96,1536]{1,0:T(8,128)(2,1)S(1)}, u32[]{:S(2)}, u32[]{:S(2)}) collective-permute-start(bf16[96,1536]{1,0:T(8,128)(2,1)} %get-tuple-element.106.refs_3_.refs_0_), channel_id=1, source_target_pairs={{0,1},{1,0},{2,3},{3,2},{4,5},{5,4},{6,7},{7,6},{8,9},{9,8},{10,11... | collective-permute-start | bytes 884744 | tf_op jit(solution)/shard_map/ppermute | solution.py:107
  26.7 6.5 %collective-permute-start.4 = (f32[4,16,128]{2,1,0:T(8,128)S(1)}, f32[4,16,128]{2,1,0:T(8,128)S(1)}, u32[]{:S(2)}, u32[]{:S(2)}) collective-permute-start(f32[4,16,128]{2,1,0:T(8,128)S(1)} %pad_maximum_fusion.2), channel_id=1, source_target_pairs={{0,4},{4,0},{8,12},{12,8},{16,20},{20,16},{24,28},{28,24},{1,5},{5... | collective-permute-start | bytes 98312 | tf_op jit(solution)/shard_map/ppermute | solution.py:107
  38.4 2.3 collective-permute-start.8
  38.9 24.0 %collective-permute-start.9 = (bf16[96,3072]{1,0:T(8,128)(2,1)}, bf16[96,3072]{1,0:T(8,128)(2,1)S(1)}, u32[]{:S(2)}, u32[]{:S(2)}) collective-permute-start(bf16[96,3072]{1,0:T(8,128)(2,1)} %w_tqkv_rows.1.refs_1_), channel_id=1, source_target_pairs={{0,8},{4,20},{8,0},{12,28},{16,24},{20,4},{24,16},{28,12},{1,9},{5... | collective-permute-start | bytes 1769480 | tf_op jit(solution)/shard_map/ppermute | solution.py:111
  42.1 20.7 %collective-permute-start.10 = (bf16[96,3072]{1,0:T(8,128)(2,1)}, bf16[96,3072]{1,0:T(8,128)(2,1)S(1)}, u32[]{:S(2)}, u32[]{:S(2)}) collective-permute-start(bf16[96,3072]{1,0:T(8,128)(2,1)} %get-tuple-element.113.refs_5_), channel_id=1, source_target_pairs={{0,8},{4,20},{8,0},{12,28},{16,24},{20,4},{24,16},{28,12},{1,9},{5... | collective-permute-start | bytes 1769480 | tf_op jit(solution)/shard_map/ppermute | solution.py:111
  43.6 16.1 %collective-permute-start.5 = (bf16[96,1536]{1,0:T(8,128)(2,1)S(1)}, bf16[96,1536]{1,0:T(8,128)(2,1)S(1)}, u32[]{:S(2)}, u32[]{:S(2)}) collective-permute-start(bf16[96,1536]{1,0:T(8,128)(2,1)S(1)} %copy-done.2), channel_id=1, source_target_pairs={{0,2},{1,3},{2,0},{3,1},{4,6},{5,7},{6,4},{7,5},{8,10},{9,11},{10,... | collective-permute-start | bytes 884744 | tf_op jit(solution)/shard_map/ppermute | solution.py:107
  46.2 14.0 %collective-permute-start.6 = (bf16[96,1536]{1,0:T(8,128)(2,1)S(1)}, bf16[96,1536]{1,0:T(8,128)(2,1)S(1)}, u32[]{:S(2)}, u32[]{:S(2)}) collective-permute-start(bf16[96,1536]{1,0:T(8,128)(2,1)S(1)} %copy-done.14), channel_id=1, source_target_pairs={{0,1},{1,0},{2,3},{3,2},{4,5},{5,4},{6,7},{7,6},{8,9},{9,8},{10,11... | collective-permute-start | bytes 884744 | tf_op jit(solution)/shard_map/ppermute | solution.py:107
  66.0 2.4 collective-permute-start.12
  66.0 3.1 collective-permute-start.13
  66.5 15.4 %collective-permute-start.16 = (bf16[96,3072]{1,0:T(8,128)(2,1)S(1)}, bf16[96,3072]{1,0:T(8,128)(2,1)S(1)}, u32[]{:S(2)}, u32[]{:S(2)}) collective-permute-start(bf16[96,3072]{1,0:T(8,128)(2,1)S(1)} %copy-done.9), channel_id=1, source_target_pairs={{0,1},{1,0},{2,3},{3,2},{4,5},{5,4},{6,7},{7,6},{8,9},{9,8},{10,11... | collective-permute-start | bytes 1769480 | tf_op jit(solution)/shard_map/ppermute | solution.py:107
  66.9 15.0 %collective-permute-start.11 = (bf16[96,3072]{1,0:T(8,128)(2,1)}, bf16[96,3072]{1,0:T(8,128)(2,1)S(1)}, u32[]{:S(2)}, u32[]{:S(2)}) collective-permute-start(bf16[96,3072]{1,0:T(8,128)(2,1)} %get-tuple-element.115.refs_2_.refs_1_.refs_14_), channel_id=1, source_target_pairs={{0,8},{4,20},{8,0},{12,28},{16,24},{20,4},{24,16},{28,12},{1,9},{5... | collective-permute-start | bytes 1769480 | tf_op jit(solution)/shard_map/ppermute | solution.py:111
  70.6 16.3 %copy-start.36 = (bf16[96,3072]{1,0:T(8,128)(2,1)S(1)}, bf16[96,3072]{1,0:T(8,128)(2,1)}, u32[]{:S(2)}) copy-start(bf16[96,3072]{1,0:T(8,128)(2,1)} %get-tuple-element.127.refs_2_) | copy-start | bytes 1769476
  70.6 12.7 %collective-permute-start.14 = (bf16[96,3072]{1,0:T(8,128)(2,1)}, bf16[96,3072]{1,0:T(8,128)(2,1)S(1)}, u32[]{:S(2)}, u32[]{:S(2)}) collective-permute-start(bf16[96,3072]{1,0:T(8,128)(2,1)} %get-tuple-element.117.refs_5_.refs_18_), channel_id=1, source_target_pairs={{0,8},{4,20},{8,0},{12,28},{16,24},{20,4},{24,16},{28,12},{1,9},{5... | collective-permute-start | bytes 1769480 | tf_op jit(solution)/shard_map/ppermute | solution.py:111
  72.0 9.9 %collective-permute-start.15 = (f32[8,128]{1,0:T(8,128)S(1)}, f32[8,128]{1,0:T(8,128)S(1)}, u32[]{:S(2)}, u32[]{:S(2)}) collective-permute-start(f32[8,128]{1,0:T(8,128)S(1)} %fusion.11), channel_id=1, source_target_pairs={{0,1},{1,0},{2,3},{3,2},{4,5},{5,4},{6,7},{7,6},{8,9},{9,8},{10,11... | collective-permute-start | bytes 12296 | tf_op jit(solution)/shard_map/ppermute | solution.py:107
  72.9 16.7 %collective-permute-start.23 = (bf16[96,3072]{1,0:T(8,128)(2,1)}, bf16[96,3072]{1,0:T(8,128)(2,1)S(1)}, u32[]{:S(2)}, u32[]{:S(2)}) collective-permute-start(bf16[96,3072]{1,0:T(8,128)(2,1)} %get-tuple-element.128.refs_3_), channel_id=1, source_target_pairs={{0,8},{4,20},{8,0},{12,28},{16,24},{20,4},{24,16},{28,12},{1,9},{5... | collective-permute-start | bytes 1769480 | tf_op jit(solution)/shard_map/ppermute | solution.py:111
  84.7 5.3 %collective-permute-start.17 = (bf16[96,3072]{1,0:T(8,128)(2,1)}, bf16[96,3072]{1,0:T(8,128)(2,1)S(1)}, u32[]{:S(2)}, u32[]{:S(2)}) collective-permute-start(bf16[96,3072]{1,0:T(8,128)(2,1)} %get-tuple-element.121.refs_7_.refs_20_), channel_id=1, source_target_pairs={{0,4},{4,0},{8,12},{12,8},{16,20},{20,16},{24,28},{28,24},{1,5},{5... | collective-permute-start | bytes 1769480 | tf_op jit(solution)/shard_map/ppermute | solution.py:107
  85.5 4.5 %collective-permute-start.18 = (f32[8,128]{1,0:T(8,128)S(1)}, f32[8,128]{1,0:T(8,128)S(1)}, u32[]{:S(2)}, u32[]{:S(2)}) collective-permute-start(f32[8,128]{1,0:T(8,128)S(1)} %fusion.21), channel_id=1, source_target_pairs={{0,2},{1,3},{2,0},{3,1},{4,6},{5,7},{6,4},{7,5},{8,10},{9,11},{10,... | collective-permute-start | bytes 12296 | tf_op jit(solution)/shard_map/ppermute | solution.py:107
  86.9 10.9 %collective-permute-start.24 = (bf16[96,3072]{1,0:T(8,128)(2,1)S(1)}, bf16[96,3072]{1,0:T(8,128)(2,1)S(1)}, u32[]{:S(2)}, u32[]{:S(2)}) collective-permute-start(bf16[96,3072]{1,0:T(8,128)(2,1)S(1)} %copy-done.36), channel_id=1, source_target_pairs={{0,4},{4,0},{8,12},{12,8},{16,20},{20,16},{24,28},{28,24},{1,5},{5... | collective-permute-start | bytes 1769480 | tf_op jit(solution)/shard_map/ppermute | solution.py:107
  89.6 8.6 %collective-permute-start.25 = (bf16[96,3072]{1,0:T(8,128)(2,1)S(1)}, bf16[96,3072]{1,0:T(8,128)(2,1)}, u32[]{:S(2)}, u32[]{:S(2)}) collective-permute-start(bf16[96,3072]{1,0:T(8,128)(2,1)S(1)} %collective-permute-done.23.refs_4_), channel_id=1, source_target_pairs={{0,4},{4,0},{8,12},{12,8},{16,20},{20,16},{24,28},{28,24},{1,5},{5... | collective-permute-start | bytes 1769480 | tf_op jit(solution)/shard_map/ppermute | solution.py:107
  92.0 10.2 %collective-permute-start.19 = (bf16[96,3072]{1,0:T(8,128)(2,1)}, bf16[96,3072]{1,0:T(8,128)(2,1)}, u32[]{:S(2)}, u32[]{:S(2)}) collective-permute-start(bf16[96,3072]{1,0:T(8,128)(2,1)} %get-tuple-element.124.refs_3_.refs_16_), channel_id=1, source_target_pairs={{0,8},{4,20},{8,0},{12,28},{16,24},{20,4},{24,16},{28,12},{1,9},{5... | collective-permute-start | bytes 1769480 | tf_op jit(solution)/shard_map/ppermute | solution.py:111
  94.0 16.3 %collective-permute-start.22 = (bf16[96,1536]{1,0:T(8,128)(2,1)}, bf16[96,1536]{1,0:T(8,128)(2,1)S(1)}, u32[]{:S(2)}, u32[]{:S(2)}) collective-permute-start(bf16[96,1536]{1,0:T(8,128)(2,1)} %pack_down.1.refs_2_.refs_0_), channel_id=1, source_target_pairs={{0,2},{1,3},{2,0},{3,1},{4,6},{5,7},{6,4},{7,5},{8,10},{9,11},{10,... | collective-permute-start | bytes 884744 | tf_op jit(solution)/shard_map/ppermute | solution.py:107
  95.4 20.4 %collective-permute-start.20 = (bf16[96,3072]{1,0:T(8,128)(2,1)S(1)}, bf16[96,3072]{1,0:T(8,128)(2,1)}, u32[]{:S(2)}, u32[]{:S(2)}) collective-permute-start(bf16[96,3072]{1,0:T(8,128)(2,1)S(1)} %copy-done.29), channel_id=1, source_target_pairs={{0,4},{4,0},{8,12},{12,8},{16,20},{20,16},{24,28},{28,24},{1,5},{5... | collective-permute-start | bytes 1769480 | tf_op jit(solution)/shard_map/ppermute | solution.py:107
  97.7 16.5 %collective-permute-start.27 = (bf16[96,6144]{1,0:T(8,128)(2,1)}, bf16[96,6144]{1,0:T(8,128)(2,1)}, u32[]{:S(2)}, u32[]{:S(2)}) collective-permute-start(bf16[96,6144]{1,0:T(8,128)(2,1)} %w_up_rows.1.refs_9_.refs_1_), channel_id=1, source_target_pairs={{0,4},{4,0},{8,12},{12,8},{16,20},{20,16},{24,28},{28,24},{1,5},{5... | collective-permute-start | bytes 3538952 | tf_op jit(solution)/shard_map/ppermute | solution.py:107
  98.3 33.0 %collective-permute-start.26 = (bf16[96,6144]{1,0:T(8,128)(2,1)}, bf16[96,6144]{1,0:T(8,128)(2,1)S(1)}, u32[]{:S(2)}, u32[]{:S(2)}) collective-permute-start(bf16[96,6144]{1,0:T(8,128)(2,1)} %w_up_rows.1.refs_9_.refs_1_), channel_id=1, source_target_pairs={{0,8},{4,20},{8,0},{12,28},{16,24},{20,4},{24,16},{28,12},{1,9},{5... | collective-permute-start | bytes 3538952 | tf_op jit(solution)/shard_map/ppermute | solution.py:111
  102.2 13.6 %collective-permute-start.21 = (bf16[96,3072]{1,0:T(8,128)(2,1)}, bf16[96,3072]{1,0:T(8,128)(2,1)}, u32[]{:S(2)}, u32[]{:S(2)}) collective-permute-start(bf16[96,3072]{1,0:T(8,128)(2,1)} %collective-permute-done.19.refs_4_.refs_17_), channel_id=1, source_target_pairs={{0,4},{4,0},{8,12},{12,8},{16,20},{20,16},{24,28},{28,24},{1,5},{5... | collective-permute-start | bytes 1769480 | tf_op jit(solution)/shard_map/ppermute | solution.py:107
  112.8 18.4 %collective-permute-start.29 = (bf16[96,3072]{1,0:T(8,128)(2,1)}, bf16[96,3072]{1,0:T(8,128)(2,1)S(1)}, u32[]{:S(2)}, u32[]{:S(2)}) collective-permute-start(bf16[96,3072]{1,0:T(8,128)(2,1)} %w_down_join.1.refs_10_.refs_1_), channel_id=1, source_target_pairs={{0,1},{1,0},{2,3},{3,2},{4,5},{5,4},{6,7},{7,6},{8,9},{9,8},{10,11... | collective-permute-start | bytes 1769480 | tf_op jit(solution)/shard_map/ppermute | solution.py:107
  114.3 17.0 %collective-permute-start.28 = (bf16[96,6144]{1,0:T(8,128)(2,1)}, bf16[96,6144]{1,0:T(8,128)(2,1)S(1)}, u32[]{:S(2)}, u32[]{:S(2)}) collective-permute-start(bf16[96,6144]{1,0:T(8,128)(2,1)} %collective-permute-done.27.refs_5_), channel_id=1, source_target_pairs={{0,8},{4,20},{8,0},{12,28},{16,24},{20,4},{24,16},{28,12},{1,9},{5... | collective-permute-start | bytes 3538952 | tf_op jit(solution)/shard_map/ppermute | solution.py:111
  133.5 3.1 collective-permute-start.30
  136.5 19.0 %collective-permute-start.31 = (bf16[96,6144]{1,0:T(8,128)(2,1)S(1)}, bf16[96,6144]{1,0:T(8,128)(2,1)S(1)}, u32[]{:S(2)}, u32[]{:S(2)}) collective-permute-start(bf16[96,6144]{1,0:T(8,128)(2,1)S(1)} %collective-permute-done.30.refs_3_), channel_id=1, source_target_pairs={{0,8},{4,20},{8,0},{12,28},{16,24},{20,4},{24,16},{28,12},{1,9},{5... | collective-permute-start | bytes 3538952 | tf_op jit(solution)/shard_map/ppermute | solution.py:111
  148.6 16.8 %collective-permute-start.34 = (bf16[96,6144]{1,0:T(8,128)(2,1)}, bf16[96,6144]{1,0:T(8,128)(2,1)}, u32[]{:S(2)}, u32[]{:S(2)}) collective-permute-start(bf16[96,6144]{1,0:T(8,128)(2,1)} %w_down_rows.1.refs_10_.refs_2_.refs_1_), channel_id=1, source_target_pairs={{0,8},{4,20},{8,0},{12,28},{16,24},{20,4},{24,16},{28,12},{1,9},{5... | collective-permute-start | bytes 3538952 | tf_op jit(solution)/shard_map/ppermute | solution.py:111
  149.5 13.2 %collective-permute-start.35 = (bf16[96,6144]{1,0:T(8,128)(2,1)}, bf16[96,6144]{1,0:T(8,128)(2,1)}, u32[]{:S(2)}, u32[]{:S(2)}) collective-permute-start(bf16[96,6144]{1,0:T(8,128)(2,1)} %w_down_rows.1.refs_10_.refs_2_.refs_1_), channel_id=1, source_target_pairs={{0,4},{4,0},{8,12},{12,8},{16,20},{20,16},{24,28},{28,24},{1,5},{5... | collective-permute-start | bytes 3538952 | tf_op jit(solution)/shard_map/ppermute | solution.py:107
  149.5 16.0 %collective-permute-start.32 = (bf16[96,6144]{1,0:T(8,128)(2,1)S(1)}, bf16[96,6144]{1,0:T(8,128)(2,1)}, u32[]{:S(2)}, u32[]{:S(2)}) collective-permute-start(bf16[96,6144]{1,0:T(8,128)(2,1)S(1)} %copy-done.17), channel_id=1, source_target_pairs={{0,4},{4,0},{8,12},{12,8},{16,20},{20,16},{24,28},{28,24},{1,5},{5... | collective-permute-start | bytes 3538952 | tf_op jit(solution)/shard_map/ppermute | solution.py:107
  162.7 3.1 collective-permute-start.33
  162.7 16.5 %collective-permute-start.36 = (bf16[96,6144]{1,0:T(8,128)(2,1)}, bf16[96,6144]{1,0:T(8,128)(2,1)S(1)}, u32[]{:S(2)}, u32[]{:S(2)}) collective-permute-start(bf16[96,6144]{1,0:T(8,128)(2,1)} %collective-permute-done.35.refs_6_.refs_5_), channel_id=1, source_target_pairs={{0,8},{4,20},{8,0},{12,28},{16,24},{20,4},{24,16},{28,12},{1,9},{5... | collective-permute-start | bytes 3538952 | tf_op jit(solution)/shard_map/ppermute | solution.py:111
  180.9 3.1 collective-permute-start.37
  180.9 20.9 %collective-permute-start.39 = (bf16[96,6144]{1,0:T(8,128)(2,1)}, bf16[96,6144]{1,0:T(8,128)(2,1)S(1)}, u32[]{:S(2)}, u32[]{:S(2)}) collective-permute-start(bf16[96,6144]{1,0:T(8,128)(2,1)} %get-tuple-element.149.refs_3_.refs_2_), channel_id=1, source_target_pairs={{0,4},{4,0},{8,12},{12,8},{16,20},{20,16},{24,28},{28,24},{1,5},{5... | collective-permute-start | bytes 3538952 | tf_op jit(solution)/shard_map/ppermute | solution.py:107
  183.9 16.2 %collective-permute-start.38 = (bf16[96,6144]{1,0:T(8,128)(2,1)S(1)}, bf16[96,6144]{1,0:T(8,128)(2,1)S(1)}, u32[]{:S(2)}, u32[]{:S(2)}) collective-permute-start(bf16[96,6144]{1,0:T(8,128)(2,1)S(1)} %collective-permute-done.37.refs_4_.refs_3_), channel_id=1, source_target_pairs={{0,8},{4,20},{8,0},{12,28},{16,24},{20,4},{24,16},{28,12},{1,9},{5... | collective-permute-start | bytes 3538952 | tf_op jit(solution)/shard_map/ppermute | solution.py:111
  201.7 3.1 collective-permute-start.40
  232.0 19.4 %collective-permute-start.42 = (bf16[384,3072]{1,0:T(8,128)(2,1)}, bf16[384,3072]{1,0:T(8,128)(2,1)}, u32[]{:S(2)}, u32[]{:S(2)}) collective-permute-start(bf16[384,3072]{1,0:T(8,128)(2,1)} %g_down_far.1.refs_11_), channel_id=1, source_target_pairs={{0,4},{4,0},{8,12},{12,8},{16,20},{20,16},{24,28},{28,24},{1,5},{5... | collective-permute-start | bytes 7077896 | tf_op jit(solution)/shard_map/ppermute | solution.py:107
  246.5 11.6 %collective-permute-start.41 = (bf16[384,3072]{1,0:T(8,128)(2,1)}, bf16[384,3072]{1,0:T(8,128)(2,1)}, u32[]{:S(2)}, u32[]{:S(2)}) collective-permute-start(bf16[384,3072]{1,0:T(8,128)(2,1)} %g_up_far.1.refs_3_), channel_id=1, source_target_pairs={{0,4},{4,0},{8,12},{12,8},{16,20},{20,16},{24,28},{28,24},{1,5},{5... | collective-permute-start | bytes 7077896 | tf_op jit(solution)/shard_map/ppermute | solution.py:107
  247.4 58.6 %all-to-all-start = ((bf16[4,192,1536]{2,1,0:T(8,128)(2,1)}), bf16[4,192,1536]{2,1,0:T(8,128)(2,1)S(1)}, u32[]{:S(2)}, u32[]{:S(2)}) async-start(bf16[4,192,1536]{2,1,0:T(8,128)(2,1)} %bitcast.96), calls=%async_computation | async-start | bytes 4718592 | tf_op jit(solution)/shard_map/all_to_all | solution.py:392
  256.9 20.1 %collective-permute-start.44 = (bf16[192,3072]{1,0:T(8,128)(2,1)}, bf16[192,3072]{1,0:T(8,128)(2,1)}, u32[]{:S(2)}, u32[]{:S(2)}) collective-permute-start(bf16[192,3072]{1,0:T(8,128)(2,1)} %get-tuple-element.161), channel_id=1, source_target_pairs={{0,8},{4,20},{8,0},{12,28},{16,24},{20,4},{24,16},{28,12},{1,9},{5... | collective-permute-start | bytes 3538952 | tf_op jit(solution)/shard_map/ppermute | solution.py:111
  263.5 31.6 %collective-permute-start.43 = (bf16[192,3072]{1,0:T(8,128)(2,1)}, bf16[192,3072]{1,0:T(8,128)(2,1)S(1)}, u32[]{:S(2)}, u32[]{:S(2)}) collective-permute-start(bf16[192,3072]{1,0:T(8,128)(2,1)} %get-tuple-element.160), channel_id=1, source_target_pairs={{0,8},{4,20},{8,0},{12,28},{16,24},{20,4},{24,16},{28,12},{1,9},{5... | collective-permute-start | bytes 3538952 | tf_op jit(solution)/shard_map/ppermute | solution.py:111
  279.8 13.0 %collective-permute-start.45 = (bf16[96,3072]{1,0:T(8,128)(2,1)}, bf16[96,3072]{1,0:T(8,128)(2,1)}, u32[]{:S(2)}, u32[]{:S(2)}) collective-permute-start(bf16[96,3072]{1,0:T(8,128)(2,1)} %get-tuple-element.165), channel_id=1, source_target_pairs={{0,16},{4,12},{8,24},{12,4},{16,0},{20,28},{24,8},{28,20},{1,17},{... | collective-permute-start | bytes 1769480 | tf_op jit(solution)/shard_map/ppermute | solution.py:115
  298.9 13.2 %collective-permute-start.46 = (bf16[96,3072]{1,0:T(8,128)(2,1)}, bf16[96,3072]{1,0:T(8,128)(2,1)S(1)}, u32[]{:S(2)}, u32[]{:S(2)}) collective-permute-start(bf16[96,3072]{1,0:T(8,128)(2,1)} %get-tuple-element.171), channel_id=1, source_target_pairs={{0,16},{4,12},{8,24},{12,4},{16,0},{20,28},{24,8},{28,20},{1,17},{... | collective-permute-start | bytes 1769480 | tf_op jit(solution)/shard_map/ppermute | solution.py:115
  299.4 12.6 %collective-permute-start.47 = (bf16[2,96,768]{2,1,0:T(8,128)(2,1)}, bf16[2,96,768]{2,1,0:T(8,128)(2,1)S(1)}, u32[]{:S(2)}, u32[]{:S(2)}) collective-permute-start(bf16[2,96,768]{2,1,0:T(8,128)(2,1)} %bitcast.24), channel_id=1, source_target_pairs={{0,1},{1,0},{2,3},{3,2},{4,5},{5,4},{6,7},{7,6},{8,9},{9,8},{10,11... | collective-permute-start | bytes 884744 | tf_op jit(solution)/shard_map/ppermute | solution.py:107
  306.0 28.4 %collective-permute-start.48 = (bf16[384,2304]{1,0:T(8,128)(2,1)}, bf16[384,2304]{1,0:T(8,128)(2,1)}, u32[]{:S(2)}, u32[]{:S(2)}) collective-permute-start(bf16[384,2304]{1,0:T(8,128)(2,1)} %g_qkv_far.1.refs_5_), channel_id=1, source_target_pairs={{0,4},{4,0},{8,12},{12,8},{16,20},{20,16},{24,28},{28,24},{1,5},{5... | collective-permute-start | bytes 5308424 | tf_op jit(solution)/shard_map/ppermute | solution.py:107
  316.4 17.9 %collective-permute-start.49 = (bf16[1,96,768]{2,1,0:T(8,128)(2,1)S(1)}, bf16[1,96,768]{2,1,0:T(8,128)(2,1)S(1)}, u32[]{:S(2)}, u32[]{:S(2)}) collective-permute-start(bf16[1,96,768]{2,1,0:T(8,128)(2,1)S(1)} %slice.131), channel_id=1, source_target_pairs={{0,2},{1,3},{2,0},{3,1},{4,6},{5,7},{6,4},{7,5},{8,10},{9,11},{10,... | collective-permute-start | bytes 442376 | tf_op jit(solution)/shard_map/ppermute | solution.py:107
  316.5 17.8 %collective-permute-start.50 = (bf16[2,96,768]{2,1,0:T(8,128)(2,1)S(1)}, bf16[2,96,768]{2,1,0:T(8,128)(2,1)S(1)}, u32[]{:S(2)}, u32[]{:S(2)}) collective-permute-start(bf16[2,96,768]{2,1,0:T(8,128)(2,1)S(1)} %bitcast.113), channel_id=1, source_target_pairs={{0,1},{1,0},{2,3},{3,2},{4,5},{5,4},{6,7},{7,6},{8,9},{9,8},{10,11... | collective-permute-start | bytes 884744 | tf_op jit(solution)/shard_map/ppermute | solution.py:107
  330.6 10.5 %collective-permute-start.52 = (bf16[384,1024]{1,0:T(8,128)(2,1)}, bf16[384,1024]{1,0:T(8,128)(2,1)}, u32[]{:S(2)}, u32[]{:S(2)}) collective-permute-start(bf16[384,1024]{1,0:T(8,128)(2,1)} %g_out_far.1.refs_5_), channel_id=1, source_target_pairs={{0,4},{4,0},{8,12},{12,8},{16,20},{20,16},{24,28},{28,24},{1,5},{5... | collective-permute-start | bytes 2359304 | tf_op jit(solution)/shard_map/ppermute | solution.py:107
  330.7 44.0 %all-to-all-start.1 = ((bf16[4,192,768]{2,1,0:T(8,128)(2,1)}), bf16[4,192,768]{2,1,0:T(8,128)(2,1)S(1)}, u32[]{:S(2)}, u32[]{:S(2)}) async-start(bf16[4,192,768]{2,1,0:T(8,128)(2,1)} %bitcast.31), calls=%async_computation.1 | async-start | bytes 2359296 | tf_op jit(solution)/shard_map/all_to_all | solution.py:392
  339.8 13.3 %collective-permute-start.51 = (bf16[192,2304]{1,0:T(8,128)(2,1)}, bf16[192,2304]{1,0:T(8,128)(2,1)S(1)}, u32[]{:S(2)}, u32[]{:S(2)}) collective-permute-start(bf16[192,2304]{1,0:T(8,128)(2,1)} %get-tuple-element.182), channel_id=1, source_target_pairs={{0,8},{4,20},{8,0},{12,28},{16,24},{20,4},{24,16},{28,12},{1,9},{5... | collective-permute-start | bytes 2654216 | tf_op jit(solution)/shard_map/ppermute | solution.py:111
  344.5 24.7 %collective-permute-start.53 = (bf16[192,1024]{1,0:T(8,128)(2,1)}, bf16[192,1024]{1,0:T(8,128)(2,1)}, u32[]{:S(2)}, u32[]{:S(2)}) collective-permute-start(bf16[192,1024]{1,0:T(8,128)(2,1)} %get-tuple-element.187), channel_id=1, source_target_pairs={{0,8},{4,20},{8,0},{12,28},{16,24},{20,4},{24,16},{28,12},{1,9},{5... | collective-permute-start | bytes 1179656 | tf_op jit(solution)/shard_map/ppermute | solution.py:111
  356.5 9.8 %collective-permute-start.54 = (bf16[96,2304]{1,0:T(8,128)(2,1)}, bf16[96,2304]{1,0:T(8,128)(2,1)S(1)}, u32[]{:S(2)}, u32[]{:S(2)}) collective-permute-start(bf16[96,2304]{1,0:T(8,128)(2,1)} %get-tuple-element.188), channel_id=1, source_target_pairs={{0,16},{4,12},{8,24},{12,4},{16,0},{20,28},{24,8},{28,20},{1,17},{... | collective-permute-start | bytes 1327112 | tf_op jit(solution)/shard_map/ppermute | solution.py:115
  358.7 14.9 %collective-permute-start.60 = (bf16[1,96,768]{2,1,0:T(8,128)(2,1)}, bf16[1,96,768]{2,1,0:T(8,128)(2,1)S(1)}, u32[]{:S(2)}, u32[]{:S(2)}) collective-permute-start(bf16[1,96,768]{2,1,0:T(8,128)(2,1)} %slice.138), channel_id=1, source_target_pairs={{0,2},{1,3},{2,0},{3,1},{4,6},{5,7},{6,4},{7,5},{8,10},{9,11},{10,... | collective-permute-start | bytes 442376 | tf_op jit(solution)/shard_map/ppermute | solution.py:107
  371.2 8.1 %collective-permute-start.57 = (bf16[96,1024]{1,0:T(8,128)(2,1)}, bf16[96,1024]{1,0:T(8,128)(2,1)S(1)}, u32[]{:S(2)}, u32[]{:S(2)}) collective-permute-start(bf16[96,1024]{1,0:T(8,128)(2,1)} %get-tuple-element.192), channel_id=1, source_target_pairs={{0,16},{4,12},{8,24},{12,4},{16,0},{20,28},{24,8},{28,20},{1,17},{... | collective-permute-start | bytes 589832 | tf_op jit(solution)/shard_map/ppermute | solution.py:115
  371.9 12.2 %collective-permute-start.55 = (bf16[2,96,576]{1,2,0:T(8,128)(2,1)S(1)}, bf16[2,96,576]{1,2,0:T(8,128)(2,1)S(1)}, u32[]{:S(2)}, u32[]{:S(2)}) collective-permute-start(bf16[2,96,576]{1,2,0:T(8,128)(2,1)S(1)} %copy.73), channel_id=1, source_target_pairs={{0,1},{1,0},{2,3},{3,2},{4,5},{5,4},{6,7},{7,6},{8,9},{9,8},{10,11... | collective-permute-start | bytes 663560 | tf_op jit(solution)/shard_map/ppermute | solution.py:107
  382.7 5.3 %collective-permute-start.58 = (bf16[2,96,256]{1,2,0:T(8,128)(2,1)S(1)}, bf16[2,96,256]{1,2,0:T(8,128)(2,1)S(1)}, u32[]{:S(2)}, u32[]{:S(2)}) collective-permute-start(bf16[2,96,256]{1,2,0:T(8,128)(2,1)S(1)} %copy.75), channel_id=1, source_target_pairs={{0,1},{1,0},{2,3},{3,2},{4,5},{5,4},{6,7},{7,6},{8,9},{9,8},{10,11... | collective-permute-start | bytes 294920 | tf_op jit(solution)/shard_map/ppermute | solution.py:107
  384.2 9.1 %collective-permute-start.56 = (bf16[1,96,576]{1,2,0:T(8,128)(2,1)S(1)}, bf16[1,96,576]{1,2,0:T(8,128)(2,1)S(1)}, u32[]{:S(2)}, u32[]{:S(2)}) collective-permute-start(bf16[1,96,576]{1,2,0:T(8,128)(2,1)S(1)} %slice.133), channel_id=1, source_target_pairs={{0,2},{1,3},{2,0},{3,1},{4,6},{5,7},{6,4},{7,5},{8,10},{9,11},{10,... | collective-permute-start | bytes 331784 | tf_op jit(solution)/shard_map/ppermute | solution.py:107
  388.1 6.7 %collective-permute-start.59 = (bf16[1,96,256]{1,2,0:T(8,128)(2,1)S(1)}, bf16[1,96,256]{1,2,0:T(8,128)(2,1)S(1)}, u32[]{:S(2)}, u32[]{:S(2)}) collective-permute-start(bf16[1,96,256]{1,2,0:T(8,128)(2,1)S(1)} %slice.135), channel_id=1, source_target_pairs={{0,2},{1,3},{2,0},{3,1},{4,6},{5,7},{6,4},{7,5},{8,10},{9,11},{10,... | collective-permute-start | bytes 147464 | tf_op jit(solution)/shard_map/ppermute | solution.py:107
  (76 other events, 331.5 us)
